TPU v7x, 256 devices: a whole 4x4x8 slice. The times are simulated.
256 devices in a mesh: dp: 4 (over x_hi, core), ctx: 64 (over y, x_lo, z).
Axes of the slice: x: 4 (x_hi: 2, x_lo: 2; x = x_hi * 2 + x_lo), y: 4, z: 8, core: 2. Of those that a mesh axis runs over, the one named last changes fastest.
Arguments:
- queries: bfloat16 [4, 16384, 1024], P('dp', 'ctx'), may hold values from -16 to 16
- key_rows: bfloat16 [4, 16384, 1024], P('dp', 'ctx'), may hold values from -8 to 8
- values: bfloat16 [4, 16384, 1024], P('dp', 'ctx'), may hold values from -6 to 6
- cotangent: bfloat16 [4, 16384, 1024], P('dp', 'ctx'), may hold values from -6 to 6
- slot_starts: int32 [4, 64], P('dp'), may hold values from -1 to 16256, as said below
- prompt_lens: int32 [4, 64], P('dp'), may hold values from 0 to 128, as said below
- prompt_bias: float32 [8], replicated, may hold values from -1 to 2
Outputs:
- attended: bfloat16 [4, 16384, 1024], P('dp', 'ctx')
- grad_queries: bfloat16 [4, 16384, 1024], P('dp', 'ctx')
- grad_keys: bfloat16 [4, 16384, 1024], P('dp', 'ctx')
- grad_values: bfloat16 [4, 16384, 1024], P('dp', 'ctx')
- grad_bias: float32 [8], replicated
Inputs may be any that keep to these rules, and one draw needn't show every extreme that they name: `slot_starts`: each index of ctx owns one slot. They hold, ascending, the first frames of the utterances that begin among that device's 256 frames, then -1. Frame 0 begins an utterance. Every start s has s % 256 <= 128, and two starts of one device lie 128 or more apart. In each packed sequence some device fills all 1 slots, and the last index of ctx starts an utterance at frame 16384 - 128. `prompt_lens`: A used slot holds 1 or more and at most the distance to the next used start; an unused slot holds 0. In each packed sequence some slot holds 128.
All inputs are finite; a program needn't handle non-finite values.
Results may differ from a plain program's by a relative error of at most 0.006.
Values may be sent and summed in bfloat16 or wider, within the bound.
No kernel may reach another device: no remote copies, remote signals or barrier semaphores. Data moves between devices by JAX's collectives and lax.ppermute only.
A program may use at most 320 MiB of HBM per device.

v0:
```python
import math

import jax
import jax.numpy as jnp
from jax import lax
from jax.sharding import PartitionSpec as P

HW = 128
PMAX = 128


def entering(value, axis, join, neutral, backward):
    count, mine = (lax.axis_size(axis), lax.axis_index(axis))
    pieces = jax.tree.map(lambda part: lax.all_gather(part, axis), value)
    if backward:
        pieces = jax.tree.map(lambda part: part[::-1], pieces)
        mine = count - 1 - mine
    total = jax.tree.map(
        lambda part, zero: jnp.full_like(part, 0) + jnp.asarray(zero, part.dtype), value, neutral
    )

    def lap(position, total):
        longer = join(total, jax.tree.map(lambda part: part[position], pieces))
        return jax.tree.map(lambda new, old: jnp.where(position < mine, new, old), longer, total)

    return lax.fori_loop(0, count - 1, lap, total)


def with_halo(block, sides, width):
    for axis, dim in sides:
        count = lax.axis_size(axis)
        forward = [(i, i + 1) for i in range(count - 1)]
        backward = [(target, source) for source, target in forward]
        low = lax.ppermute(
            lax.slice_in_dim(block, block.shape[dim] - width, None, axis=dim), axis, forward
        )
        high = lax.ppermute(lax.slice_in_dim(block, 0, width, axis=dim), axis, backward)
        block = jnp.concatenate([low, block, high], axis=dim)
    return block


def shifted(x, axis, by):
    peers = lax.axis_size(axis)
    pairs = [(i, i + by) for i in range(peers) if 0 <= i + by < peers]
    return lax.ppermute(x, axis, pairs)


def utterance_info(positions, starts, plens):
    usable = starts >= 0
    reached = usable[None, :] & (starts[None, :] <= positions[:, None])
    start_of = jnp.max(jnp.where(reached, starts[None, :], -2), axis=1)
    owning = reached & (starts[None, :] == start_of[:, None])
    length = jnp.sum(jnp.where(owning, plens[None, :], 0), axis=1)
    return (start_of, length)


def window_mask(query_pos, key_pos, starts, plens, frames):
    query_start = utterance_info(query_pos, starts, plens)[0]
    key_info = utterance_info(key_pos, starts, plens)
    near_rows = jnp.abs(query_pos[:, None] - key_pos[None, :]) <= HW
    usable = (key_pos >= 0) & (key_pos < frames) & (key_pos - key_info[0] >= key_info[1])
    living = (query_pos >= 0) & (query_pos < frames)
    return (
        near_rows
        & (query_start[:, None] == key_info[0][None, :])
        & usable[None, :]
        & living[:, None]
    )


def prompt_mask(query_start, cand_starts, cand_lens):
    offsets = jnp.arange(PMAX, dtype=jnp.int32)
    matched = (query_start[:, None, None] == cand_starts[None, :, None]) & (
        offsets[None, None, :] < cand_lens[None, :, None]
    )
    return matched.reshape(query_start.shape[0], -1)


def head_group(query_part, cotan_part, key_part, value_part, allowed, bias_part, score_scale):
    scores = (
        jnp.einsum("rhd,khd->hrk", query_part, key_part, preferred_element_type=jnp.float32)
        * score_scale
        + bias_part[:, None, :]
    )
    scores = jnp.where(allowed[None], scores, -1e30)
    row_max = jnp.max(scores, axis=2, keepdims=True)
    raised = jnp.where(allowed[None], jnp.exp(scores - row_max), 0.0)
    row_total = jnp.sum(raised, axis=2, keepdims=True)
    probs = raised / row_total
    low_probs = probs.astype(jnp.bfloat16)
    attended = jnp.einsum("hrk,khd->rhd", low_probs, value_part, preferred_element_type=jnp.float32)
    dprobs = jnp.einsum("rhd,khd->hrk", cotan_part, value_part, preferred_element_type=jnp.float32)
    row_delta = jnp.sum(probs * dprobs, axis=2, keepdims=True)
    dscores = probs * (dprobs - row_delta)
    low_dscores = (dscores * score_scale).astype(jnp.bfloat16)
    grad_q = jnp.einsum("hrk,khd->rhd", low_dscores, key_part, preferred_element_type=jnp.float32)
    grad_k = jnp.einsum("hrk,rhd->khd", low_dscores, query_part, preferred_element_type=jnp.float32)
    grad_v = jnp.einsum("hrk,rhd->khd", low_probs, cotan_part, preferred_element_type=jnp.float32)
    return (
        attended,
        grad_q,
        grad_k,
        grad_v,
        jnp.sum(dscores, axis=1),
        row_max[:, :, 0],
        row_total[:, :, 0],
        row_delta[:, :, 0],
    )


def keep_later(earlier, later):
    chosen = later[1][0] > 0
    return (jnp.where(chosen, later[0], earlier[0]), jnp.maximum(earlier[1], later[1]))


def add_until_start(earlier, later):
    stopped = later[1][0] > 0
    return (later[0] + jnp.where(stopped, 0.0, earlier[0]), jnp.maximum(earlier[1], later[1]))


def local(queries, key_rows, values, cotangent, slot_starts, prompt_lens, prompt_bias):
    query_rows = queries[0]
    key_local = key_rows[0]
    value_local = values[0]
    cotan_rows = cotangent[0]
    starts = slot_starts[0]
    plens = prompt_lens[0]
    row_count, width = query_rows.shape
    head_count = prompt_bias.shape[0]
    head_width = width // head_count
    score_scale = 1.0 / math.sqrt(head_width)
    shard_count = lax.axis_size("ctx")
    frames = row_count * shard_count
    shard_index = lax.axis_index("ctx")
    first_frame = shard_index * row_count
    slot_count = starts.shape[0] // shard_count
    window_len = row_count + 2 * HW
    earlier_starts = (starts >= 0) & (starts < first_frame)
    carried = jnp.max(jnp.where(earlier_starts, starts, -3))
    carried_len = jnp.sum(jnp.where(earlier_starts & (starts == carried), plens, 0))
    local_starts = lax.dynamic_slice_in_dim(starts, shard_index * slot_count, slot_count)
    local_lens = lax.dynamic_slice_in_dim(plens, shard_index * slot_count, slot_count)
    anchors = jnp.clip(local_starts - first_frame, 0, row_count - PMAX)
    joined = jnp.concatenate([key_local, value_local], axis=1)
    prompts = jnp.stack([lax.dynamic_slice_in_dim(joined, anchors[0], PMAX, 0)])
    started = jnp.sum((local_starts >= 0).astype(jnp.int32))
    last_slot = jnp.maximum(started - 1, 0)
    has_start = jnp.minimum(started, 1).reshape(1)
    own_prompt = lax.dynamic_index_in_dim(prompts, last_slot, 0, keepdims=False)
    carried_kv = entering(
        (own_prompt, has_start),
        "ctx",
        keep_later,
        (jnp.zeros_like(own_prompt), jnp.zeros((1,), jnp.int32)),
        False,
    )[0]
    window = with_halo(joined, (("ctx", 0),), HW)
    key_block = jnp.concatenate(
        [window, carried_kv, prompts.reshape(slot_count * PMAX, 2 * width)], axis=0
    )
    query_pos = first_frame + jnp.arange(row_count, dtype=jnp.int32)
    key_pos = first_frame - HW + jnp.arange(window_len, dtype=jnp.int32)
    query_start = utterance_info(query_pos, starts, plens)[0]
    cand_starts = jnp.concatenate([carried.reshape(1), local_starts])
    cand_lens = jnp.concatenate([carried_len.reshape(1), local_lens])
    allowed = jnp.concatenate(
        [
            window_mask(query_pos, key_pos, starts, plens, frames),
            prompt_mask(query_start, cand_starts, cand_lens),
        ],
        axis=1,
    )
    prompt_cols = (slot_count + 1) * PMAX
    column_bias = jnp.concatenate(
        [
            jnp.zeros((head_count, window_len), jnp.float32),
            jnp.broadcast_to(prompt_bias[:, None], (head_count, prompt_cols)),
        ],
        axis=1,
    )
    groups = 4
    per_group = head_count // groups

    def split_heads(rows_in):
        return jnp.moveaxis(rows_in.reshape(rows_in.shape[0], groups, per_group, head_width), 1, 0)

    def join_heads(stacked):
        return jnp.moveaxis(stacked, 0, 1).reshape(stacked.shape[1], width)

    def run_group(pieces):
        return head_group(
            pieces[0], pieces[1], pieces[2], pieces[3], allowed, pieces[4], score_scale
        )

    results = lax.map(
        run_group,
        (
            split_heads(query_rows),
            split_heads(cotan_rows),
            split_heads(key_block[:, :width]),
            split_heads(key_block[:, width:]),
            column_bias.reshape(groups, per_group, -1),
        ),
    )
    attended = join_heads(results[0]).astype(jnp.bfloat16)
    grad_q = join_heads(results[1]).astype(jnp.bfloat16)
    grad_kv = jnp.concatenate([join_heads(results[2]), join_heads(results[3])], axis=1)
    bias_terms = results[4].reshape(head_count, -1)
    own_grad = grad_kv[HW : HW + row_count]
    from_right = shifted(grad_kv[:HW].astype(jnp.bfloat16), "ctx", -1).astype(jnp.float32)
    from_left = shifted(grad_kv[row_count + HW : window_len].astype(jnp.bfloat16), "ctx", 1).astype(
        jnp.float32
    )
    own_grad = own_grad.at[row_count - HW :].add(from_right).at[:HW].add(from_left)
    carried_grad = grad_kv[window_len : window_len + PMAX]
    slot_grads = grad_kv[window_len + PMAX :].reshape(slot_count, PMAX, 2 * width)
    returned = entering(
        (carried_grad, has_start),
        "ctx",
        add_until_start,
        (jnp.zeros_like(carried_grad), jnp.zeros((1,), jnp.int32)),
        True,
    )[0]
    slot_grads = slot_grads.at[last_slot].add(jnp.where(has_start[0] > 0, returned, 0.0))
    current = lax.dynamic_slice_in_dim(own_grad, anchors[0], PMAX, 0)
    own_grad = lax.dynamic_update_slice_in_dim(own_grad, current + slot_grads[0], anchors[0], 0)
    local_bias = jnp.sum(bias_terms[:, window_len:], axis=1)
    grad_bias = lax.psum(local_bias, ("dp", "ctx"))
    return (
        attended[None],
        grad_q[None],
        own_grad[:, :width].astype(jnp.bfloat16)[None],
        own_grad[:, width:].astype(jnp.bfloat16)[None],
        grad_bias,
    )


def solution(mesh):
    return jax.shard_map(
        local,
        mesh=mesh,
        in_specs=(
            P("dp", "ctx", None),
            P("dp", "ctx", None),
            P("dp", "ctx", None),
            P("dp", "ctx", None),
            P("dp", None),
            P("dp", None),
            P(),
        ),
        out_specs=(
            P("dp", "ctx", None),
            P("dp", "ctx", None),
            P("dp", "ctx", None),
            P("dp", "ctx", None),
            P(),
        ),
        check_vma=False,
    )
```

profile of v0, /device:TPU:4, one launch (start us, length us, event | category | flops | bytes accessed | tf_op | source)
XLA Modules:
  0.0 1936.9 jit_solution(1600335913525713917)
XLA Ops:
  15.8 4.8 collective-permute-start
  30.2 33.7 %all-reduce.1 = s32[64]{0:T(128)S(1)} all-reduce(s32[64]{0:T(128)S(1)} %get-tuple-element.429), channel_id=2, replica_groups=mesh['dp'=4,'ctx'=64] {'ctx'}, use_global_device_ids=true, to_apply=%add.1 | all-reduce | flops 64 | bytes 512
  67.9 441.1 %all-gather.6.cloned.1.call-done = bf16[8192,2048]{0,1:T(8,128)(2,1)} async-done(((bf16[128,2048]{0,1:T(8,128)(2,1)}), bf16[8192,2048]{0,1:T(8,128)(2,1)}) %all-gather.6.cloned.1.call-update) | async-done | bytes 33554448 | tf_op jit(solution)/shard_map/all_gather | solution.py:14
  509.0 41.3 %copy.61 = bf16[8192,2048]{1,0:T(8,128)(2,1)} copy(bf16[8192,2048]{0,1:T(8,128)(2,1)} %all-gather.6.cloned.1.call-done) | data formatting | bytes 67108864
  550.3 161.5 %while.50 = (s32[]{:T(128)}, bf16[128,2048]{1,0:T(8,128)(2,1)S(1)}, s32[]{:T(128)}, s32[64,1]{0,1:T(1,128)S(1)}, bf16[64,128,2048]{2,1,0:T(8,128)(2,1)}, /*index=5*/s32[]{:T(128)}, s32[]{:T(128)}) while((s32[]{:T(128)}, bf16[128,2048]{1,0:T(8,128)(2,1)S(1)}, s32[]{:T(128)}, s32[64,1]{0,1:T(1,128)S(1)}, ...), condition=%wide.region_1.2_spmd.clone, body=%wide.region_0.1_spmd.clone.sunk | while | flops 786437 | bytes 1572975 | solution.py:26
  716.1 93.1 %while.49 = (s32[]{:T(128)}, bf16[4,256,2,128]{1,3,2,0:T(8,128)(2,1)}, bf16[4,256,2,128]{1,3,2,0:T(8,128)(2,1)}, f32[4,768,2,128]{1,3,2,0:T(8,128)}, f32[4,768,2...) while((s32[]{:T(128)}, ...), condition=%wide.region_12.13_spmd, body=%wide.region_7.12_spmd.sunk | while | flops 615779328 | bytes 45541592 | solution.py:195
  720.5 5.4 fusion.138
  731.6 5.1 fusion.137
  743.8 5.5 fusion.138
  754.9 5.1 fusion.137
  767.0 5.4 fusion.138
  778.2 5.1 fusion.137
  790.3 5.5 fusion.138
  801.5 5.1 fusion.137
  811.6 3.5 copy.65
  820.0 9.6 collective-permute-done.2
  838.2 780.7 %psum.7 = f32[8]{0:T(128)} all-reduce(f32[8]{0:T(128)S(1)} %slice_reduce_fusion), channel_id=1, replica_groups=mesh['dp'=4,'ctx'=64] {'dp','ctx'}, use_global_device_ids=true, to_apply=%region_17.18 | all-reduce | flops 8 | bytes 64 | tf_op jit(solution)/shard_map/psum | solution.py:228
  1625.5 43.5 %rev.6 = f32[64,128,2048]{2,1,0:T(8,128)} reverse(f32[64,128,2048]{2,1,0:T(8,128)} %bitcast.48), dimensions={0} | reverse | bytes 134217728 | tf_op jit(solution)/shard_map/rev | solution.py:16
  1669.0 249.8 %while.51 = (s32[]{:T(128)}, f32[128,2048]{1,0:T(8,128)}, s32[]{:T(128)}, f32[64,128,2048]{2,1,0:T(8,128)}, s32[64,1]{0,1:T(1,128)S(1)}, /*index=5*/s32[]{:T(128)}, s32[]{:T(128)}) while((s32[]{:T(128)}, f32[128,2048]{1,0:T(8,128)}, s32[]{:T(128)}, f32[64,128,2048]{2,1,0:T(8,128)}, s32[64,1]{0,1:T(1,128)S(1)}, ...), condition=%wide.region_15.16_spmd.clone, body=%wide.region_14.15_spmd.clone.sunk | while | flops 1048581 | bytes 3145839 | solution.py:26
  1673.3 3.4 fusion.143
  1681.2 3.4 fusion.143
  1685.2 3.4 fusion.143
  1693.1 3.4 fusion.143
  1697.1 3.4 fusion.143
  1709.0 3.4 fusion.143
  1720.9 3.4 fusion.143
  1732.8 3.4 fusion.143
  1744.7 3.4 fusion.143
  1748.7 3.4 fusion.143
  1756.6 3.4 fusion.143
  1918.8 4.2 fusion.66
  1923.0 4.3 dynamic_update_slice.21
  (380 shorter events, 474.0 us)
Async XLA Ops:
  7.2 501.8 %all-gather.6.cloned.1.call-start = ((), (), s32[]{:S(2)}) async-start(), calls=%async_computation | async-start | bytes 34078720 | tf_op jit(solution)/shard_map/all_gather | solution.py:14
  13.4 8.4 copy-start.8
  13.4 9.0 copy-start.7
  13.5 14.7 copy-start.5
  15.7 13.5 copy-start.6
  15.7 14.4 copy-start.9
  15.7 1609.8 %all-gather.8.cloned.1.call-start = ((), (), s32[]{:S(2)}) async-start(), calls=%async_computation.1 | async-start | bytes 68157440 | tf_op jit(solution)/shard_map/all_gather | solution.py:14
  15.8 48.2 %collective-permute-start = (bf16[128,2048]{0,1:T(8,128)(2,1)}, bf16[128,2048]{0,1:T(8,128)(2,1)}, u32[]{:S(2)}, u32[]{:S(2)}) collective-permute-start(bf16[128,2048]{0,1:T(8,128)(2,1)} %get-tuple-element.427), channel_id=1, source_target_pairs={{0,1},{1,2},{2,3},{3,4},{4,5},{5,6},{6,7},{7,8},{8,9},{9,10},{10,1... | collective-permute-start | bytes 1572872 | tf_op jit(solution)/shard_map/ppermute | solution.py:34
  20.5 46.5 %collective-permute-start.1 = (bf16[128,2048]{0,1:T(8,128)(2,1)}, bf16[128,2048]{0,1:T(8,128)(2,1)S(1)}, u32[]{:S(2)}, u32[]{:S(2)}) collective-permute-start(bf16[128,2048]{0,1:T(8,128)(2,1)} %get-tuple-element.428), channel_id=1, source_target_pairs={{1,0},{2,1},{3,2},{4,3},{5,4},{6,5},{7,6},{8,7},{9,8},{10,9},{11,1... | collective-permute-start | bytes 1572872 | tf_op jit(solution)/shard_map/ppermute | solution.py:37
  711.8 1.2 copy-start.2
  716.1 3.1 copy-start.3
  726.0 2.8 copy-start.10
  736.7 2.7 copy-start.4
  739.4 3.1 copy-start.3
  749.2 2.8 copy-start.10
  760.0 2.7 copy-start.4
  762.6 3.1 copy-start.3
  772.5 2.8 copy-start.10
  783.2 2.7 copy-start.4
  785.9 3.1 copy-start.3
  795.7 2.9 copy-start.10
  806.5 2.7 copy-start.4
  815.1 4.7 copy-start
  818.5 11.1 collective-permute-start.2
  830.8 1.4 copy-start.1
  832.2 790.9 %collective-permute-start.3 = (bf16[128,2048]{1,0:T(8,128)(2,1)}, bf16[128,2048]{1,0:T(8,128)(2,1)}, u32[]{:S(2)}, u32[]{:S(2)}) collective-permute-start(bf16[128,2048]{1,0:T(8,128)(2,1)} %get-tuple-element.420), channel_id=1, source_target_pairs={{0,1},{1,2},{2,3},{3,4},{4,5},{5,6},{6,7},{7,8},{8,9},{9,10},{10,1... | collective-permute-start | bytes 1572872 | tf_op jit(solution)/shard_map/ppermute | solution.py:45
Sparse Core Ops, SparseCore 0:
  15.8 493.1 all-gather.5
  832.3 726.0 all-gather.7
where the time goes:
time: 1950 us; the launch traced here: 1940 us
  blocking collectives  814 us (42%)
  waiting for transfers between devices  451 us (23%)
  other arithmetic  447 us (23%)
  local copies, waits for them, and re-layouts  116 us (6%)
  matrix products  81.6 us (4%)
    psum x1, blocking collectives, local(): grad_bias = lax.psum(local_bias, ('dp', 'ctx'))  781 us
    all_gather x2, waiting for transfers between devices, entering(): pieces = jax.tree.map(lambda part: lax.all_gather(part, axis), value)  441 us
    select_n x126, other arithmetic, lap(): jnp.where(position < mine, new, old)  336 us
    unnamed x27, local copies, waits for them, and re-layouts  52.4 us
    rev x1, local copies, waits for them, and re-layouts, entering(): pieces = jax.tree.map(lambda part: part[::-1], pieces)  43.5 us
  transfers between devices with their start and end apart: 6, of which 2 were waited for; matrix products, arithmetic and copies ran while one was open for 1% of the time, Pallas kernels for 0%

commit v1 on v0

v1 whole, which is shorter than its diff:
```python
import math

import jax
import jax.numpy as jnp
from jax import lax
from jax.experimental import pallas as pl
from jax.experimental.pallas import tpu as pltpu
from jax.sharding import PartitionSpec as P

HW = 128
PMAX = 128
ROWS = 256
HD = 128
HEADS = 8
WIDTH = HEADS * HD
BANDS = 8
BAND = PMAX // BANDS
NEG = -1e30
LOG2E = math.log2(math.e)
SCALE = 1.0 / math.sqrt(HD)

SMEM = pl.BlockSpec(memory_space=pltpu.SMEM)
VMEM = pl.BlockSpec(memory_space=pltpu.VMEM)
PARAMS = pltpu.CompilerParams(vmem_limit_bytes=48 * 1024 * 1024)


def nt(a, b):
    return lax.dot_general(a, b, (((1,), (1,)), ((), ())), preferred_element_type=jnp.float32)


def tn(a, b):
    return lax.dot_general(a, b, (((0,), (0,)), ((), ())), preferred_element_type=jnp.float32)


def nn(a, b):
    return lax.dot_general(a, b, (((1,), (0,)), ((), ())), preferred_element_type=jnp.float32)


def own_start(starts_ref, me):
    start = starts_ref[0, me]
    return start >= 0, jnp.where(start >= 0, start - me * ROWS, 0)


def columns(head):
    return slice(head * HD, (head + 1) * HD)


def cut_kernel(starts_ref, k_ref, v_ref, out_ref):
    me = lax.axis_index("ctx")
    offset = own_start(starts_ref, me)[1]
    row = lax.broadcasted_iota(jnp.int32, (PMAX, ROWS), 0)
    frame = lax.broadcasted_iota(jnp.int32, (PMAX, ROWS), 1)
    pick = (frame == row + offset).astype(jnp.bfloat16)
    for head in range(HEADS):
        for part, ref in enumerate((k_ref, v_ref)):
            rows = nn(pick, ref[0, :, columns(head)]).astype(jnp.bfloat16)
            out_ref[:, head, part * BAND : (part + 1) * BAND, :] = rows.reshape(BANDS, BAND, HD)


def cut_prompt(starts, key_rows, values):
    return pl.pallas_call(
        cut_kernel,
        out_shape=jax.ShapeDtypeStruct((BANDS, HEADS, 2 * BAND, HD), jnp.bfloat16),
        in_specs=[SMEM, VMEM, VMEM],
        out_specs=VMEM,
        compiler_params=PARAMS,
        name="cut_prompt",
    )(starts, key_rows, values)


def route_kernel(starts_ref, in_ref, out_ref):
    count = in_ref.shape[0]

    def step(target, source):
        out_ref[target] = in_ref[source]
        return jnp.where(starts_ref[0, target] >= 0, target, source)

    lax.fori_loop(0, count, step, jnp.int32(0), unroll=8)


def route(starts, pieces):
    return pl.pallas_call(
        route_kernel,
        out_shape=jax.ShapeDtypeStruct(pieces.shape, pieces.dtype),
        in_specs=[SMEM, VMEM],
        out_specs=VMEM,
        compiler_params=PARAMS,
        name="route",
    )(starts, pieces)


def gather_kernel(starts_ref, in_ref, out_ref, bias_ref):
    count = in_ref.shape[0]
    out_ref[...] = jnp.zeros_like(out_ref)

    def step(target, carry):
        source, total, bias = carry
        block = in_ref[target].astype(jnp.float32)
        total = total + block[: 2 * BAND]
        out_ref[source] = total.astype(jnp.bfloat16)
        bias = bias + block[2 * BAND : 2 * BAND + HEADS] + block[2 * BAND + HEADS :]
        begins = starts_ref[0, target] >= 0
        return jnp.where(begins, target, source), jnp.where(begins, 0.0, total), bias

    first = in_ref[0].astype(jnp.float32)
    bias = first[2 * BAND : 2 * BAND + HEADS] + first[2 * BAND + HEADS :]
    carry = (jnp.int32(0), jnp.zeros((2 * BAND, HD), jnp.float32), bias)
    bias_ref[...] = lax.fori_loop(1, count, step, carry, unroll=7)[2]


def gather(starts, pieces):
    return pl.pallas_call(
        gather_kernel,
        out_shape=(
            jax.ShapeDtypeStruct((pieces.shape[0], 2 * BAND, HD), jnp.bfloat16),
            jax.ShapeDtypeStruct((HEADS, HD), jnp.float32),
        ),
        in_specs=[SMEM, VMEM],
        out_specs=(VMEM, VMEM),
        compiler_params=PARAMS,
        name="gather",
    )(starts, pieces)


def attention_kernel(
    starts_ref,
    lens_ref,
    bias_ref,
    q_ref,
    d_ref,
    k_ref,
    v_ref,
    low_ref,
    high_ref,
    prompt_ref,
    attended_ref,
    gq_ref,
    gk_ref,
    gv_ref,
    glow_ref,
    ghigh_ref,
    gprompt_ref,
    own_mask,
    own_flag,
    low_mask,
    high_mask,
    prompt_mask,
    bias_sums,
):
    head = pl.program_id(0)
    me = lax.axis_index("ctx")
    last = starts_ref.shape[1] - 1

    @pl.when(head == 0)
    def _():
        begins, offset = own_start(starts_ref, me)
        offset = jnp.where(begins, offset, ROWS)
        own_len = jnp.where(begins, lens_ref[0, me], 0)

        def carried_info(index, found):
            used = starts_ref[0, index] >= 0
            return (
                jnp.where(used, starts_ref[0, index], found[0]),
                jnp.where(used, lens_ref[0, index], found[1]),
            )

        start, length = lax.fori_loop(0, me, carried_info, (jnp.int32(0), jnp.int32(0)))
        prompt_end = start + length - (me * ROWS - HW)
        after = jnp.minimum(me + 1, last)
        next_begins, next_offset = own_start(starts_ref, after)
        next_offset = jnp.where(next_begins, next_offset, HW)
        next_offset = jnp.where(me < last, next_offset, 0)

        def hold(ref, allowed):
            ref[...] = jnp.where(allowed, 0.0, NEG)

        key = lax.broadcasted_iota(jnp.int32, (ROWS, ROWS), 0)
        row = lax.broadcasted_iota(jnp.int32, (ROWS, ROWS), 1)
        prompt = (key >= offset) & (key < offset + own_len)
        near = jnp.abs(row - key) <= HW
        hold(own_mask, ((row >= offset) == (key >= offset)) & (prompt | near))
        own_flag[...] = prompt[:, :HW].astype(jnp.float32)
        key = lax.broadcasted_iota(jnp.int32, (HW, HW), 0)
        row = lax.broadcasted_iota(jnp.int32, (HW, HW), 1)
        hold(low_mask, (key >= row) & (row < offset) & (key >= prompt_end) & (me > 0))
        hold(high_mask, (key <= row) & (key < next_offset))
        key = lax.broadcasted_iota(jnp.int32, (PMAX, ROWS), 0)
        row = lax.broadcasted_iota(jnp.int32, (PMAX, ROWS), 1)
        hold(prompt_mask, (row < offset) & (key < length))
        bias_sums[...] = jnp.zeros_like(bias_sums)

    q, d, k, v = q_ref[0], d_ref[0], k_ref[0], v_ref[0]
    kl, vl = low_ref[0], low_ref[1]
    kr, vr = high_ref[0], high_ref[1]
    kp = prompt_ref[:, 0, :BAND, :].reshape(PMAX, HD)
    vp = prompt_ref[:, 0, BAND:, :].reshape(PMAX, HD)
    bias = bias_ref[head] * LOG2E
    s_own, s_prompt = nt(k, q), nt(kp, q)
    dp_own, dp_prompt = nt(v, d), nt(vp, d)
    own_probs, own_ds, prompt_probs, prompt_ds = [], [], [], []
    bias_sum = jnp.zeros((1, HW), jnp.float32)
    for half, (kh, vh, mask_ref) in enumerate(((kl, vl, low_mask), (kr, vr, high_mask))):
        part = slice(half * HW, (half + 1) * HW)
        q_half, d_half = q[part], d[part]
        scores = [
            nt(kh, q_half) * (SCALE * LOG2E) + mask_ref[...],
            s_own[:, part] * (SCALE * LOG2E) + (own_mask[:, part] + own_flag[...] * bias),
            s_prompt[:, part] * (SCALE * LOG2E) + (prompt_mask[:, part] + bias),
        ]
        dprobs = [nt(vh, d_half), dp_own[:, part], dp_prompt[:, part]]
        tops = [jnp.max(x, axis=0, keepdims=True) for x in scores]
        top = jnp.maximum(jnp.maximum(tops[0], tops[1]), tops[2])
        raised = [jnp.exp2(x - top) for x in scores]
        sums = [jnp.sum(x, axis=0, keepdims=True) for x in raised]
        inverse = 1.0 / (sums[0] + sums[1] + sums[2])
        probs = [x * inverse for x in raised]
        deltas = [jnp.sum(x * y, axis=0, keepdims=True) for x, y in zip(probs, dprobs)]
        delta = deltas[0] + deltas[1] + deltas[2]
        dscores = [(x * SCALE) * (y - delta) for x, y in zip(probs, dprobs)]
        bias_sum = (
            bias_sum
            + jnp.sum(dscores[1] * own_flag[...], axis=0, keepdims=True)
            + jnp.sum(dscores[2], axis=0, keepdims=True)
        )
        low_probs = [x.astype(jnp.bfloat16) for x in probs]
        low_ds = [x.astype(jnp.bfloat16) for x in dscores]
        attended = tn(low_probs[0], vh) + tn(low_probs[1], v) + tn(low_probs[2], vp)
        attended_ref[0, part, :] = attended.astype(jnp.bfloat16)
        grad_q = tn(low_ds[0], kh) + tn(low_ds[1], k) + tn(low_ds[2], kp)
        gq_ref[0, part, :] = grad_q.astype(jnp.bfloat16)
        ref = (glow_ref, ghigh_ref)[half]
        ref[0] = nn(low_ds[0], q_half).astype(jnp.bfloat16)
        ref[1] = nn(low_probs[0], d_half).astype(jnp.bfloat16)
        own_probs.append(low_probs[1])
        own_ds.append(low_ds[1])
        prompt_probs.append(low_probs[2])
        prompt_ds.append(low_ds[2])

    gk_ref[...] = nn(jnp.concatenate(own_ds, axis=1), q)
    gv_ref[...] = nn(jnp.concatenate(own_probs, axis=1), d)
    gkp = nn(jnp.concatenate(prompt_ds, axis=1), q).astype(jnp.bfloat16)
    gvp = nn(jnp.concatenate(prompt_probs, axis=1), d).astype(jnp.bfloat16)
    gprompt_ref[:, pl.ds(head, 1), :BAND, :] = gkp.reshape(BANDS, 1, BAND, HD)
    gprompt_ref[:, pl.ds(head, 1), BAND : 2 * BAND, :] = gvp.reshape(BANDS, 1, BAND, HD)
    bias_sums[pl.ds(head, 1), :] = bias_sum * (1.0 / SCALE)

    @pl.when(head == HEADS - 1)
    def _():
        sums = bias_sums[...]
        upper = sums.astype(jnp.bfloat16)
        lower = (sums - upper.astype(jnp.float32)).astype(jnp.bfloat16)
        tile = jnp.concatenate([upper, lower], axis=0)
        for band in range(BANDS):
            for member in range(HEADS):
                gprompt_ref[band, member, 2 * BAND :, :] = tile


def attention(starts, lens, bias, queries, cotangent, key_rows, values, low, high, prompt):
    rows = pl.BlockSpec((1, ROWS, HD), lambda head: (0, 0, head))
    halo = pl.BlockSpec((2, HW, HD), lambda head: (0, 0, head))
    pieces = pl.BlockSpec((BANDS, 1, 2 * BAND, HD), lambda head: (0, head, 0, 0))
    total = pl.BlockSpec((ROWS, HD), lambda head: (0, head))
    whole = pl.BlockSpec((BANDS, HEADS, 2 * BAND + 2 * HEADS, HD), lambda head: (0, 0, 0, 0))
    return pl.pallas_call(
        attention_kernel,
        grid=(HEADS,),
        out_shape=(
            jax.ShapeDtypeStruct((1, ROWS, WIDTH), jnp.bfloat16),
            jax.ShapeDtypeStruct((1, ROWS, WIDTH), jnp.bfloat16),
            jax.ShapeDtypeStruct((ROWS, WIDTH), jnp.float32),
            jax.ShapeDtypeStruct((ROWS, WIDTH), jnp.float32),
            jax.ShapeDtypeStruct((2, HW, WIDTH), jnp.bfloat16),
            jax.ShapeDtypeStruct((2, HW, WIDTH), jnp.bfloat16),
            jax.ShapeDtypeStruct((BANDS, HEADS, 2 * BAND + 2 * HEADS, HD), jnp.bfloat16),
        ),
        in_specs=[SMEM, SMEM, SMEM, rows, rows, rows, rows, halo, halo, pieces],
        out_specs=(rows, rows, total, total, halo, halo, whole),
        scratch_shapes=[
            pltpu.VMEM((ROWS, ROWS), jnp.float32),
            pltpu.VMEM((ROWS, HW), jnp.float32),
            pltpu.VMEM((HW, HW), jnp.float32),
            pltpu.VMEM((HW, HW), jnp.float32),
            pltpu.VMEM((PMAX, ROWS), jnp.float32),
            pltpu.VMEM((HEADS, HW), jnp.float32),
        ],
        compiler_params=PARAMS,
        cost_estimate=pl.CostEstimate(
            flops=2 * 6 * ROWS * 640 * WIDTH, bytes_accessed=10 << 20, transcendentals=1 << 20
        ),
        name="attention",
    )(starts, lens, bias, queries, cotangent, key_rows, values, low, high, prompt)


def finish_kernel(starts_ref, gk_ref, gv_ref, left_ref, right_ref, prompt_ref, outk_ref, outv_ref):
    me = lax.axis_index("ctx")
    begins, offset = own_start(starts_ref, me)
    offset = jnp.where(begins, offset, 2 * ROWS)
    frame = lax.broadcasted_iota(jnp.int32, (ROWS, PMAX), 0)
    row = lax.broadcasted_iota(jnp.int32, (ROWS, PMAX), 1)
    place = (frame == row + offset).astype(jnp.bfloat16)
    for head in range(HEADS):
        cols = columns(head)
        for part, (ref, out) in enumerate(((gk_ref, outk_ref), (gv_ref, outv_ref))):
            piece = prompt_ref[:, head, part * BAND : (part + 1) * BAND, :].reshape(PMAX, HD)
            total = ref[:, cols] + nn(place, piece)
            sides = jnp.concatenate([left_ref[part, :, cols], right_ref[part, :, cols]], axis=0)
            out[0, :, cols] = (total + sides.astype(jnp.float32)).astype(jnp.bfloat16)


def finish(starts, gk, gv, left, right, prompt):
    return pl.pallas_call(
        finish_kernel,
        out_shape=(jax.ShapeDtypeStruct((1, ROWS, WIDTH), jnp.bfloat16),) * 2,
        in_specs=[SMEM, VMEM, VMEM, VMEM, VMEM, VMEM],
        out_specs=(VMEM, VMEM),
        compiler_params=PARAMS,
        name="finish",
    )(starts, gk, gv, left, right, prompt)


def exchange(pieces):
    return lax.all_to_all(pieces, "ctx", 0, 0, tiled=True)


def shifted(x, by):
    peers = lax.axis_size("ctx")
    return lax.ppermute(x, "ctx", [(i, i + by) for i in range(peers) if 0 <= i + by < peers])


def local(queries, key_rows, values, cotangent, starts, lens, bias):
    count = lax.axis_size("ctx")
    cut = cut_prompt(starts, key_rows, values)
    held = exchange(cut.reshape(count, 2 * BAND, HD))
    low = shifted(jnp.concatenate([key_rows[:, HW:], values[:, HW:]], axis=0), 1)
    high = shifted(jnp.concatenate([key_rows[:, :HW], values[:, :HW]], axis=0), -1)
    prompt = exchange(route(starts, held)).reshape(BANDS, HEADS, 2 * BAND, HD)
    attended, grad_q, gk, gv, glow, ghigh, gprompt = attention(
        starts, lens, bias, queries, cotangent, key_rows, values, low, high, prompt
    )
    held = exchange(gprompt.reshape(count, 2 * BAND + 2 * HEADS, HD))
    right = shifted(glow, -1)
    left = shifted(ghigh, 1)
    owned, bias_sums = gather(starts, held)
    peers = lax.axis_size("dp")
    others = [
        lax.ppermute(bias_sums, "dp", [(i, i ^ step) for i in range(peers)])
        for step in range(1, peers)
    ]
    total = (bias_sums + others[0]) + (others[1] + others[2])
    grad_bias = jnp.sum(total, axis=1)
    returned = exchange(owned).reshape(BANDS, HEADS, 2 * BAND, HD)
    grad_k, grad_v = finish(starts, gk, gv, left, right, returned)
    return attended, grad_q, grad_k, grad_v, grad_bias


def solution(mesh):
    split = P("dp", "ctx", None)
    return jax.shard_map(
        local,
        mesh=mesh,
        in_specs=(split, split, split, split, P("dp", None), P("dp", None), P()),
        out_specs=(split, split, split, split, P()),
        check_vma=False,
    )
```

time: 1950 us -> 152 us (0.08)
  the two profiles are of different devices: /device:TPU:4 before, /device:TPU:24 now
where the time goes in v1:
time: 152 us; the launch traced here: 151 us
  blocking collectives  57.5 us (38%)
  starting transfers between devices  37 us (24%)
  waiting for transfers between devices  28 us (18%)
  Pallas kernels  19 us (12%)
  local copies, waits for them, and re-layouts  8.35 us (5%)
    all_to_all x2, blocking collectives, exchange(): return lax.all_to_all(pieces, 'ctx', 0, 0, tiled=True)  57.5 us
    ppermute x4, waiting for transfers between devices, shifted(): lax.ppermute(x, 'ctx', [(i, i + by) for i in range(peers) if 0 <= i + by...  26.1 us
    ppermute x4, starting transfers between devices, shifted(): lax.ppermute(x, 'ctx', [(i, i + by) for i in range(peers) if 0 <= i + by...  17.8 us
    all_to_all x2, starting transfers between devices, exchange(): return lax.all_to_all(pieces, 'ctx', 0, 0, tiled=True)  15.7 us
    pallas_call x1, Pallas kernels, attention(): pl.pallas_call(attention_kernel, grid=(HEADS,), out_shape=(jax.ShapeDtype...  12.9 us
    unnamed x40, local copies, waits for them, and re-layouts  8.28 us
    ppermute x3, starting transfers between devices, local(): lax.ppermute(bias_sums, 'dp', [(i, i ^ step) for i in range(peers)])  3.44 us
  transfers between devices with their start and end apart: 9, of which 4 were waited for; matrix products, arithmetic and copies ran while one was open for 1% of the time, Pallas kernels for 0%

profile of v1, /device:TPU:24, one launch (start us, length us, event | category | flops | bytes accessed | tf_op | source)
XLA Modules:
  0.0 151.5 jit_solution(9290377091956132310)
XLA Ops:
  0.6 1.0 copy-done
  1.7 1.0 copy-done.2
  2.7 0.7 copy-done.8
  3.4 1.0 cut_prompt.1
  4.4 29.1 %all_to_all.20.in_ref = bf16[64,32,128]{2,1,0:T(8,128)(2,1)S(1)} all-to-all(bf16[64,32,128]{2,1,0:T(8,128)(2,1)S(1)} %bitcast.4), channel_id=1, replica_groups=mesh['dp'=4,'ctx'=64] {'ctx'}, dimensions={0} | all-to-all | bytes 1048576 | tf_op jit(solution)/shard_map/all_to_all | solution.py:322
  33.4 1.5 route.1
  34.9 7.6 %all-to-all-start.1 = ((bf16[64,32,128]{2,1,0:T(8,128)(2,1)}), bf16[64,32,128]{2,1,0:T(8,128)(2,1)S(1)}, u32[]{:S(2)}, u32[]{:S(2)}) async-start(bf16[64,32,128]{2,1,0:T(8,128)(2,1)} %route.1), calls=%async_computation.1 | async-start | bytes 1048576 | tf_op jit(solution)/shard_map/all_to_all | solution.py:322
  42.5 0.1 fusion
  42.6 0.1 pad_maximum_fusion
  42.7 3.4 %collective-permute-start = (bf16[2,128,1024]{2,1,0:T(8,128)(2,1)S(1)}, bf16[2,128,1024]{2,1,0:T(8,128)(2,1)S(1)}, u32[]{:S(2)}, u32[]{:S(2)}) collective-permute-start(bf16[2,128,1024]{2,1,0:T(8,128)(2,1)S(1)} %pad_maximum_fusion), channel_id=1, source_target_pairs={{0,1},{1,2},{2,3},{3,4},{4,5},{5,6},{6,7},{7,8},{8,9},{9,10},{10,1... | collective-permute-start | bytes 1572872 | tf_op jit(solution)/shard_map/ppermute | solution.py:327
  46.2 5.6 %collective-permute-start.1 = (bf16[2,128,1024]{2,1,0:T(8,128)(2,1)S(1)}, bf16[2,128,1024]{2,1,0:T(8,128)(2,1)S(1)}, u32[]{:S(2)}, u32[]{:S(2)}) collective-permute-start(bf16[2,128,1024]{2,1,0:T(8,128)(2,1)S(1)} %pad_maximum_fusion.1), channel_id=1, source_target_pairs={{1,0},{2,1},{3,2},{4,3},{5,4},{6,5},{7,6},{8,7},{9,8},{10,9},{11,1... | collective-permute-start | bytes 1572872 | tf_op jit(solution)/shard_map/ppermute | solution.py:327
  51.8 16.1 %collective-permute-done.low_ref = bf16[2,128,1024]{2,1,0:T(8,128)(2,1)S(1)} collective-permute-done((bf16[2,128,1024]{2,1,0:T(8,128)(2,1)S(1)}, bf16[2,128,1024]{2,1,0:T(8,128)(2,1)S(1)}, u32[]{:S(2)}, u32[]{:S(2)}) %collective-permute-start) | collective-permute-done | bytes 524320 | tf_op jit(solution)/shard_map/ppermute | solution.py:327
  67.9 0.8 copy-done.14
  68.7 0.8 copy-done.16
  69.5 1.0 copy-done.15
  70.6 1.0 copy-done.17
  71.6 12.9 %attention.1 = (bf16[1,256,1024]{2,1,0:T(8,128)(2,1)}, bf16[1,256,1024]{2,1,0:T(8,128)(2,1)}, f32[256,1024]{1,0:T(8,128)}, f32[256,1024]{1,0:T(8,128)}, bf16[2,1...) custom-call(s32[1,64]{1,0:T(1,128)S(1)} %copy-done.9, ...), custom_call_target="tpu_custom_call" | custom-call | flops 2013265920 | bytes 10485760 | tf_op jit(solution)/shard_map/attention/pallas_call | solution.py:264
  84.5 28.5 %all_to_all.21.in_ref = bf16[64,48,128]{2,1,0:T(8,128)(2,1)S(1)} all-to-all(bf16[64,48,128]{2,1,0:T(8,128)(2,1)S(1)} %bitcast.6), channel_id=1, replica_groups=mesh['dp'=4,'ctx'=64] {'ctx'}, dimensions={0} | all-to-all | bytes 1572864 | tf_op jit(solution)/shard_map/all_to_all | solution.py:322
  112.9 1.6 %gather.1 = (bf16[64,32,128]{2,1,0:T(8,128)(2,1)}, f32[8,128]{1,0:T(8,128)S(1)}) custom-call(s32[1,64]{1,0:T(1,128)S(1)} %copy-done.9, bf16[64,48,128]{2,1,0:T(8,128)(2,1)S(1)} %all_to_all.21.in_ref), custom_call_target="tpu_custom_call" | custom-call | tf_op jit(solution)/shard_map/gather/pallas_call | solution.py:112
  114.6 8.1 %all-to-all-start.3 = ((bf16[64,32,128]{2,1,0:T(8,128)(2,1)}), bf16[64,32,128]{2,1,0:T(8,128)(2,1)S(1)}, u32[]{:S(2)}, u32[]{:S(2)}) async-start(bf16[64,32,128]{2,1,0:T(8,128)(2,1)} %get-tuple-element.23), calls=%async_computation.3 | async-start | bytes 1048576 | tf_op jit(solution)/shard_map/all_to_all | solution.py:322
  122.6 3.4 %collective-permute-start.2 = (bf16[2,128,1024]{2,1,0:T(8,128)(2,1)}, bf16[2,128,1024]{2,1,0:T(8,128)(2,1)S(1)}, u32[]{:S(2)}, u32[]{:S(2)}) collective-permute-start(bf16[2,128,1024]{2,1,0:T(8,128)(2,1)} %copy-done.13), channel_id=1, source_target_pairs={{0,1},{1,2},{2,3},{3,4},{4,5},{5,6},{6,7},{7,8},{8,9},{9,10},{10,1... | collective-permute-start | bytes 1572872 | tf_op jit(solution)/shard_map/ppermute | solution.py:327
  126.0 5.5 %collective-permute-start.3 = (bf16[2,128,1024]{2,1,0:T(8,128)(2,1)}, bf16[2,128,1024]{2,1,0:T(8,128)(2,1)S(1)}, u32[]{:S(2)}, u32[]{:S(2)}) collective-permute-start(bf16[2,128,1024]{2,1,0:T(8,128)(2,1)} %copy-done.12), channel_id=1, source_target_pairs={{1,0},{2,1},{3,2},{4,3},{5,4},{6,5},{7,6},{8,7},{9,8},{10,9},{11,1... | collective-permute-start | bytes 1572872 | tf_op jit(solution)/shard_map/ppermute | solution.py:327
  131.5 0.1 collective-permute-start.6
  131.6 2.8 %collective-permute-start.5 = (f32[8,128]{1,0:T(8,128)S(1)}, f32[8,128]{1,0:T(8,128)S(1)}, u32[]{:S(2)}, u32[]{:S(2)}) collective-permute-start(f32[8,128]{1,0:T(8,128)S(1)} %get-tuple-element.26), channel_id=1, source_target_pairs={{0,128},{64,192},{128,0},{192,64},{1,129},{65,193},{129,1},{193,65... | collective-permute-start | bytes 12296 | tf_op jit(solution)/shard_map/ppermute | solution.py:346
  134.4 0.5 collective-permute-start.4
  135.0 1.2 collective-permute-done.6
  136.2 0.7 collective-permute-done.5
  136.9 0.6 add_reduce_fusion
  137.5 10.0 %collective-permute-done.2.left_ref = bf16[2,128,1024]{2,1,0:T(8,128)(2,1)S(1)} collective-permute-done((bf16[2,128,1024]{2,1,0:T(8,128)(2,1)}, bf16[2,128,1024]{2,1,0:T(8,128)(2,1)S(1)}, u32[]{:S(2)}, u32[]{:S(2)}) %collective-permute-start.2) | collective-permute-done | bytes 524320 | tf_op jit(solution)/shard_map/ppermute | solution.py:327
  147.5 0.8 copy-done.6
  148.3 1.0 copy-done.7
  149.4 2.1 %finish.1 = (bf16[1,256,1024]{2,1,0:T(8,128)(2,1)}, bf16[1,256,1024]{2,1,0:T(8,128)(2,1)}) custom-call(s32[1,64]{1,0:T(1,128)S(1)} %copy-done.9, f32[256,1024]{1,0:T(8,128)S(1)} %copy-done.4, f32[256,1024]{1,0:T(8,128)S(1)} %copy-done.5, bf16[2,128,1024]{2,1,0:T(8,128)(2,1)S(1)} %collective-permute-done.2.left_ref, bf16[2,128,1024]{2,1,0:T(8,128)(2,1)S(1)} %copy-done.7, ...), custom_call_target="tpu_custom_call" | custom-call | tf_op jit(solution)/shard_map/finish/pallas_call | solution.py:311
  (37 shorter events, 0.1 us)
Async XLA Ops:
  0.6 1.0 copy-start
  1.7 1.0 copy-start.2
  2.7 0.7 copy-start.8
  34.9 7.6 %copy-start.1 = (bf16[1,256,1024]{2,1,0:T(8,128)(2,1)S(1)}, bf16[1,256,1024]{2,1,0:T(8,128)(2,1)}, u32[]{:S(2)}) copy-start(bf16[1,256,1024]{2,1,0:T(8,128)(2,1)} %k_ref.3) | copy-start | bytes 1572868
  34.9 7.6 %copy-start.3 = (bf16[1,256,1024]{2,1,0:T(8,128)(2,1)S(1)}, bf16[1,256,1024]{2,1,0:T(8,128)(2,1)}, u32[]{:S(2)}) copy-start(bf16[1,256,1024]{2,1,0:T(8,128)(2,1)} %v_ref.3) | copy-start | bytes 1572868
  34.9 34.6 %all-to-all-start.1 = ((bf16[64,32,128]{2,1,0:T(8,128)(2,1)}), bf16[64,32,128]{2,1,0:T(8,128)(2,1)S(1)}, u32[]{:S(2)}, u32[]{:S(2)}) async-start(bf16[64,32,128]{2,1,0:T(8,128)(2,1)} %route.1), calls=%async_computation.1 | async-start | bytes 1048576 | tf_op jit(solution)/shard_map/all_to_all | solution.py:322
  42.7 25.2 %collective-permute-start = (bf16[2,128,1024]{2,1,0:T(8,128)(2,1)S(1)}, bf16[2,128,1024]{2,1,0:T(8,128)(2,1)S(1)}, u32[]{:S(2)}, u32[]{:S(2)}) collective-permute-start(bf16[2,128,1024]{2,1,0:T(8,128)(2,1)S(1)} %pad_maximum_fusion), channel_id=1, source_target_pairs={{0,1},{1,2},{2,3},{3,4},{4,5},{5,6},{6,7},{7,8},{8,9},{9,10},{10,1... | collective-permute-start | bytes 1572872 | tf_op jit(solution)/shard_map/ppermute | solution.py:327
  46.1 23.4 %copy-start.10 = (bf16[1,256,1024]{2,1,0:T(8,128)(2,1)S(1)}, bf16[1,256,1024]{2,1,0:T(8,128)(2,1)}, u32[]{:S(2)}) copy-start(bf16[1,256,1024]{2,1,0:T(8,128)(2,1)} %q_ref.1) | copy-start | bytes 1572868
  46.1 23.4 %copy-start.11 = (bf16[1,256,1024]{2,1,0:T(8,128)(2,1)S(1)}, bf16[1,256,1024]{2,1,0:T(8,128)(2,1)}, u32[]{:S(2)}) copy-start(bf16[1,256,1024]{2,1,0:T(8,128)(2,1)} %d_ref.1) | copy-start | bytes 1572868
  46.2 23.3 %copy-start.9 = (s32[1,64]{1,0:T(1,128)S(1)}, s32[1,64]{1,0:T(1,128)}, u32[]{:S(2)}) copy-start(s32[1,64]{1,0:T(1,128)} %starts_ref.9) | copy-start | bytes 772
  46.2 23.3 %copy-start.18 = (s32[1,64]{1,0:T(1,128)S(1)}, s32[1,64]{1,0:T(1,128)}, u32[]{:S(2)}) copy-start(s32[1,64]{1,0:T(1,128)} %lens_ref.1) | copy-start | bytes 772
  46.2 23.3 %copy-start.19 = (f32[8]{0:T(128)S(1)}, f32[8]{0:T(128)}, u32[]{:S(2)}) copy-start(f32[8]{0:T(128)} %bias_ref.1) | copy-start | bytes 100
  46.2 22.5 %collective-permute-start.1 = (bf16[2,128,1024]{2,1,0:T(8,128)(2,1)S(1)}, bf16[2,128,1024]{2,1,0:T(8,128)(2,1)S(1)}, u32[]{:S(2)}, u32[]{:S(2)}) collective-permute-start(bf16[2,128,1024]{2,1,0:T(8,128)(2,1)S(1)} %pad_maximum_fusion.1), channel_id=1, source_target_pairs={{1,0},{2,1},{3,2},{4,3},{5,4},{6,5},{7,6},{8,7},{9,8},{10,9},{11,1... | collective-permute-start | bytes 1572872 | tf_op jit(solution)/shard_map/ppermute | solution.py:327
  67.9 0.8 copy-start.14
  68.7 0.8 copy-start.16
  69.5 1.0 copy-start.15
  70.6 1.0 copy-start.17
  84.5 28.5 %copy-start.12 = (bf16[2,128,1024]{2,1,0:T(8,128)(2,1)}, bf16[2,128,1024]{2,1,0:T(8,128)(2,1)S(1)}, u32[]{:S(2)}) copy-start(bf16[2,128,1024]{2,1,0:T(8,128)(2,1)S(1)} %get-tuple-element.21) | copy-start | bytes 1572868
  84.5 28.5 %copy-start.13 = (bf16[2,128,1024]{2,1,0:T(8,128)(2,1)}, bf16[2,128,1024]{2,1,0:T(8,128)(2,1)S(1)}, u32[]{:S(2)}) copy-start(bf16[2,128,1024]{2,1,0:T(8,128)(2,1)S(1)} %get-tuple-element.20) | copy-start | bytes 1572868
  84.5 63.8 %copy-start.5 = (f32[256,1024]{1,0:T(8,128)S(1)}, f32[256,1024]{1,0:T(8,128)}, u32[]{:S(2)}) copy-start(f32[256,1024]{1,0:T(8,128)} %get-tuple-element.19.gv_ref) | copy-start | bytes 3145732
  112.9 35.4 %copy-start.4 = (f32[256,1024]{1,0:T(8,128)S(1)}, f32[256,1024]{1,0:T(8,128)}, u32[]{:S(2)}) copy-start(f32[256,1024]{1,0:T(8,128)} %get-tuple-element.18.gk_ref) | copy-start | bytes 3145732
  114.6 33.7 %all-to-all-start.3 = ((bf16[64,32,128]{2,1,0:T(8,128)(2,1)}), bf16[64,32,128]{2,1,0:T(8,128)(2,1)S(1)}, u32[]{:S(2)}, u32[]{:S(2)}) async-start(bf16[64,32,128]{2,1,0:T(8,128)(2,1)} %get-tuple-element.23), calls=%async_computation.3 | async-start | bytes 1048576 | tf_op jit(solution)/shard_map/all_to_all | solution.py:322
  122.6 24.9 %collective-permute-start.2 = (bf16[2,128,1024]{2,1,0:T(8,128)(2,1)}, bf16[2,128,1024]{2,1,0:T(8,128)(2,1)S(1)}, u32[]{:S(2)}, u32[]{:S(2)}) collective-permute-start(bf16[2,128,1024]{2,1,0:T(8,128)(2,1)} %copy-done.13), channel_id=1, source_target_pairs={{0,1},{1,2},{2,3},{3,4},{4,5},{5,6},{6,7},{7,8},{8,9},{9,10},{10,1... | collective-permute-start | bytes 1572872 | tf_op jit(solution)/shard_map/ppermute | solution.py:327
  126.0 21.5 %collective-permute-start.3 = (bf16[2,128,1024]{2,1,0:T(8,128)(2,1)}, bf16[2,128,1024]{2,1,0:T(8,128)(2,1)S(1)}, u32[]{:S(2)}, u32[]{:S(2)}) collective-permute-start(bf16[2,128,1024]{2,1,0:T(8,128)(2,1)} %copy-done.12), channel_id=1, source_target_pairs={{1,0},{2,1},{3,2},{4,3},{5,4},{6,5},{7,6},{8,7},{9,8},{10,9},{11,1... | collective-permute-start | bytes 1572872 | tf_op jit(solution)/shard_map/ppermute | solution.py:327
  131.5 4.7 %collective-permute-start.6 = (f32[8,128]{1,0:T(8,128)S(1)}, f32[8,128]{1,0:T(8,128)S(1)}, u32[]{:S(2)}, u32[]{:S(2)}) collective-permute-start(f32[8,128]{1,0:T(8,128)S(1)} %get-tuple-element.26), channel_id=1, source_target_pairs={{0,192},{64,128},{128,64},{192,0},{1,193},{65,129},{129,65},{193,1... | collective-permute-start | bytes 12296 | tf_op jit(solution)/shard_map/ppermute | solution.py:346
  131.6 5.3 %collective-permute-start.5 = (f32[8,128]{1,0:T(8,128)S(1)}, f32[8,128]{1,0:T(8,128)S(1)}, u32[]{:S(2)}, u32[]{:S(2)}) collective-permute-start(f32[8,128]{1,0:T(8,128)S(1)} %get-tuple-element.26), channel_id=1, source_target_pairs={{0,128},{64,192},{128,0},{192,64},{1,129},{65,193},{129,1},{193,65... | collective-permute-start | bytes 12296 | tf_op jit(solution)/shard_map/ppermute | solution.py:346
  134.4 2.5 %collective-permute-start.4 = (f32[8,128]{1,0:T(8,128)S(1)}, f32[8,128]{1,0:T(8,128)S(1)}, u32[]{:S(2)}, u32[]{:S(2)}) collective-permute-start(f32[8,128]{1,0:T(8,128)S(1)} %get-tuple-element.26), channel_id=1, source_target_pairs={{0,64},{64,0},{128,192},{192,128},{1,65},{65,1},{129,193},{193,129... | collective-permute-start | bytes 12296 | tf_op jit(solution)/shard_map/ppermute | solution.py:346
  147.5 0.8 copy-start.6
  148.3 1.0 copy-start.7

commit v2 on v1

v2 whole, which is shorter than its diff:
```python
import math

import jax
import jax.numpy as jnp
from jax import lax
from jax.experimental import pallas as pl
from jax.experimental.pallas import tpu as pltpu
from jax.sharding import PartitionSpec as P

HW = 128
PMAX = 128
ROWS = 256
HD = 128
HEADS = 8
WIDTH = HEADS * HD
BANDS = 8
BAND = PMAX // BANDS
SENT = 2 * BAND + HEADS
GROUP = 2
STAGED = 4
NEG = -1e30
LOG2E = math.log2(math.e)
SCALE = 1.0 / math.sqrt(HD)
FACTOR = SCALE * LOG2E

SMEM = pl.BlockSpec(memory_space=pltpu.SMEM)
VMEM = pl.BlockSpec(memory_space=pltpu.VMEM)
HBM = pl.BlockSpec(memory_space=pltpu.HBM)
PARAMS = pltpu.CompilerParams(vmem_limit_bytes=20 * 1024 * 1024)
FROM_HBM = pltpu.CompilerParams(vmem_limit_bytes=60 * 1024 * 1024)


def nt(a, b):
    return lax.dot_general(a, b, (((1,), (1,)), ((), ())), preferred_element_type=jnp.float32)


def tn(a, b):
    return lax.dot_general(a, b, (((0,), (0,)), ((), ())), preferred_element_type=jnp.float32)


def nn(a, b):
    return lax.dot_general(a, b, (((1,), (0,)), ((), ())), preferred_element_type=jnp.float32)


def own_start(starts_ref, me):
    start = starts_ref[0, me]
    return start >= 0, jnp.where(start >= 0, start - me * ROWS, 0)


def columns(head):
    return slice(head * HD, (head + 1) * HD)


def float_array(*shape):
    return jax.ShapeDtypeStruct(shape, jnp.float32)


def low_array(*shape):
    return jax.ShapeDtypeStruct(shape, jnp.bfloat16)


def cut_kernel(starts_ref, k_hbm, v_hbm, out_ref, last_hbm, first_hbm, k_ref, v_ref, sems, out_sems):
    me = lax.axis_index("ctx")
    offset = own_start(starts_ref, me)[1]
    halves = (slice(0, HW), slice(HW, ROWS))
    loads, stores = [], []
    for part, (source, ref) in enumerate(((k_hbm, k_ref), (v_hbm, v_ref))):
        for half, (rows, target) in enumerate(zip(halves, (first_hbm, last_hbm))):
            loads.append(
                pltpu.make_async_copy(source.at[0, rows, :], ref.at[rows, :], sems.at[part, half])
            )
            stores.append(
                pltpu.make_async_copy(ref.at[rows, :], target.at[part], out_sems.at[part, half])
            )
    for copy in loads:
        copy.start()
    row = lax.broadcasted_iota(jnp.int32, (PMAX, ROWS), 0)
    frame = lax.broadcasted_iota(jnp.int32, (PMAX, ROWS), 1)
    pick = (frame == row + offset).astype(jnp.bfloat16)
    for load, store in zip(loads, stores):
        load.wait()
        store.start()
    for head in range(HEADS):
        for part, ref in enumerate((k_ref, v_ref)):
            rows = nn(pick, ref[:, columns(head)]).astype(jnp.bfloat16)
            out_ref[:, head, part * BAND : (part + 1) * BAND, :] = rows.reshape(BANDS, BAND, HD)
    for store in stores:
        store.wait()


def cut_prompt(starts, key_rows, values):
    return pl.pallas_call(
        cut_kernel,
        out_shape=(
            low_array(BANDS, HEADS, 2 * BAND, HD),
            low_array(2, HW, WIDTH),
            low_array(2, HW, WIDTH),
        ),
        in_specs=[SMEM, HBM, HBM],
        out_specs=(VMEM, HBM, HBM),
        scratch_shapes=[
            pltpu.VMEM((ROWS, WIDTH), jnp.bfloat16),
            pltpu.VMEM((ROWS, WIDTH), jnp.bfloat16),
            pltpu.SemaphoreType.DMA((2, 2)),
            pltpu.SemaphoreType.DMA((2, 2)),
        ],
        compiler_params=FROM_HBM,
        name="cut_prompt",
    )(starts, key_rows, values)


def route_kernel(starts_ref, in_ref, out_ref):
    count = in_ref.shape[0]

    def step(target, source):
        out_ref[target] = in_ref[source]
        return jnp.where(starts_ref[0, target] >= 0, target, source)

    lax.fori_loop(0, count, step, jnp.int32(0), unroll=8)


def route(starts, pieces):
    return pl.pallas_call(
        route_kernel,
        out_shape=jax.ShapeDtypeStruct(pieces.shape, pieces.dtype),
        in_specs=[SMEM, VMEM],
        out_specs=VMEM,
        compiler_params=PARAMS,
        name="route",
    )(starts, pieces)


def gather_kernel(starts_ref, in_ref, out_ref, sums_ref):
    count = in_ref.shape[0]
    out_ref[...] = jnp.zeros_like(out_ref)

    def step(target, carry):
        source, total, sums = carry
        block = in_ref[target].astype(jnp.float32)
        total = total + block[: 2 * BAND]
        sums = sums + block[2 * BAND :]
        out_ref[source] = total.astype(jnp.bfloat16)
        begins = starts_ref[0, target] >= 0
        return jnp.where(begins, target, source), jnp.where(begins, 0.0, total), sums

    sums = in_ref[0].astype(jnp.float32)[2 * BAND :]
    carry = (jnp.int32(0), jnp.zeros((2 * BAND, HD), jnp.float32), sums)
    sums_ref[...] = lax.fori_loop(1, count, step, carry, unroll=7)[2]


def gather(starts, pieces):
    return pl.pallas_call(
        gather_kernel,
        out_shape=(low_array(pieces.shape[0], 2 * BAND, HD), float_array(HEADS, HD)),
        in_specs=[SMEM, VMEM],
        out_specs=(VMEM, VMEM),
        compiler_params=PARAMS,
        name="gather",
    )(starts, pieces)


def carried_prompt(starts_ref, lens_ref, me):
    def later(index, found):
        used = starts_ref[0, index] >= 0
        return (
            jnp.where(used, starts_ref[0, index], found[0]),
            jnp.where(used, lens_ref[0, index], found[1]),
        )

    return lax.fori_loop(0, me, later, (jnp.int32(0), jnp.int32(0)))


def grid_of(keys, rows):
    key = lax.broadcasted_iota(jnp.int32, (keys, rows), 0)
    return key, lax.broadcasted_iota(jnp.int32, (keys, rows), 1)


def hold(ref, allowed):
    ref[...] = jnp.where(allowed, 0.0, NEG)


def hold_masks(starts_ref, lens_ref, own_mask, own_flag, halo_mask, prompt_mask):
    me = lax.axis_index("ctx")
    last = starts_ref.shape[1] - 1
    begins, offset = own_start(starts_ref, me)
    offset = jnp.where(begins, offset, ROWS)
    own_len = jnp.where(begins, lens_ref[0, me], 0)
    key, row = grid_of(ROWS, ROWS)
    prompt = (key >= offset) & (key < offset + own_len)
    near = jnp.abs(row - key) <= HW
    hold(own_mask, ((row >= offset) == (key >= offset)) & (prompt | near))
    own_flag[...] = prompt.astype(jnp.float32)
    start, length = carried_prompt(starts_ref, lens_ref, me)
    prompt_end = start + length - (me * ROWS - HW)
    next_begins, next_offset = own_start(starts_ref, jnp.minimum(me + 1, last))
    next_offset = jnp.where(next_begins, next_offset, HW)
    next_offset = jnp.where(me < last, next_offset, 0)
    key, row = grid_of(HW, HW)
    hold(halo_mask.at[0], (key >= row) & (row < offset) & (key >= prompt_end) & (me > 0))
    hold(halo_mask.at[1], (key <= row) & (key < next_offset))
    key, row = grid_of(PMAX, ROWS)
    hold(prompt_mask, (row < offset) & (key < length))


def top_of(x):
    return jnp.max(x, axis=0, keepdims=True)


def sum_of(x):
    return jnp.sum(x, axis=0, keepdims=True)


def window_kernel(
    starts_ref,
    lens_ref,
    bias_ref,
    q_ref,
    d_ref,
    k_ref,
    v_ref,
    low_ref,
    high_ref,
    stats_ref,
    own_mask,
    own_flag,
    halo_mask,
    prompt_mask,
):
    head = pl.program_id(0)

    @pl.when(head == 0)
    def _():
        hold_masks(starts_ref, lens_ref, own_mask, own_flag, halo_mask, prompt_mask)

    q, d, k, v = q_ref[0], d_ref[0], k_ref[0], v_ref[0]
    bias = bias_ref[head] * LOG2E
    flag = own_flag[...]
    x_own = nt(k, q) * FACTOR + (own_mask[...] + flag * bias)
    x_low = nt(low_ref[0], q[:HW]) * FACTOR + halo_mask[0]
    x_high = nt(high_ref[0], q[HW:]) * FACTOR + halo_mask[1]
    tops = jnp.concatenate([top_of(x_low), top_of(x_high)], axis=1)
    top = jnp.maximum(top_of(x_own), tops)
    e_own = jnp.exp2(x_own - top)
    e_low = jnp.exp2(x_low - top[:, :HW])
    e_high = jnp.exp2(x_high - top[:, HW:])
    w_own = e_own * nt(v, d)
    w_low = e_low * nt(low_ref[1], d[:HW])
    w_high = e_high * nt(high_ref[1], d[HW:])
    total = sum_of(e_own) + jnp.concatenate([sum_of(e_low), sum_of(e_high)], axis=1)
    weighted = sum_of(w_own) + jnp.concatenate([sum_of(w_low), sum_of(w_high)], axis=1)
    inverse = 1.0 / total
    own_bias = (sum_of(w_own * flag) - weighted * inverse * sum_of(e_own * flag)) * inverse
    stats_ref[0] = jnp.concatenate(
        [top, total, weighted, own_bias, jnp.zeros((4, ROWS), jnp.float32)], axis=0
    )


def head_rows(part=ROWS):
    return pl.BlockSpec((1, part, HD), lambda head: (0, 0, head))


def head_halo():
    return pl.BlockSpec((2, HW, HD), lambda head: (0, 0, head))


def head_tile(*shape):
    return pl.BlockSpec((1, *shape), lambda head: (head,) + (0,) * len(shape))


def head_pieces():
    return pl.BlockSpec((BANDS, 1, 2 * BAND, HD), lambda head: (0, head, 0, 0))


MASKS = (
    float_array(ROWS, ROWS),
    float_array(ROWS, ROWS),
    float_array(2, HW, HW),
    float_array(PMAX, ROWS),
)


def whole(array):
    return pl.BlockSpec(array.shape, lambda head: (0,) * len(array.shape))


def cost(micros):
    return pl.CostEstimate(flops=micros * 10**9, bytes_accessed=8 << 20, transcendentals=0)


def window(starts, lens, bias, queries, cotangent, key_rows, values, low, high):
    rows = head_rows()
    return pl.pallas_call(
        window_kernel,
        grid=(HEADS,),
        out_shape=(float_array(HEADS, 8, ROWS), *MASKS),
        in_specs=[SMEM, SMEM, SMEM, rows, rows, rows, rows, head_halo(), head_halo()],
        out_specs=(head_tile(8, ROWS), *(whole(mask) for mask in MASKS)),
        compiler_params=PARAMS,
        cost_estimate=cost(20),
        name="window",
    )(starts, lens, bias, queries, cotangent, key_rows, values, low, high)


def prompt_kernel(
    bias_ref, q_ref, d_ref, prompt_ref, stats_ref, mask_ref, grad_ref, final_ref
):
    mask = mask_ref[...]
    all_sums = []
    for first in range(0, HEADS, STAGED):
        heads = range(first, first + STAGED)
        rows = [(q_ref[0, :, columns(head)], d_ref[0, :, columns(head)]) for head in heads]
        products = []
        for head, (q, d) in zip(heads, rows):
            kp = prompt_ref[:, head, :BAND, :].reshape(PMAX, HD)
            vp = prompt_ref[:, head, BAND:, :].reshape(PMAX, HD)
            products.append((nt(kp, q), nt(vp, d)))
        settled_rows = []
        for head, (scores, dprobs) in zip(heads, products):
            x = scores * FACTOR + (mask + bias_ref[head] * LOG2E)
            stats = stats_ref[head]
            top = jnp.maximum(stats[0:1], top_of(x))
            rescale = jnp.exp2(stats[0:1] - top)
            raised = jnp.exp2(x - top)
            inverse = 1.0 / (stats[1:2] * rescale + sum_of(raised))
            delta = (stats[2:3] * rescale + sum_of(raised * dprobs)) * inverse
            probs = raised * inverse
            dscores = (probs * SCALE) * (dprobs - delta)
            settled_rows.append((probs.astype(jnp.bfloat16), dscores.astype(jnp.bfloat16)))
            final_ref[head] = jnp.concatenate(
                [top, inverse, delta, jnp.zeros((5, ROWS), jnp.float32)], axis=0
            )
            sums = stats[3:4] + sum_of(dscores) * (1.0 / SCALE)
            all_sums.append(sums[:, :HW] + sums[:, HW:])
        grads = [
            (nn(low_ds, q).astype(jnp.bfloat16), nn(low_probs, d).astype(jnp.bfloat16))
            for (q, d), (low_probs, low_ds) in zip(rows, settled_rows)
        ]
        for head, (gk, gv) in zip(heads, grads):
            grad_ref[:, head, :BAND, :] = gk.reshape(BANDS, BAND, HD)
            grad_ref[:, head, BAND : 2 * BAND, :] = gv.reshape(BANDS, BAND, HD)

    sums = jnp.concatenate(all_sums, axis=0)
    sums = sums + pltpu.roll(sums, HW // 2, 1)
    upper = sums.astype(jnp.bfloat16).astype(jnp.float32)
    lane = lax.broadcasted_iota(jnp.int32, (HEADS, HW), 1)
    tile = jnp.where(lane < HW // 2, upper, sums - upper).astype(jnp.bfloat16)
    for band in range(BANDS):
        for head in range(HEADS):
            grad_ref[band, head, 2 * BAND :, :] = tile


def prompt_part(bias, queries, cotangent, prompt, stats, prompt_mask):
    return pl.pallas_call(
        prompt_kernel,
        out_shape=(low_array(BANDS, HEADS, SENT, HD), float_array(HEADS, 8, ROWS)),
        in_specs=[SMEM, VMEM, VMEM, VMEM, VMEM, VMEM],
        out_specs=(VMEM,) * 2,
        compiler_params=PARAMS,
        cost_estimate=cost(4),
        name="prompt_part",
    )(bias, queries, cotangent, prompt, stats, prompt_mask)


def settled(keys, values, q, d, added, final):
    x = nt(keys, q) * FACTOR + added
    probs = jnp.exp2(x - final[0:1]) * final[1:2]
    dscores = (probs * SCALE) * (nt(values, d) - final[2:3])
    return probs.astype(jnp.bfloat16), dscores.astype(jnp.bfloat16)


def halo_kernel(q_ref, d_ref, low_ref, high_ref, final_ref, mask_ref, glow_ref, ghigh_ref):
    for head in range(HEADS):
        cols = columns(head)
        for half, (ref, out) in enumerate(((low_ref, glow_ref), (high_ref, ghigh_ref))):
            part = slice(half * HW, (half + 1) * HW)
            q, d = q_ref[0, part, cols], d_ref[0, part, cols]
            final = final_ref[head, :, part]
            probs, ds = settled(ref[0, :, cols], ref[1, :, cols], q, d, mask_ref[half], final)
            out[0, :, cols] = nn(ds, q).astype(jnp.bfloat16)
            out[1, :, cols] = nn(probs, d).astype(jnp.bfloat16)


def halo_grads(queries, cotangent, low, high, final, halo_mask):
    return pl.pallas_call(
        halo_kernel,
        out_shape=(low_array(2, HW, WIDTH), low_array(2, HW, WIDTH)),
        in_specs=[VMEM] * 6,
        out_specs=(VMEM, VMEM),
        compiler_params=PARAMS,
        cost_estimate=cost(4),
        name="halo_grads",
    )(queries, cotangent, low, high, final, halo_mask)


def row_kernel(
    bias_ref,
    q_ref,
    d_ref,
    k_ref,
    v_ref,
    low_ref,
    high_ref,
    prompt_ref,
    final_ref,
    own_mask,
    own_flag,
    halo_mask,
    prompt_mask,
    attended_ref,
    gq_ref,
):
    bias = bias_ref[pl.program_id(0)] * LOG2E
    q, d, k, v = q_ref[0], d_ref[0], k_ref[0], v_ref[0]
    kp = prompt_ref[:, 0, :BAND, :].reshape(PMAX, HD)
    vp = prompt_ref[:, 0, BAND:, :].reshape(PMAX, HD)
    final = final_ref[0]
    probs, ds = settled(k, v, q, d, own_mask[...] + own_flag[...] * bias, final)
    prompt_probs, prompt_ds = settled(kp, vp, q, d, prompt_mask[...] + bias, final)
    attended = tn(probs, v) + tn(prompt_probs, vp)
    grad_q = tn(ds, k) + tn(prompt_ds, kp)
    for half, ref in enumerate((low_ref, high_ref)):
        part = slice(half * HW, (half + 1) * HW)
        probs, ds = settled(ref[0], ref[1], q[part], d[part], halo_mask[half], final[:, part])
        attended_ref[0, part, :] = (attended[part] + tn(probs, ref[1])).astype(jnp.bfloat16)
        gq_ref[0, part, :] = (grad_q[part] + tn(ds, ref[0])).astype(jnp.bfloat16)


def row_part(bias, queries, cotangent, key_rows, values, low, high, prompt, final, masks):
    rows, halo = head_rows(), head_halo()
    return pl.pallas_call(
        row_kernel,
        grid=(HEADS,),
        out_shape=(low_array(1, ROWS, WIDTH), low_array(1, ROWS, WIDTH)),
        in_specs=[SMEM, rows, rows, rows, rows, halo, halo, head_pieces(), head_tile(8, ROWS)]
        + [whole(mask) for mask in MASKS],
        out_specs=(rows, rows),
        compiler_params=PARAMS,
        cost_estimate=cost(10),
        name="row_part",
    )(bias, queries, cotangent, key_rows, values, low, high, prompt, final, *masks)


def own_kernel(
    bias_ref,
    q_ref,
    d_ref,
    k_ref,
    v_ref,
    final_ref,
    own_mask,
    own_flag,
    left_ref,
    right_ref,
    gk_ref,
    gv_ref,
):
    q, d = q_ref[0], d_ref[0]
    added = own_mask[...] + own_flag[...] * (bias_ref[pl.program_id(0)] * LOG2E)
    probs, ds = settled(k_ref[0], v_ref[0], q, d, added, final_ref[0])
    for part, (ref, total) in enumerate(((gk_ref, nn(ds, q)), (gv_ref, nn(probs, d)))):
        sides = jnp.concatenate([left_ref[part], right_ref[part]], axis=0)
        ref[...] = total + sides.astype(jnp.float32)


def own_part(bias, queries, cotangent, key_rows, values, final, masks, left, right):
    rows, halo = head_rows(), head_halo()
    total = pl.BlockSpec((ROWS, HD), lambda head: (0, head))
    return pl.pallas_call(
        own_kernel,
        grid=(HEADS,),
        out_shape=(float_array(ROWS, WIDTH), float_array(ROWS, WIDTH)),
        in_specs=[SMEM, rows, rows, rows, rows, head_tile(8, ROWS)]
        + [whole(mask) for mask in MASKS[:2]]
        + [halo, halo],
        out_specs=(total, total),
        compiler_params=FROM_HBM,
        cost_estimate=cost(20),
        name="own_part",
    )(bias, queries, cotangent, key_rows, values, final, *masks[:2], left, right)


def finish_kernel(starts_ref, gk_ref, gv_ref, prompt_ref, outk_ref, outv_ref):
    me = lax.axis_index("ctx")
    begins, offset = own_start(starts_ref, me)
    offset = jnp.where(begins, offset, 2 * ROWS)
    frame = lax.broadcasted_iota(jnp.int32, (ROWS, PMAX), 0)
    row = lax.broadcasted_iota(jnp.int32, (ROWS, PMAX), 1)
    place = (frame == row + offset).astype(jnp.bfloat16)
    for member in range(GROUP):
        cols = columns(member)
        for part, (ref, out) in enumerate(((gk_ref, outk_ref), (gv_ref, outv_ref))):
            piece = prompt_ref[:, member, part * BAND : (part + 1) * BAND, :].reshape(PMAX, HD)
            out[0, :, cols] = (ref[:, cols] + nn(place, piece)).astype(jnp.bfloat16)


def finish(starts, gk, gv, prompt):
    total = pl.BlockSpec((ROWS, GROUP * HD), lambda step: (0, step))
    rows = pl.BlockSpec((1, ROWS, GROUP * HD), lambda step: (0, 0, step))
    pieces = pl.BlockSpec((BANDS, GROUP, 2 * BAND, HD), lambda step: (0, step, 0, 0))
    return pl.pallas_call(
        finish_kernel,
        grid=(HEADS // GROUP,),
        out_shape=(low_array(1, ROWS, WIDTH),) * 2,
        in_specs=[SMEM, total, total, pieces],
        out_specs=(rows, rows),
        compiler_params=FROM_HBM,
        name="finish",
    )(starts, gk, gv, prompt)


def exchange(pieces):
    return lax.all_to_all(pieces, "ctx", 0, 0, tiled=True)


def shifted(x, by):
    peers = lax.axis_size("ctx")
    return lax.ppermute(x, "ctx", [(i, i + by) for i in range(peers) if 0 <= i + by < peers])


def partners(x, axis, steps):
    peers = lax.axis_size(axis)
    return [lax.ppermute(x, axis, [(i, i ^ step) for i in range(peers)]) for step in steps]


def summed(x, axis, low, high):
    first, second, third = partners(x, axis, (low, high, low | high))
    return (x + first) + (second + third)


def local(queries, key_rows, values, cotangent, starts, lens, bias):
    count = lax.axis_size("ctx")
    cut, last, first = cut_prompt(starts, key_rows, values)
    held = exchange(cut.reshape(count, 2 * BAND, HD))
    low = shifted(last, 1)
    high = shifted(first, -1)
    stats, *masks = window(
        starts, lens, bias, queries, cotangent, key_rows, values, low, high
    )
    held, stats = lax.optimization_barrier((held, stats))
    prompt = exchange(route(starts, held)).reshape(BANDS, HEADS, 2 * BAND, HD)
    gprompt, final = prompt_part(bias, queries, cotangent, prompt, stats, masks[3])
    held = exchange(gprompt.reshape(count, SENT, HD))
    attended, grad_q = row_part(
        bias, queries, cotangent, key_rows, values, low, high, prompt, final, masks
    )
    final, grad_q = lax.optimization_barrier((final, grad_q))
    glow, ghigh = halo_grads(queries, cotangent, low, high, final, masks[2])
    right = shifted(glow, -1)
    left = shifted(ghigh, 1)
    held, final, glow, ghigh = lax.optimization_barrier((held, final, glow, ghigh))
    owned, sums = gather(starts, held)
    returned = exchange(owned).reshape(BANDS, HEADS, 2 * BAND, HD)
    gk, gv = own_part(bias, queries, cotangent, key_rows, values, final, masks, left, right)
    sums, gk = lax.optimization_barrier((sums, gk))
    grad_bias = jnp.sum(summed(sums, "dp", 1, 2), axis=1)
    grad_k, grad_v = finish(starts, gk, gv, returned)
    return attended, grad_q, grad_k, grad_v, grad_bias


def solution(mesh):
    split = P("dp", "ctx", None)
    return jax.shard_map(
        local,
        mesh=mesh,
        in_specs=(split, split, split, split, P("dp", None), P("dp", None), P()),
        out_specs=(split, split, split, split, P()),
        check_vma=False,
    )
```

time: 152 us -> 140 us (0.921)
  the two profiles are of different devices: /device:TPU:24 before, /device:TPU:25 now
where the time goes in v2:
time: 140 us; the launch traced here: 138 us
  starting transfers between devices  59.9 us (43%)
  Pallas kernels  39.3 us (28%)
  blocking collectives  20.7 us (15%)
  waiting for transfers between devices  9.37 us (7%)
  local copies, waits for them, and re-layouts  7.46 us (5%)
    all_to_all x3, starting transfers between devices, exchange(): return lax.all_to_all(pieces, 'ctx', 0, 0, tiled=True)  24.7 us
    all_to_all x1, blocking collectives, exchange(): return lax.all_to_all(pieces, 'ctx', 0, 0, tiled=True)  20.7 us
    ppermute x4, starting transfers between devices, shifted(): lax.ppermute(x, 'ctx', [(i, i + by) for i in range(peers) if 0 <= i + by...  17.9 us
    ppermute x3, starting transfers between devices, partners(): lax.ppermute(x, axis, [(i, i ^ step) for i in range(peers)])  17.3 us
    pallas_call x1, Pallas kernels, row_part(): pl.pallas_call(row_kernel, grid=(HEADS,), out_shape=(low_array(1, ROWS, W...  8.81 us
    pallas_call x1, Pallas kernels, own_part(): pl.pallas_call(own_kernel, grid=(HEADS,), out_shape=(float_array(ROWS, WI...  7.73 us
    unnamed x38, local copies, waits for them, and re-layouts  7.46 us
    pallas_call x1, Pallas kernels, window(): pl.pallas_call(window_kernel, grid=(HEADS,), out_shape=(float_array(HEADS...  6.38 us
  transfers between devices with their start and end apart: 10, of which 6 were waited for; matrix products, arithmetic and copies ran while one was open for 0% of the time, Pallas kernels for 21%

profile of v2, /device:TPU:25, one launch (start us, length us, event | category | flops | bytes accessed | tf_op | source)
XLA Modules:
  0.0 138.3 jit_solution(4177755413390454166)
XLA Ops:
  0.7 3.6 %cut_prompt.1 = (bf16[8,8,32,128]{3,2,1,0:T(8,128)(2,1)}, bf16[2,128,1024]{2,1,0:T(8,128)(2,1)}, bf16[2,128,1024]{2,1,0:T(8,128)(2,1)}) custom-call(s32[1,64]{1,0:T(1,128)} %starts_ref.9, bf16[1,256,1024]{2,1,0:T(8,128)(2,1)} %k_ref.5, bf16[1,256,1024]{2,1,0:T(8,128)(2,1)} %v_ref.5), custom_call_target="tpu_custom_call" | custom-call | tf_op jit(solution)/shard_map/cut_prompt/pallas_call | solution.py:92
  4.3 3.5 %collective-permute-start = (bf16[2,128,1024]{2,1,0:T(8,128)(2,1)}, bf16[2,128,1024]{2,1,0:T(8,128)(2,1)S(1)}, u32[]{:S(2)}, u32[]{:S(2)}) collective-permute-start(bf16[2,128,1024]{2,1,0:T(8,128)(2,1)} %get-tuple-element.33), channel_id=1, source_target_pairs={{0,1},{1,2},{2,3},{3,4},{4,5},{5,6},{6,7},{7,8},{8,9},{9,10},{10,1... | collective-permute-start | bytes 1572872 | tf_op jit(solution)/shard_map/ppermute | solution.py:517
  7.8 7.0 %collective-permute-start.1 = (bf16[2,128,1024]{2,1,0:T(8,128)(2,1)}, bf16[2,128,1024]{2,1,0:T(8,128)(2,1)}, u32[]{:S(2)}, u32[]{:S(2)}) collective-permute-start(bf16[2,128,1024]{2,1,0:T(8,128)(2,1)} %get-tuple-element.34), channel_id=1, source_target_pairs={{1,0},{2,1},{3,2},{4,3},{5,4},{6,5},{7,6},{8,7},{9,8},{10,9},{11,1... | collective-permute-start | bytes 1572872 | tf_op jit(solution)/shard_map/ppermute | solution.py:517
  14.8 8.6 %all-to-all-start = ((bf16[64,32,128]{2,1,0:T(8,128)(2,1)}), bf16[64,32,128]{2,1,0:T(8,128)(2,1)S(1)}, u32[]{:S(2)}, u32[]{:S(2)}) async-start(bf16[64,32,128]{2,1,0:T(8,128)(2,1)} %bitcast.7), calls=%async_computation | async-start | bytes 1048576 | tf_op jit(solution)/shard_map/all_to_all | solution.py:512
  23.4 1.3 collective-permute-done.low_ref
  24.7 2.1 %collective-permute-done.1.high_ref = bf16[2,128,1024]{2,1,0:T(8,128)(2,1)} collective-permute-done((bf16[2,128,1024]{2,1,0:T(8,128)(2,1)}, bf16[2,128,1024]{2,1,0:T(8,128)(2,1)}, u32[]{:S(2)}, u32[]{:S(2)}) %collective-permute-start.1) | collective-permute-done | bytes 524320 | tf_op jit(solution)/shard_map/ppermute | solution.py:517
  26.9 6.4 %window.1 = (f32[8,8,256]{2,1,0:T(8,128)S(1)}, f32[256,256]{1,0:T(8,128)S(1)}, f32[256,256]{1,0:T(8,128)S(1)}, f32[2,128,128]{2,1,0:T(8,128)S(1)}, f32[128,256]{1,0:T(8,128)S(1)}) custom-call(s32[1,64]{1,0:T(1,128)S(1)} %copy-done.2, s32[1,64]{1,0:T(1,128)S(1)} %copy-done.7, f32[8]{0:T(128)S(1)} %copy-done.8, bf16[1,256,1024]{2,1,0:T(8,128)(2,1)S(1)} %copy-done.3, ...), custom_call_target="tpu_custom_call" | custom-call | flops 20000000000 | bytes 8388608 | tf_op jit(solution)/shard_map/window/pallas_call | solution.py:292
  33.3 0.6 copy-done.11
  33.9 0.7 copy-done.13
  34.6 0.7 copy-done.15
  35.3 1.9 %all-to-all-done.in_ref = bf16[64,32,128]{2,1,0:T(8,128)(2,1)S(1)} async-done(((bf16[64,32,128]{2,1,0:T(8,128)(2,1)}), bf16[64,32,128]{2,1,0:T(8,128)(2,1)S(1)}, u32[]{:S(2)}, u32[]{:S(2)}) %all-to-all-start) | async-done | bytes 524320 | tf_op jit(solution)/shard_map/all_to_all | solution.py:512
  37.2 0.7 route.1
  37.9 20.7 %all_to_all.20 = bf16[64,32,128]{2,1,0:T(8,128)(2,1)S(1)} all-to-all(bf16[64,32,128]{2,1,0:T(8,128)(2,1)S(1)} %route.1), channel_id=1, replica_groups=mesh['dp'=4,'ctx'=64] {'ctx'}, dimensions={0} | all-to-all | bytes 1048576 | tf_op jit(solution)/shard_map/all_to_all | solution.py:512
  58.7 2.6 %prompt_part.1 = (bf16[8,8,40,128]{3,2,1,0:T(8,128)(2,1)}, f32[8,8,256]{2,1,0:T(8,128)S(1)}) custom-call(f32[8]{0:T(128)S(1)} %copy-done.8, bf16[1,256,1024]{2,1,0:T(8,128)(2,1)S(1)} %copy-done.3, bf16[1,256,1024]{2,1,0:T(8,128)(2,1)S(1)} %copy-done.4, bf16[8,8,32,128]{3,2,1,0:T(8,128)(2,1)S(1)} %bitcast.4, f32[8,8,256]{2,1,0:T(8,128)S(1)} %copy-done.12, ...), custom_call_target="tpu_custom_call" | custom-call | flops 4000000000 | bytes 8388608 | tf_op jit(solution)/shard_map/prompt_part/pallas_call | solution.py:353
  61.9 7.2 %all-to-all-start.2 = ((bf16[64,40,128]{2,1,0:T(8,128)(2,1)}), bf16[64,40,128]{2,1,0:T(8,128)(2,1)S(1)}, u32[]{:S(2)}, u32[]{:S(2)}) async-start(bf16[64,40,128]{2,1,0:T(8,128)(2,1)} %bitcast.2), calls=%async_computation.2 | async-start | bytes 1310720 | tf_op jit(solution)/shard_map/all_to_all | solution.py:512
  69.1 1.0 copy-done.6
  70.1 0.8 copy-done.10
  71.0 0.9 copy-done.14
  71.9 0.9 copy-done.16
  72.9 8.8 %row_part.1 = (bf16[1,256,1024]{2,1,0:T(8,128)(2,1)}, bf16[1,256,1024]{2,1,0:T(8,128)(2,1)}) custom-call(f32[8]{0:T(128)S(1)} %copy-done.8, bf16[1,256,1024]{2,1,0:T(8,128)(2,1)S(1)} %copy-done.3, bf16[1,256,1024]{2,1,0:T(8,128)(2,1)S(1)} %copy-done.4, bf16[1,256,1024]{2,1,0:T(8,128)(2,1)S(1)} %copy-done, bf16[1,256,1024]{2,1,0:T(8,128)(2,1)S(1)} %copy-done.1, ...), custom_call_target="tpu_custom_call" | custom-call | flops 10000000000 | bytes 8388608 | tf_op jit(solution)/shard_map/row_part/pallas_call | solution.py:430
  81.7 4.0 %halo_grads.1 = (bf16[2,128,1024]{2,1,0:T(8,128)(2,1)S(1)}, bf16[2,128,1024]{2,1,0:T(8,128)(2,1)S(1)}) custom-call(bf16[1,256,1024]{2,1,0:T(8,128)(2,1)S(1)} %copy-done.3, bf16[1,256,1024]{2,1,0:T(8,128)(2,1)S(1)} %copy-done.4, bf16[2,128,1024]{2,1,0:T(8,128)(2,1)S(1)} %copy-done.6, bf16[2,128,1024]{2,1,0:T(8,128)(2,1)} %collective-permute-done.1.high_ref, ...), custom_call_target="tpu_custom_call" | custom-call | flops 4000000000 | bytes 8388608 | tf_op jit(solution)/shard_map/halo_grads/pallas_call | solution.py:384
  85.6 5.5 %collective-permute-start.3 = (bf16[2,128,1024]{2,1,0:T(8,128)(2,1)S(1)}, bf16[2,128,1024]{2,1,0:T(8,128)(2,1)S(1)}, u32[]{:S(2)}, u32[]{:S(2)}) collective-permute-start(bf16[2,128,1024]{2,1,0:T(8,128)(2,1)S(1)} %get-tuple-element.49), channel_id=1, source_target_pairs={{1,0},{2,1},{3,2},{4,3},{5,4},{6,5},{7,6},{8,7},{9,8},{10,9},{11,1... | collective-permute-start | bytes 1572872 | tf_op jit(solution)/shard_map/ppermute | solution.py:517
  91.1 1.9 %collective-permute-start.2 = (bf16[2,128,1024]{2,1,0:T(8,128)(2,1)S(1)}, bf16[2,128,1024]{2,1,0:T(8,128)(2,1)}, u32[]{:S(2)}, u32[]{:S(2)}) collective-permute-start(bf16[2,128,1024]{2,1,0:T(8,128)(2,1)S(1)} %get-tuple-element.50), channel_id=1, source_target_pairs={{0,1},{1,2},{2,3},{3,4},{4,5},{5,6},{6,7},{7,8},{8,9},{9,10},{10,1... | collective-permute-start | bytes 1572872 | tf_op jit(solution)/shard_map/ppermute | solution.py:517
  93.1 1.6 %gather.1 = (bf16[64,32,128]{2,1,0:T(8,128)(2,1)}, f32[8,128]{1,0:T(8,128)S(1)}) custom-call(s32[1,64]{1,0:T(1,128)S(1)} %copy-done.2, bf16[64,40,128]{2,1,0:T(8,128)(2,1)S(1)} %all-to-all-done.2.in_ref), custom_call_target="tpu_custom_call" | custom-call | tf_op jit(solution)/shard_map/gather/pallas_call | solution.py:152
  94.7 8.9 %all-to-all-start.3 = ((bf16[64,32,128]{2,1,0:T(8,128)(2,1)}), bf16[64,32,128]{2,1,0:T(8,128)(2,1)S(1)}, u32[]{:S(2)}, u32[]{:S(2)}) async-start(bf16[64,32,128]{2,1,0:T(8,128)(2,1)} %get-tuple-element.57), calls=%async_computation.3 | async-start | bytes 1048576 | tf_op jit(solution)/shard_map/all_to_all | solution.py:512
  104.4 7.7 %own_part.1 = (f32[256,1024]{1,0:T(8,128)}, f32[256,1024]{1,0:T(8,128)}) custom-call(f32[8]{0:T(128)} %bias_ref.7, bf16[1,256,1024]{2,1,0:T(8,128)(2,1)} %q_ref.9, bf16[1,256,1024]{2,1,0:T(8,128)(2,1)} %d_ref.9, bf16[1,256,1024]{2,1,0:T(8,128)(2,1)} %k_ref.5, bf16[1,256,1024]{2,1,0:T(8,128)(2,1)} %v_ref.5, f32[8,8,256]{2,1,0:T(8,128)} %copy-done.9, ...), custom_call_target="tpu_custom_call" | custom-call | flops 20000000000 | bytes 8388608 | tf_op jit(solution)/shard_map/own_part/pallas_call | solution.py:468
  112.1 16.7 %collective-permute-start.6 = (f32[8,128]{1,0:T(8,128)S(1)}, f32[8,128]{1,0:T(8,128)S(1)}, u32[]{:S(2)}, u32[]{:S(2)}) collective-permute-start(f32[8,128]{1,0:T(8,128)S(1)} %get-tuple-element.60), channel_id=1, source_target_pairs={{0,192},{64,128},{128,64},{192,0},{1,193},{65,129},{129,65},{193,1... | collective-permute-start | bytes 12296 | tf_op jit(solution)/shard_map/ppermute | solution.py:522
  129.4 0.7 collective-permute-done.6
  130.1 2.7 %collective-permute-done.5 = f32[8,128]{1,0:T(8,128)S(1)} collective-permute-done((f32[8,128]{1,0:T(8,128)S(1)}, f32[8,128]{1,0:T(8,128)S(1)}, u32[]{:S(2)}, u32[]{:S(2)}) %collective-permute-start.5) | collective-permute-done | bytes 4128 | tf_op jit(solution)/shard_map/ppermute | solution.py:522
  132.8 0.6 add_reduce_fusion
  133.4 0.8 copy-done.17
  134.2 4.0 %finish.1 = (bf16[1,256,1024]{2,1,0:T(8,128)(2,1)}, bf16[1,256,1024]{2,1,0:T(8,128)(2,1)}) custom-call(s32[1,64]{1,0:T(1,128)} %starts_ref.9, f32[256,1024]{1,0:T(8,128)} %get-tuple-element.55.gk_ref, f32[256,1024]{1,0:T(8,128)} %get-tuple-element.56.gv_ref, bf16[8,8,32,128]{3,2,1,0:T(8,128)(2,1)} %bitcast.6), custom_call_target="tpu_custom_call" | custom-call | tf_op jit(solution)/shard_map/finish/pallas_call | solution.py:500
  (37 shorter events, 2.0 us)
Async XLA Ops:
  0.6 26.2 %copy-start.2 = (s32[1,64]{1,0:T(1,128)S(1)}, s32[1,64]{1,0:T(1,128)}, u32[]{:S(2)}) copy-start(s32[1,64]{1,0:T(1,128)} %starts_ref.9) | copy-start | bytes 772
  0.6 26.2 %copy-start.3 = (bf16[1,256,1024]{2,1,0:T(8,128)(2,1)S(1)}, bf16[1,256,1024]{2,1,0:T(8,128)(2,1)}, u32[]{:S(2)}) copy-start(bf16[1,256,1024]{2,1,0:T(8,128)(2,1)} %q_ref.9) | copy-start | bytes 1572868
  0.7 26.2 %copy-start.4 = (bf16[1,256,1024]{2,1,0:T(8,128)(2,1)S(1)}, bf16[1,256,1024]{2,1,0:T(8,128)(2,1)}, u32[]{:S(2)}) copy-start(bf16[1,256,1024]{2,1,0:T(8,128)(2,1)} %d_ref.9) | copy-start | bytes 1572868
  0.7 26.2 %copy-start.7 = (s32[1,64]{1,0:T(1,128)S(1)}, s32[1,64]{1,0:T(1,128)}, u32[]{:S(2)}) copy-start(s32[1,64]{1,0:T(1,128)} %lens_ref.1) | copy-start | bytes 772
  0.7 26.2 %copy-start.8 = (f32[8]{0:T(128)S(1)}, f32[8]{0:T(128)}, u32[]{:S(2)}) copy-start(f32[8]{0:T(128)} %bias_ref.7) | copy-start | bytes 100
  4.3 20.4 %collective-permute-start = (bf16[2,128,1024]{2,1,0:T(8,128)(2,1)}, bf16[2,128,1024]{2,1,0:T(8,128)(2,1)S(1)}, u32[]{:S(2)}, u32[]{:S(2)}) collective-permute-start(bf16[2,128,1024]{2,1,0:T(8,128)(2,1)} %get-tuple-element.33), channel_id=1, source_target_pairs={{0,1},{1,2},{2,3},{3,4},{4,5},{5,6},{6,7},{7,8},{8,9},{9,10},{10,1... | collective-permute-start | bytes 1572872 | tf_op jit(solution)/shard_map/ppermute | solution.py:517
  7.8 19.0 %collective-permute-start.1 = (bf16[2,128,1024]{2,1,0:T(8,128)(2,1)}, bf16[2,128,1024]{2,1,0:T(8,128)(2,1)}, u32[]{:S(2)}, u32[]{:S(2)}) collective-permute-start(bf16[2,128,1024]{2,1,0:T(8,128)(2,1)} %get-tuple-element.34), channel_id=1, source_target_pairs={{1,0},{2,1},{3,2},{4,3},{5,4},{6,5},{7,6},{8,7},{9,8},{10,9},{11,1... | collective-permute-start | bytes 1572872 | tf_op jit(solution)/shard_map/ppermute | solution.py:517
  14.8 12.1 %copy-start = (bf16[1,256,1024]{2,1,0:T(8,128)(2,1)S(1)}, bf16[1,256,1024]{2,1,0:T(8,128)(2,1)}, u32[]{:S(2)}) copy-start(bf16[1,256,1024]{2,1,0:T(8,128)(2,1)} %k_ref.5) | copy-start | bytes 1572868
  14.8 12.1 %copy-start.1 = (bf16[1,256,1024]{2,1,0:T(8,128)(2,1)S(1)}, bf16[1,256,1024]{2,1,0:T(8,128)(2,1)}, u32[]{:S(2)}) copy-start(bf16[1,256,1024]{2,1,0:T(8,128)(2,1)} %v_ref.5) | copy-start | bytes 1572868
  14.8 22.4 %all-to-all-start = ((bf16[64,32,128]{2,1,0:T(8,128)(2,1)}), bf16[64,32,128]{2,1,0:T(8,128)(2,1)S(1)}, u32[]{:S(2)}, u32[]{:S(2)}) async-start(bf16[64,32,128]{2,1,0:T(8,128)(2,1)} %bitcast.7), calls=%async_computation | async-start | bytes 1048576 | tf_op jit(solution)/shard_map/all_to_all | solution.py:512
  24.7 8.6 %copy-start.5 = (bf16[2,128,1024]{2,1,0:T(8,128)(2,1)}, bf16[2,128,1024]{2,1,0:T(8,128)(2,1)S(1)}, u32[]{:S(2)}) copy-start(bf16[2,128,1024]{2,1,0:T(8,128)(2,1)S(1)} %collective-permute-done.low_ref) | copy-start | bytes 1572868
  33.3 0.6 copy-start.11
  33.9 0.7 copy-start.13
  34.6 0.7 copy-start.15
  37.9 20.8 %copy-start.12 = (f32[8,8,256]{2,1,0:T(8,128)S(1)}, f32[8,8,256]{2,1,0:T(8,128)}, u32[]{:S(2)}) copy-start(f32[8,8,256]{2,1,0:T(8,128)} %copy-done.11) | copy-start | bytes 196612
  61.2 0.6 copy-start.9
  61.9 31.2 %all-to-all-start.2 = ((bf16[64,40,128]{2,1,0:T(8,128)(2,1)}), bf16[64,40,128]{2,1,0:T(8,128)(2,1)S(1)}, u32[]{:S(2)}, u32[]{:S(2)}) async-start(bf16[64,40,128]{2,1,0:T(8,128)(2,1)} %bitcast.2), calls=%async_computation.2 | async-start | bytes 1310720 | tf_op jit(solution)/shard_map/all_to_all | solution.py:512
  69.1 1.0 copy-start.6
  70.1 0.8 copy-start.10
  71.0 0.9 copy-start.14
  71.9 0.9 copy-start.16
  85.6 17.9 %collective-permute-start.3 = (bf16[2,128,1024]{2,1,0:T(8,128)(2,1)S(1)}, bf16[2,128,1024]{2,1,0:T(8,128)(2,1)S(1)}, u32[]{:S(2)}, u32[]{:S(2)}) collective-permute-start(bf16[2,128,1024]{2,1,0:T(8,128)(2,1)S(1)} %get-tuple-element.49), channel_id=1, source_target_pairs={{1,0},{2,1},{3,2},{4,3},{5,4},{6,5},{7,6},{8,7},{9,8},{10,9},{11,1... | collective-permute-start | bytes 1572872 | tf_op jit(solution)/shard_map/ppermute | solution.py:517
  91.1 13.0 %collective-permute-start.2 = (bf16[2,128,1024]{2,1,0:T(8,128)(2,1)S(1)}, bf16[2,128,1024]{2,1,0:T(8,128)(2,1)}, u32[]{:S(2)}, u32[]{:S(2)}) collective-permute-start(bf16[2,128,1024]{2,1,0:T(8,128)(2,1)S(1)} %get-tuple-element.50), channel_id=1, source_target_pairs={{0,1},{1,2},{2,3},{3,4},{4,5},{5,6},{6,7},{7,8},{8,9},{9,10},{10,1... | collective-permute-start | bytes 1572872 | tf_op jit(solution)/shard_map/ppermute | solution.py:517
  94.7 38.8 %all-to-all-start.3 = ((bf16[64,32,128]{2,1,0:T(8,128)(2,1)}), bf16[64,32,128]{2,1,0:T(8,128)(2,1)S(1)}, u32[]{:S(2)}, u32[]{:S(2)}) async-start(bf16[64,32,128]{2,1,0:T(8,128)(2,1)} %get-tuple-element.57), calls=%async_computation.3 | async-start | bytes 1048576 | tf_op jit(solution)/shard_map/all_to_all | solution.py:512
  103.6 0.8 copy-start.18
  112.1 18.0 %collective-permute-start.6 = (f32[8,128]{1,0:T(8,128)S(1)}, f32[8,128]{1,0:T(8,128)S(1)}, u32[]{:S(2)}, u32[]{:S(2)}) collective-permute-start(f32[8,128]{1,0:T(8,128)S(1)} %get-tuple-element.60), channel_id=1, source_target_pairs={{0,192},{64,128},{128,64},{192,0},{1,193},{65,129},{129,65},{193,1... | collective-permute-start | bytes 12296 | tf_op jit(solution)/shard_map/ppermute | solution.py:522
  128.8 4.0 %collective-permute-start.5 = (f32[8,128]{1,0:T(8,128)S(1)}, f32[8,128]{1,0:T(8,128)S(1)}, u32[]{:S(2)}, u32[]{:S(2)}) collective-permute-start(f32[8,128]{1,0:T(8,128)S(1)} %get-tuple-element.60), channel_id=1, source_target_pairs={{0,128},{64,192},{128,0},{192,64},{1,129},{65,193},{129,1},{193,65... | collective-permute-start | bytes 12296 | tf_op jit(solution)/shard_map/ppermute | solution.py:522
  129.4 3.4 %collective-permute-start.4 = (f32[8,128]{1,0:T(8,128)S(1)}, f32[8,128]{1,0:T(8,128)S(1)}, u32[]{:S(2)}, u32[]{:S(2)}) collective-permute-start(f32[8,128]{1,0:T(8,128)S(1)} %get-tuple-element.60), channel_id=1, source_target_pairs={{0,64},{64,0},{128,192},{192,128},{1,65},{65,1},{129,193},{193,129... | collective-permute-start | bytes 12296 | tf_op jit(solution)/shard_map/ppermute | solution.py:522
  133.4 0.8 copy-start.17

commit v3 on v2

--- a/solution.py
+++ b/solution.py
@@ -16,6 +16,7 @@
 BANDS = 8
 BAND = PMAX // BANDS
 SENT = 2 * BAND + HEADS
+SPAN = PMAX + BAND
 GROUP = 2
 STAGED = 4
 NEG = -1e30
@@ -392,7 +393,7 @@
     )(queries, cotangent, low, high, final, halo_mask)
 
 
-def row_kernel(
+def own_kernel(
     bias_ref,
     q_ref,
     d_ref,
@@ -408,6 +409,8 @@
     prompt_mask,
     attended_ref,
     gq_ref,
+    gk_ref,
+    gv_ref,
 ):
     bias = bias_ref[pl.program_id(0)] * LOG2E
     q, d, k, v = q_ref[0], d_ref[0], k_ref[0], v_ref[0]
@@ -416,6 +419,8 @@
     final = final_ref[0]
     probs, ds = settled(k, v, q, d, own_mask[...] + own_flag[...] * bias, final)
     prompt_probs, prompt_ds = settled(kp, vp, q, d, prompt_mask[...] + bias, final)
+    gk_ref[...] = nn(ds, q)
+    gv_ref[...] = nn(probs, d)
     attended = tn(probs, v) + tn(prompt_probs, vp)
     grad_q = tn(ds, k) + tn(prompt_ds, kp)
     for half, ref in enumerate((low_ref, high_ref)):
@@ -425,87 +430,114 @@
         gq_ref[0, part, :] = (grad_q[part] + tn(ds, ref[0])).astype(jnp.bfloat16)
 
 
-def row_part(bias, queries, cotangent, key_rows, values, low, high, prompt, final, masks):
+def own_part(bias, queries, cotangent, key_rows, values, low, high, prompt, final, masks):
     rows, halo = head_rows(), head_halo()
-    return pl.pallas_call(
-        row_kernel,
+    total = pl.BlockSpec((ROWS, HD), lambda head: (0, head))
+    return pl.pallas_call(
+        own_kernel,
         grid=(HEADS,),
-        out_shape=(low_array(1, ROWS, WIDTH), low_array(1, ROWS, WIDTH)),
+        out_shape=(
+            low_array(1, ROWS, WIDTH),
+            low_array(1, ROWS, WIDTH),
+            float_array(ROWS, WIDTH),
+            float_array(ROWS, WIDTH),
+        ),
         in_specs=[SMEM, rows, rows, rows, rows, halo, halo, head_pieces(), head_tile(8, ROWS)]
         + [whole(mask) for mask in MASKS],
-        out_specs=(rows, rows),
-        compiler_params=PARAMS,
+        out_specs=(rows, rows, total, total),
+        compiler_params=FROM_HBM,
         cost_estimate=cost(10),
-        name="row_part",
+        name="own_part",
     )(bias, queries, cotangent, key_rows, values, low, high, prompt, final, *masks)
 
 
-def own_kernel(
-    bias_ref,
-    q_ref,
-    d_ref,
-    k_ref,
-    v_ref,
-    final_ref,
-    own_mask,
-    own_flag,
-    left_ref,
-    right_ref,
-    gk_ref,
-    gv_ref,
-):
-    q, d = q_ref[0], d_ref[0]
-    added = own_mask[...] + own_flag[...] * (bias_ref[pl.program_id(0)] * LOG2E)
-    probs, ds = settled(k_ref[0], v_ref[0], q, d, added, final_ref[0])
-    for part, (ref, total) in enumerate(((gk_ref, nn(ds, q)), (gv_ref, nn(probs, d)))):
-        sides = jnp.concatenate([left_ref[part], right_ref[part]], axis=0)
-        ref[...] = total + sides.astype(jnp.float32)
-
-
-def own_part(bias, queries, cotangent, key_rows, values, final, masks, left, right):
-    rows, halo = head_rows(), head_halo()
-    total = pl.BlockSpec((ROWS, HD), lambda head: (0, head))
-    return pl.pallas_call(
-        own_kernel,
-        grid=(HEADS,),
-        out_shape=(float_array(ROWS, WIDTH), float_array(ROWS, WIDTH)),
-        in_specs=[SMEM, rows, rows, rows, rows, head_tile(8, ROWS)]
-        + [whole(mask) for mask in MASKS[:2]]
-        + [halo, halo],
-        out_specs=(total, total),
+def merge_kernel(gk_ref, gv_ref, left_ref, right_ref, outk_ref, outv_ref, sumk_ref, sumv_ref):
+    terms = ((gk_ref, outk_ref, sumk_ref), (gv_ref, outv_ref, sumv_ref))
+    for part, (ref, out, sums) in enumerate(terms):
+        for half, side in enumerate((left_ref, right_ref)):
+            rows = slice(half * HW, (half + 1) * HW)
+            total = ref[rows, :] + side[part].astype(jnp.float32)
+            sums[rows, :] = total
+            out[0, rows, :] = total.astype(jnp.bfloat16)
+
+
+def merge(gk, gv, left, right):
+    total = pl.BlockSpec((ROWS, GROUP * HD), lambda step: (0, step))
+    rows = pl.BlockSpec((1, ROWS, GROUP * HD), lambda step: (0, 0, step))
+    side = pl.BlockSpec((2, HW, GROUP * HD), lambda step: (0, 0, step))
+    return pl.pallas_call(
+        merge_kernel,
+        grid=(HEADS // GROUP,),
+        out_shape=(low_array(1, ROWS, WIDTH),) * 2 + (float_array(ROWS, WIDTH),) * 2,
+        in_specs=[total, total, side, side],
+        out_specs=(rows, rows, total, total),
         compiler_params=FROM_HBM,
         cost_estimate=cost(20),
-        name="own_part",
-    )(bias, queries, cotangent, key_rows, values, final, *masks[:2], left, right)
-
-
-def finish_kernel(starts_ref, gk_ref, gv_ref, prompt_ref, outk_ref, outv_ref):
+        name="merge",
+    )(gk, gv, left, right)
+
+
+def finish_kernel(
+    starts_ref,
+    sumk_hbm,
+    sumv_hbm,
+    prompt_ref,
+    _ink,
+    _inv,
+    outk_hbm,
+    outv_hbm,
+    sums_ref,
+    rows_ref,
+    load_sems,
+    store_sems,
+):
     me = lax.axis_index("ctx")
     begins, offset = own_start(starts_ref, me)
-    offset = jnp.where(begins, offset, 2 * ROWS)
-    frame = lax.broadcasted_iota(jnp.int32, (ROWS, PMAX), 0)
-    row = lax.broadcasted_iota(jnp.int32, (ROWS, PMAX), 1)
-    place = (frame == row + offset).astype(jnp.bfloat16)
-    for member in range(GROUP):
-        cols = columns(member)
-        for part, (ref, out) in enumerate(((gk_ref, outk_ref), (gv_ref, outv_ref))):
-            piece = prompt_ref[:, member, part * BAND : (part + 1) * BAND, :].reshape(PMAX, HD)
-            out[0, :, cols] = (ref[:, cols] + nn(place, piece)).astype(jnp.bfloat16)
-
-
-def finish(starts, gk, gv, prompt):
-    total = pl.BlockSpec((ROWS, GROUP * HD), lambda step: (0, step))
-    rows = pl.BlockSpec((1, ROWS, GROUP * HD), lambda step: (0, 0, step))
-    pieces = pl.BlockSpec((BANDS, GROUP, 2 * BAND, HD), lambda step: (0, step, 0, 0))
+
+    @pl.when(begins)
+    def _():
+        base = pl.multiple_of(jnp.minimum(offset // BAND * BAND, ROWS - SPAN), BAND)
+        span = pl.ds(base, SPAN)
+        loads = [
+            pltpu.make_async_copy(ref.at[span, :], sums_ref.at[part], load_sems.at[part])
+            for part, ref in enumerate((sumk_hbm, sumv_hbm))
+        ]
+        stores = [
+            pltpu.make_async_copy(rows_ref.at[part], ref.at[0, span, :], store_sems.at[part])
+            for part, ref in enumerate((outk_hbm, outv_hbm))
+        ]
+        for copy in loads:
+            copy.start()
+        frame, row = grid_of(SPAN, PMAX)
+        place = (frame == row + (offset - base)).astype(jnp.bfloat16)
+        for part in range(2):
+            loads[part].wait()
+            for head in range(HEADS):
+                cols = columns(head)
+                piece = prompt_ref[:, head, part * BAND : (part + 1) * BAND, :].reshape(PMAX, HD)
+                total = sums_ref[part, :, cols] + nn(place, piece)
+                rows_ref[part, :, cols] = total.astype(jnp.bfloat16)
+            stores[part].start()
+        for copy in stores:
+            copy.wait()
+
+
+def finish(starts, outk, outv, sumk, sumv, prompt):
     return pl.pallas_call(
         finish_kernel,
-        grid=(HEADS // GROUP,),
         out_shape=(low_array(1, ROWS, WIDTH),) * 2,
-        in_specs=[SMEM, total, total, pieces],
-        out_specs=(rows, rows),
+        in_specs=[SMEM, HBM, HBM, VMEM, HBM, HBM],
+        out_specs=(HBM, HBM),
+        input_output_aliases={4: 0, 5: 1},
+        scratch_shapes=[
+            pltpu.VMEM((2, SPAN, WIDTH), jnp.float32),
+            pltpu.VMEM((2, SPAN, WIDTH), jnp.bfloat16),
+            pltpu.SemaphoreType.DMA((2,)),
+            pltpu.SemaphoreType.DMA((2,)),
+        ],
         compiler_params=FROM_HBM,
         name="finish",
-    )(starts, gk, gv, prompt)
+    )(starts, sumk, sumv, prompt, outk, outv)
 
 
 def exchange(pieces):
@@ -536,24 +568,23 @@
     stats, *masks = window(
         starts, lens, bias, queries, cotangent, key_rows, values, low, high
     )
-    held, stats = lax.optimization_barrier((held, stats))
     prompt = exchange(route(starts, held)).reshape(BANDS, HEADS, 2 * BAND, HD)
     gprompt, final = prompt_part(bias, queries, cotangent, prompt, stats, masks[3])
     held = exchange(gprompt.reshape(count, SENT, HD))
-    attended, grad_q = row_part(
+    attended, grad_q, gk, gv = own_part(
         bias, queries, cotangent, key_rows, values, low, high, prompt, final, masks
     )
-    final, grad_q = lax.optimization_barrier((final, grad_q))
+    final, gk = lax.optimization_barrier((final, gk))
     glow, ghigh = halo_grads(queries, cotangent, low, high, final, masks[2])
     right = shifted(glow, -1)
     left = shifted(ghigh, 1)
-    held, final, glow, ghigh = lax.optimization_barrier((held, final, glow, ghigh))
+    held, glow, ghigh = lax.optimization_barrier((held, glow, ghigh))
     owned, sums = gather(starts, held)
     returned = exchange(owned).reshape(BANDS, HEADS, 2 * BAND, HD)
-    gk, gv = own_part(bias, queries, cotangent, key_rows, values, final, masks, left, right)
-    sums, gk = lax.optimization_barrier((sums, gk))
+    outk, outv, sumk, sumv = merge(gk, gv, left, right)
+    sums, sumk = lax.optimization_barrier((sums, sumk))
     grad_bias = jnp.sum(summed(sums, "dp", 1, 2), axis=1)
-    grad_k, grad_v = finish(starts, gk, gv, returned)
+    grad_k, grad_v = finish(starts, outk, outv, sumk, sumv, returned)
     return attended, grad_q, grad_k, grad_v, grad_bias
 
 

time: 140 us -> 126 us (0.900)
  the two profiles are of different devices: /device:TPU:25 before, /device:TPU:9 now
where the time goes in v3:
time: 126 us; the launch traced here: 125 us
  starting transfers between devices  65.1 us (52%)
  Pallas kernels  36.8 us (29%)
  waiting for transfers between devices  17.7 us (14%)
  local copies, waits for them, and re-layouts  4.34 us (3%)
    all_to_all x4, starting transfers between devices, exchange(): return lax.all_to_all(pieces, 'ctx', 0, 0, tiled=True)  35.7 us
    ppermute x4, starting transfers between devices, shifted(): lax.ppermute(x, 'ctx', [(i, i + by) for i in range(peers) if 0 <= i + by...  15.4 us
    ppermute x3, starting transfers between devices, partners(): lax.ppermute(x, axis, [(i, i ^ step) for i in range(peers)])  13.9 us
    all_to_all x4, waiting for transfers between devices, exchange(): return lax.all_to_all(pieces, 'ctx', 0, 0, tiled=True)  11.3 us
    pallas_call x1, Pallas kernels, own_part(): pl.pallas_call(own_kernel, grid=(HEADS,), out_shape=(low_array(1, ROWS, W...  9.67 us
    pallas_call x1, Pallas kernels, window(): pl.pallas_call(window_kernel, grid=(HEADS,), out_shape=(float_array(HEADS...  6.27 us
    unnamed x42, local copies, waits for them, and re-layouts  4.34 us
    pallas_call x1, Pallas kernels, merge(): pl.pallas_call(merge_kernel, grid=(HEADS // GROUP,), out_shape=(low_array...  4.15 us
  transfers between devices with their start and end apart: 11, of which 6 were waited for; matrix products, arithmetic and copies ran while one was open for 1% of the time, Pallas kernels for 22%

profile of v3, /device:TPU:9, one launch (start us, length us, event | category | flops | bytes accessed | tf_op | source)
XLA Modules:
  0.0 125.4 jit_solution(8627149202761219279)
XLA Ops:
  0.6 3.4 %cut_prompt.1 = (bf16[8,8,32,128]{3,2,1,0:T(8,128)(2,1)}, bf16[2,128,1024]{2,1,0:T(8,128)(2,1)}, bf16[2,128,1024]{2,1,0:T(8,128)(2,1)}) custom-call(s32[1,64]{1,0:T(1,128)} %starts_ref.9, bf16[1,256,1024]{2,1,0:T(8,128)(2,1)} %k_ref.3, bf16[1,256,1024]{2,1,0:T(8,128)(2,1)} %v_ref.3), custom_call_target="tpu_custom_call" | custom-call | tf_op jit(solution)/shard_map/cut_prompt/pallas_call | solution.py:93
  4.1 12.6 %all-to-all-start = ((bf16[64,32,128]{2,1,0:T(8,128)(2,1)}), bf16[64,32,128]{2,1,0:T(8,128)(2,1)S(1)}, u32[]{:S(2)}, u32[]{:S(2)}) async-start(bf16[64,32,128]{2,1,0:T(8,128)(2,1)} %bitcast.7), calls=%async_computation | async-start | bytes 1048576 | tf_op jit(solution)/shard_map/all_to_all | solution.py:544
  16.7 3.1 %collective-permute-start = (bf16[2,128,1024]{2,1,0:T(8,128)(2,1)}, bf16[2,128,1024]{2,1,0:T(8,128)(2,1)}, u32[]{:S(2)}, u32[]{:S(2)}) collective-permute-start(bf16[2,128,1024]{2,1,0:T(8,128)(2,1)} %get-tuple-element.34), channel_id=1, source_target_pairs={{0,1},{1,2},{2,3},{3,4},{4,5},{5,6},{6,7},{7,8},{8,9},{9,10},{10,1... | collective-permute-start | bytes 1572872 | tf_op jit(solution)/shard_map/ppermute | solution.py:549
  19.8 5.2 %collective-permute-start.1 = (bf16[2,128,1024]{2,1,0:T(8,128)(2,1)S(1)}, bf16[2,128,1024]{2,1,0:T(8,128)(2,1)}, u32[]{:S(2)}, u32[]{:S(2)}) collective-permute-start(bf16[2,128,1024]{2,1,0:T(8,128)(2,1)S(1)} %copy-done.19), channel_id=1, source_target_pairs={{1,0},{2,1},{3,2},{4,3},{5,4},{6,5},{7,6},{8,7},{9,8},{10,9},{11,1... | collective-permute-start | bytes 1572872 | tf_op jit(solution)/shard_map/ppermute | solution.py:549
  25.1 7.6 %all-to-all-done.in_ref = bf16[64,32,128]{2,1,0:T(8,128)(2,1)S(1)} async-done(((bf16[64,32,128]{2,1,0:T(8,128)(2,1)}), bf16[64,32,128]{2,1,0:T(8,128)(2,1)S(1)}, u32[]{:S(2)}, u32[]{:S(2)}) %all-to-all-start) | async-done | bytes 524320 | tf_op jit(solution)/shard_map/all_to_all | solution.py:544
  32.7 1.5 %route.1 = bf16[64,32,128]{2,1,0:T(8,128)(2,1)} custom-call(s32[1,64]{1,0:T(1,128)S(1)} %copy-done.3, bf16[64,32,128]{2,1,0:T(8,128)(2,1)S(1)} %all-to-all-done.in_ref), custom_call_target="tpu_custom_call" | custom-call | tf_op jit(solution)/shard_map/route/pallas_call | solution.py:124
  34.2 6.7 %all-to-all-start.1 = ((bf16[64,32,128]{2,1,0:T(8,128)(2,1)}), bf16[64,32,128]{2,1,0:T(8,128)(2,1)S(1)}, u32[]{:S(2)}, u32[]{:S(2)}) async-start(bf16[64,32,128]{2,1,0:T(8,128)(2,1)} %route.1), calls=%async_computation.1 | async-start | bytes 1048576 | tf_op jit(solution)/shard_map/all_to_all | solution.py:544
  40.9 1.7 %collective-permute-done.low_ref = bf16[2,128,1024]{2,1,0:T(8,128)(2,1)} collective-permute-done((bf16[2,128,1024]{2,1,0:T(8,128)(2,1)}, bf16[2,128,1024]{2,1,0:T(8,128)(2,1)}, u32[]{:S(2)}, u32[]{:S(2)}) %collective-permute-start) | collective-permute-done | bytes 524320 | tf_op jit(solution)/shard_map/ppermute | solution.py:549
  42.6 6.3 %window.1 = (f32[8,8,256]{2,1,0:T(8,128)S(1)}, f32[256,256]{1,0:T(8,128)S(1)}, f32[256,256]{1,0:T(8,128)S(1)}, f32[2,128,128]{2,1,0:T(8,128)S(1)}, f32[128,256]{1,0:T(8,128)S(1)}) custom-call(s32[1,64]{1,0:T(1,128)S(1)} %copy-done.3, s32[1,64]{1,0:T(1,128)S(1)} %copy-done.8, f32[8]{0:T(128)S(1)} %copy-done.9, bf16[1,256,1024]{2,1,0:T(8,128)(2,1)S(1)} %copy-done.4, ...), custom_call_target="tpu_custom_call" | custom-call | flops 20000000000 | bytes 8388608 | tf_op jit(solution)/shard_map/window/pallas_call | solution.py:293
  48.9 0.6 copy-done.10
  49.5 0.7 copy-done.15
  50.2 0.7 copy-done.16
  51.0 3.7 %all-to-all-done.1 = bf16[64,32,128]{2,1,0:T(8,128)(2,1)S(1)} async-done(((bf16[64,32,128]{2,1,0:T(8,128)(2,1)}), bf16[64,32,128]{2,1,0:T(8,128)(2,1)S(1)}, u32[]{:S(2)}, u32[]{:S(2)}) %all-to-all-start.1) | async-done | bytes 524320 | tf_op jit(solution)/shard_map/all_to_all | solution.py:544
  54.6 2.6 %prompt_part.1 = (bf16[8,8,40,128]{3,2,1,0:T(8,128)(2,1)}, f32[8,8,256]{2,1,0:T(8,128)S(1)}) custom-call(f32[8]{0:T(128)S(1)} %copy-done.9, bf16[1,256,1024]{2,1,0:T(8,128)(2,1)S(1)} %copy-done.4, bf16[1,256,1024]{2,1,0:T(8,128)(2,1)S(1)} %copy-done.6, bf16[8,8,32,128]{3,2,1,0:T(8,128)(2,1)S(1)} %bitcast.4, f32[8,8,256]{2,1,0:T(8,128)S(1)} %get-tuple-element.37.stats_ref, ...), custom_call_target="tpu_custom_call" | custom-call | flops 4000000000 | bytes 8388608 | tf_op jit(solution)/shard_map/prompt_part/pallas_call | solution.py:354
  57.2 0.6 copy-done.13
  57.8 7.2 %all-to-all-start.2 = ((bf16[64,40,128]{2,1,0:T(8,128)(2,1)}), bf16[64,40,128]{2,1,0:T(8,128)(2,1)S(1)}, u32[]{:S(2)}, u32[]{:S(2)}) async-start(bf16[64,40,128]{2,1,0:T(8,128)(2,1)} %bitcast.2), calls=%async_computation.2 | async-start | bytes 1310720 | tf_op jit(solution)/shard_map/all_to_all | solution.py:544
  65.1 9.7 %own_part.1 = (bf16[1,256,1024]{2,1,0:T(8,128)(2,1)}, bf16[1,256,1024]{2,1,0:T(8,128)(2,1)}, f32[256,1024]{1,0:T(8,128)}, f32[256,1024]{1,0:T(8,128)}) custom-call(f32[8]{0:T(128)} %bias_ref.5, bf16[1,256,1024]{2,1,0:T(8,128)(2,1)} %q_ref.7, bf16[1,256,1024]{2,1,0:T(8,128)(2,1)} %d_ref.7, bf16[1,256,1024]{2,1,0:T(8,128)(2,1)} %k_ref.3, ...), custom_call_target="tpu_custom_call" | custom-call | flops 10000000000 | bytes 8388608 | tf_op jit(solution)/shard_map/own_part/pallas_call | solution.py:436
  74.8 4.1 %halo_grads.1 = (bf16[2,128,1024]{2,1,0:T(8,128)(2,1)S(1)}, bf16[2,128,1024]{2,1,0:T(8,128)(2,1)S(1)}) custom-call(bf16[1,256,1024]{2,1,0:T(8,128)(2,1)S(1)} %copy-done.5, bf16[1,256,1024]{2,1,0:T(8,128)(2,1)S(1)} %copy-done.7, bf16[2,128,1024]{2,1,0:T(8,128)(2,1)} %collective-permute-done.low_ref, bf16[2,128,1024]{2,1,0:T(8,128)(2,1)} %collective-permute-done.1.high_ref, ...), custom_call_target="tpu_custom_call" | custom-call | flops 4000000000 | bytes 8388608 | tf_op jit(solution)/shard_map/halo_grads/pallas_call | solution.py:385
  79.0 5.2 %collective-permute-start.3 = (bf16[2,128,1024]{2,1,0:T(8,128)(2,1)S(1)}, bf16[2,128,1024]{2,1,0:T(8,128)(2,1)S(1)}, u32[]{:S(2)}, u32[]{:S(2)}) collective-permute-start(bf16[2,128,1024]{2,1,0:T(8,128)(2,1)S(1)} %get-tuple-element.48), channel_id=1, source_target_pairs={{1,0},{2,1},{3,2},{4,3},{5,4},{6,5},{7,6},{8,7},{9,8},{10,9},{11,1... | collective-permute-start | bytes 1572872 | tf_op jit(solution)/shard_map/ppermute | solution.py:549
  84.2 1.9 %collective-permute-start.2 = (bf16[2,128,1024]{2,1,0:T(8,128)(2,1)S(1)}, bf16[2,128,1024]{2,1,0:T(8,128)(2,1)S(1)}, u32[]{:S(2)}, u32[]{:S(2)}) collective-permute-start(bf16[2,128,1024]{2,1,0:T(8,128)(2,1)S(1)} %get-tuple-element.49), channel_id=1, source_target_pairs={{0,1},{1,2},{2,3},{3,4},{4,5},{5,6},{6,7},{7,8},{8,9},{9,10},{10,1... | collective-permute-start | bytes 1572872 | tf_op jit(solution)/shard_map/ppermute | solution.py:549
  86.1 1.6 %gather.1 = (bf16[64,32,128]{2,1,0:T(8,128)(2,1)}, f32[8,128]{1,0:T(8,128)S(1)}) custom-call(s32[1,64]{1,0:T(1,128)S(1)} %copy-done.3, bf16[64,40,128]{2,1,0:T(8,128)(2,1)S(1)} %all-to-all-done.2.in_ref), custom_call_target="tpu_custom_call" | custom-call | tf_op jit(solution)/shard_map/gather/pallas_call | solution.py:153
  87.7 9.2 %all-to-all-start.3 = ((bf16[64,32,128]{2,1,0:T(8,128)(2,1)}), bf16[64,32,128]{2,1,0:T(8,128)(2,1)S(1)}, u32[]{:S(2)}, u32[]{:S(2)}) async-start(bf16[64,32,128]{2,1,0:T(8,128)(2,1)} %get-tuple-element.57), calls=%async_computation.3 | async-start | bytes 1048576 | tf_op jit(solution)/shard_map/all_to_all | solution.py:544
  96.9 1.3 collective-permute-done.2.left_ref
  98.2 0.8 copy-done.20
  99.0 4.1 %merge.1 = (bf16[1,256,1024]{2,1,0:T(8,128)(2,1)}, bf16[1,256,1024]{2,1,0:T(8,128)(2,1)}, f32[256,1024]{1,0:T(8,128)}, f32[256,1024]{1,0:T(8,128)}) custom-call(f32[256,1024]{1,0:T(8,128)} %get-tuple-element.52.gk_ref, f32[256,1024]{1,0:T(8,128)} %get-tuple-element.53.gv_ref, bf16[2,128,1024]{2,1,0:T(8,128)(2,1)} %copy-done.20, bf16[2,128,1024]{2,1,0:T(8,128)(2,1)} %copy-done.18), custom_call_target="tpu_custom_call" | custom-call | flops 20000000000 | bytes 8388608 | tf_op jit(solution)/shard_map/merge/pallas_call | solution.py:468
  103.1 13.4 %collective-permute-start.6 = (f32[8,128]{1,0:T(8,128)S(1)}, f32[8,128]{1,0:T(8,128)S(1)}, u32[]{:S(2)}, u32[]{:S(2)}) collective-permute-start(f32[8,128]{1,0:T(8,128)S(1)} %get-tuple-element.62), channel_id=1, source_target_pairs={{0,192},{64,128},{128,64},{192,0},{1,193},{65,129},{129,65},{193,1... | collective-permute-start | bytes 12296 | tf_op jit(solution)/shard_map/ppermute | solution.py:554
  116.5 0.5 collective-permute-start.5
  117.1 0.8 collective-permute-done.6
  117.8 2.7 %collective-permute-done.5 = f32[8,128]{1,0:T(8,128)S(1)} collective-permute-done((f32[8,128]{1,0:T(8,128)S(1)}, f32[8,128]{1,0:T(8,128)S(1)}, u32[]{:S(2)}, u32[]{:S(2)}) %collective-permute-start.5) | collective-permute-done | bytes 4128 | tf_op jit(solution)/shard_map/ppermute | solution.py:554
  120.5 0.6 add_reduce_fusion
  121.1 0.8 copy-done.17
  121.9 3.5 %finish.1 = (bf16[1,256,1024]{2,1,0:T(8,128)(2,1)}, bf16[1,256,1024]{2,1,0:T(8,128)(2,1)}) custom-call(s32[1,64]{1,0:T(1,128)} %starts_ref.9, f32[256,1024]{1,0:T(8,128)} %get-tuple-element.55.sumk_hbm, f32[256,1024]{1,0:T(8,128)} %get-tuple-element.56.sumv_hbm, bf16[8,8,32,128]{3,2,1,0:T(8,128)(2,1)} %bitcast.6, ...), custom_call_target="tpu_custom_call", output_to_operand_aliasing={{0}: (4, {}), {1}: (5, {})} | custom-call | tf_op jit(solution)/shard_map/finish/pallas_call | solution.py:526
  (42 shorter events, 0.1 us)
Async XLA Ops:
  4.1 15.8 %copy-start.19 = (bf16[2,128,1024]{2,1,0:T(8,128)(2,1)S(1)}, bf16[2,128,1024]{2,1,0:T(8,128)(2,1)}, u32[]{:S(2)}) copy-start(bf16[2,128,1024]{2,1,0:T(8,128)(2,1)} %get-tuple-element.35) | copy-start | bytes 1572868
  4.1 38.5 %copy-start.9 = (f32[8]{0:T(128)S(1)}, f32[8]{0:T(128)}, u32[]{:S(2)}) copy-start(f32[8]{0:T(128)} %bias_ref.5) | copy-start | bytes 100
  4.1 28.6 %all-to-all-start = ((bf16[64,32,128]{2,1,0:T(8,128)(2,1)}), bf16[64,32,128]{2,1,0:T(8,128)(2,1)S(1)}, u32[]{:S(2)}, u32[]{:S(2)}) async-start(bf16[64,32,128]{2,1,0:T(8,128)(2,1)} %bitcast.7), calls=%async_computation | async-start | bytes 1048576 | tf_op jit(solution)/shard_map/all_to_all | solution.py:544
  16.7 16.0 %copy-start.3 = (s32[1,64]{1,0:T(1,128)S(1)}, s32[1,64]{1,0:T(1,128)}, u32[]{:S(2)}) copy-start(s32[1,64]{1,0:T(1,128)} %starts_ref.9) | copy-start | bytes 772
  16.7 25.8 %collective-permute-start = (bf16[2,128,1024]{2,1,0:T(8,128)(2,1)}, bf16[2,128,1024]{2,1,0:T(8,128)(2,1)}, u32[]{:S(2)}, u32[]{:S(2)}) collective-permute-start(bf16[2,128,1024]{2,1,0:T(8,128)(2,1)} %get-tuple-element.34), channel_id=1, source_target_pairs={{0,1},{1,2},{2,3},{3,4},{4,5},{5,6},{6,7},{7,8},{8,9},{9,10},{10,1... | collective-permute-start | bytes 1572872 | tf_op jit(solution)/shard_map/ppermute | solution.py:549
  19.8 22.7 %collective-permute-start.1 = (bf16[2,128,1024]{2,1,0:T(8,128)(2,1)S(1)}, bf16[2,128,1024]{2,1,0:T(8,128)(2,1)}, u32[]{:S(2)}, u32[]{:S(2)}) collective-permute-start(bf16[2,128,1024]{2,1,0:T(8,128)(2,1)S(1)} %copy-done.19), channel_id=1, source_target_pairs={{1,0},{2,1},{3,2},{4,3},{5,4},{6,5},{7,6},{8,7},{9,8},{10,9},{11,1... | collective-permute-start | bytes 1572872 | tf_op jit(solution)/shard_map/ppermute | solution.py:549
  32.7 9.9 %copy-start.4 = (bf16[1,256,1024]{2,1,0:T(8,128)(2,1)S(1)}, bf16[1,256,1024]{2,1,0:T(8,128)(2,1)}, u32[]{:S(2)}) copy-start(bf16[1,256,1024]{2,1,0:T(8,128)(2,1)} %q_ref.7) | copy-start | bytes 1572868
  32.7 9.9 %copy-start.6 = (bf16[1,256,1024]{2,1,0:T(8,128)(2,1)S(1)}, bf16[1,256,1024]{2,1,0:T(8,128)(2,1)}, u32[]{:S(2)}) copy-start(bf16[1,256,1024]{2,1,0:T(8,128)(2,1)} %d_ref.7) | copy-start | bytes 1572868
  32.7 9.9 %copy-start.8 = (s32[1,64]{1,0:T(1,128)S(1)}, s32[1,64]{1,0:T(1,128)}, u32[]{:S(2)}) copy-start(s32[1,64]{1,0:T(1,128)} %lens_ref.1) | copy-start | bytes 772
  34.2 8.4 %copy-start.1 = (bf16[1,256,1024]{2,1,0:T(8,128)(2,1)S(1)}, bf16[1,256,1024]{2,1,0:T(8,128)(2,1)}, u32[]{:S(2)}) copy-start(bf16[1,256,1024]{2,1,0:T(8,128)(2,1)} %k_ref.3) | copy-start | bytes 1572868
  34.2 8.4 %copy-start.2 = (bf16[1,256,1024]{2,1,0:T(8,128)(2,1)S(1)}, bf16[1,256,1024]{2,1,0:T(8,128)(2,1)}, u32[]{:S(2)}) copy-start(bf16[1,256,1024]{2,1,0:T(8,128)(2,1)} %v_ref.3) | copy-start | bytes 1572868
  34.2 20.4 %all-to-all-start.1 = ((bf16[64,32,128]{2,1,0:T(8,128)(2,1)}), bf16[64,32,128]{2,1,0:T(8,128)(2,1)S(1)}, u32[]{:S(2)}, u32[]{:S(2)}) async-start(bf16[64,32,128]{2,1,0:T(8,128)(2,1)} %route.1), calls=%async_computation.1 | async-start | bytes 1048576 | tf_op jit(solution)/shard_map/all_to_all | solution.py:544
  48.9 0.7 copy-start.10
  49.5 0.7 copy-start.15
  50.2 0.7 copy-start.16
  51.0 6.3 %copy-start.12 = (f32[128,256]{1,0:T(8,128)}, f32[128,256]{1,0:T(8,128)S(1)}, u32[]{:S(2)}) copy-start(f32[128,256]{1,0:T(8,128)S(1)} %get-tuple-element.38.mask_ref.prompt_mask) | copy-start | bytes 393220
  54.6 2.6 %copy-start = (bf16[64,32,128]{2,1,0:T(8,128)(2,1)}, bf16[64,32,128]{2,1,0:T(8,128)(2,1)S(1)}, u32[]{:S(2)}) copy-start(bf16[64,32,128]{2,1,0:T(8,128)(2,1)S(1)} %all-to-all-done.1) | copy-start | bytes 1572868
  57.2 0.6 copy-start.13
  57.8 28.2 %all-to-all-start.2 = ((bf16[64,40,128]{2,1,0:T(8,128)(2,1)}), bf16[64,40,128]{2,1,0:T(8,128)(2,1)S(1)}, u32[]{:S(2)}, u32[]{:S(2)}) async-start(bf16[64,40,128]{2,1,0:T(8,128)(2,1)} %bitcast.2), calls=%async_computation.2 | async-start | bytes 1310720 | tf_op jit(solution)/shard_map/all_to_all | solution.py:544
  65.1 9.7 %copy-start.5 = (bf16[1,256,1024]{2,1,0:T(8,128)(2,1)S(1)}, bf16[1,256,1024]{2,1,0:T(8,128)(2,1)}, u32[]{:S(2)}) copy-start(bf16[1,256,1024]{2,1,0:T(8,128)(2,1)} %q_ref.7) | copy-start | bytes 1572868
  65.1 9.7 %copy-start.7 = (bf16[1,256,1024]{2,1,0:T(8,128)(2,1)S(1)}, bf16[1,256,1024]{2,1,0:T(8,128)(2,1)}, u32[]{:S(2)}) copy-start(bf16[1,256,1024]{2,1,0:T(8,128)(2,1)} %d_ref.7) | copy-start | bytes 1572868
  65.1 9.7 %copy-start.11 = (f32[2,128,128]{2,1,0:T(8,128)S(1)}, f32[2,128,128]{2,1,0:T(8,128)}, u32[]{:S(2)}) copy-start(f32[2,128,128]{2,1,0:T(8,128)} %copy-done.10) | copy-start | bytes 393220
  65.1 9.7 %copy-start.14 = (f32[8,8,256]{2,1,0:T(8,128)S(1)}, f32[8,8,256]{2,1,0:T(8,128)}, u32[]{:S(2)}) copy-start(f32[8,8,256]{2,1,0:T(8,128)} %copy-done.13) | copy-start | bytes 196612
  79.0 17.9 %collective-permute-start.3 = (bf16[2,128,1024]{2,1,0:T(8,128)(2,1)S(1)}, bf16[2,128,1024]{2,1,0:T(8,128)(2,1)S(1)}, u32[]{:S(2)}, u32[]{:S(2)}) collective-permute-start(bf16[2,128,1024]{2,1,0:T(8,128)(2,1)S(1)} %get-tuple-element.48), channel_id=1, source_target_pairs={{1,0},{2,1},{3,2},{4,3},{5,4},{6,5},{7,6},{8,7},{9,8},{10,9},{11,1... | collective-permute-start | bytes 1572872 | tf_op jit(solution)/shard_map/ppermute | solution.py:549
  84.2 14.0 %collective-permute-start.2 = (bf16[2,128,1024]{2,1,0:T(8,128)(2,1)S(1)}, bf16[2,128,1024]{2,1,0:T(8,128)(2,1)S(1)}, u32[]{:S(2)}, u32[]{:S(2)}) collective-permute-start(bf16[2,128,1024]{2,1,0:T(8,128)(2,1)S(1)} %get-tuple-element.49), channel_id=1, source_target_pairs={{0,1},{1,2},{2,3},{3,4},{4,5},{5,6},{6,7},{7,8},{8,9},{9,10},{10,1... | collective-permute-start | bytes 1572872 | tf_op jit(solution)/shard_map/ppermute | solution.py:549
  87.7 33.4 %all-to-all-start.3 = ((bf16[64,32,128]{2,1,0:T(8,128)(2,1)}), bf16[64,32,128]{2,1,0:T(8,128)(2,1)S(1)}, u32[]{:S(2)}, u32[]{:S(2)}) async-start(bf16[64,32,128]{2,1,0:T(8,128)(2,1)} %get-tuple-element.57), calls=%async_computation.3 | async-start | bytes 1048576 | tf_op jit(solution)/shard_map/all_to_all | solution.py:544
  96.9 1.3 %copy-start.18 = (bf16[2,128,1024]{2,1,0:T(8,128)(2,1)}, bf16[2,128,1024]{2,1,0:T(8,128)(2,1)S(1)}, u32[]{:S(2)}) copy-start(bf16[2,128,1024]{2,1,0:T(8,128)(2,1)S(1)} %collective-permute-done.3.right_ref) | copy-start | bytes 1572868
  98.2 0.8 copy-start.20
  103.1 14.7 %collective-permute-start.6 = (f32[8,128]{1,0:T(8,128)S(1)}, f32[8,128]{1,0:T(8,128)S(1)}, u32[]{:S(2)}, u32[]{:S(2)}) collective-permute-start(f32[8,128]{1,0:T(8,128)S(1)} %get-tuple-element.62), channel_id=1, source_target_pairs={{0,192},{64,128},{128,64},{192,0},{1,193},{65,129},{129,65},{193,1... | collective-permute-start | bytes 12296 | tf_op jit(solution)/shard_map/ppermute | solution.py:554
  116.5 4.0 %collective-permute-start.5 = (f32[8,128]{1,0:T(8,128)S(1)}, f32[8,128]{1,0:T(8,128)S(1)}, u32[]{:S(2)}, u32[]{:S(2)}) collective-permute-start(f32[8,128]{1,0:T(8,128)S(1)} %get-tuple-element.62), channel_id=1, source_target_pairs={{0,128},{64,192},{128,0},{192,64},{1,129},{65,193},{129,1},{193,65... | collective-permute-start | bytes 12296 | tf_op jit(solution)/shard_map/ppermute | solution.py:554
  117.1 3.5 %collective-permute-start.4 = (f32[8,128]{1,0:T(8,128)S(1)}, f32[8,128]{1,0:T(8,128)S(1)}, u32[]{:S(2)}, u32[]{:S(2)}) collective-permute-start(f32[8,128]{1,0:T(8,128)S(1)} %get-tuple-element.62), channel_id=1, source_target_pairs={{0,64},{64,0},{128,192},{192,128},{1,65},{65,1},{129,193},{193,129... | collective-permute-start | bytes 12296 | tf_op jit(solution)/shard_map/ppermute | solution.py:554
  121.1 0.8 copy-start.17

commit v4 on v3

--- a/solution.py
+++ b/solution.py
@@ -19,6 +19,7 @@
 SPAN = PMAX + BAND
 GROUP = 2
 STAGED = 4
+MERGE = 8
 NEG = -1e30
 LOG2E = math.log2(math.e)
 SCALE = 1.0 / math.sqrt(HD)
@@ -29,6 +30,7 @@
 HBM = pl.BlockSpec(memory_space=pltpu.HBM)
 PARAMS = pltpu.CompilerParams(vmem_limit_bytes=20 * 1024 * 1024)
 FROM_HBM = pltpu.CompilerParams(vmem_limit_bytes=60 * 1024 * 1024)
+NEARLY = pltpu.CompilerParams(vmem_limit_bytes=58 * 1024 * 1024)
 
 
 def nt(a, b):
@@ -60,31 +62,53 @@
     return jax.ShapeDtypeStruct(shape, jnp.bfloat16)
 
 
-def cut_kernel(starts_ref, k_hbm, v_hbm, out_ref, last_hbm, first_hbm, k_ref, v_ref, sems, out_sems):
+def cut_kernel(
+    starts_ref,
+    k_hbm,
+    v_hbm,
+    out_hbm,
+    last_hbm,
+    first_hbm,
+    k_ref,
+    v_ref,
+    out_ref,
+    sems,
+    edge_sems,
+    out_sems,
+):
     me = lax.axis_index("ctx")
     offset = own_start(starts_ref, me)[1]
-    halves = (slice(0, HW), slice(HW, ROWS))
-    loads, stores = [], []
-    for part, (source, ref) in enumerate(((k_hbm, k_ref), (v_hbm, v_ref))):
-        for half, (rows, target) in enumerate(zip(halves, (first_hbm, last_hbm))):
-            loads.append(
-                pltpu.make_async_copy(source.at[0, rows, :], ref.at[rows, :], sems.at[part, half])
-            )
-            stores.append(
-                pltpu.make_async_copy(ref.at[rows, :], target.at[part], out_sems.at[part, half])
-            )
+    sources = (k_hbm, v_hbm)
+    scratch = (k_ref, v_ref)
+    loads = [
+        pltpu.make_async_copy(source.at[0], ref, sems.at[part])
+        for part, (source, ref) in enumerate(zip(sources, scratch))
+    ]
+    stores = [
+        pltpu.make_async_copy(ref.at[rows, :], target.at[part], edge_sems.at[part, half])
+        for part, ref in enumerate(scratch)
+        for half, (rows, target) in enumerate(
+            ((slice(0, HW), first_hbm), (slice(HW, ROWS), last_hbm))
+        )
+    ]
     for copy in loads:
         copy.start()
     row = lax.broadcasted_iota(jnp.int32, (PMAX, ROWS), 0)
     frame = lax.broadcasted_iota(jnp.int32, (PMAX, ROWS), 1)
     pick = (frame == row + offset).astype(jnp.bfloat16)
-    for load, store in zip(loads, stores):
-        load.wait()
+    for part, ref in enumerate(scratch):
+        loads[part].wait()
+        stores[2 * part].start()
+        stores[2 * part + 1].start()
+        here = pl.ds(part * BAND, BAND)
+        for head in range(HEADS):
+            rows = nn(pick, ref[:, columns(head)]).astype(jnp.bfloat16)
+            out_ref[:, head, here, :] = rows.reshape(BANDS, BAND, HD)
+        store = pltpu.make_async_copy(
+            out_ref.at[:, :, here, :], out_hbm.at[:, :, here, :], out_sems.at[part]
+        )
         store.start()
-    for head in range(HEADS):
-        for part, ref in enumerate((k_ref, v_ref)):
-            rows = nn(pick, ref[:, columns(head)]).astype(jnp.bfloat16)
-            out_ref[:, head, part * BAND : (part + 1) * BAND, :] = rows.reshape(BANDS, BAND, HD)
+        stores.append(store)
     for store in stores:
         store.wait()
 
@@ -98,12 +122,14 @@
             low_array(2, HW, WIDTH),
         ),
         in_specs=[SMEM, HBM, HBM],
-        out_specs=(VMEM, HBM, HBM),
+        out_specs=(HBM, HBM, HBM),
         scratch_shapes=[
             pltpu.VMEM((ROWS, WIDTH), jnp.bfloat16),
             pltpu.VMEM((ROWS, WIDTH), jnp.bfloat16),
+            pltpu.VMEM((BANDS, HEADS, 2 * BAND, HD), jnp.bfloat16),
+            pltpu.SemaphoreType.DMA((2,)),
             pltpu.SemaphoreType.DMA((2, 2)),
-            pltpu.SemaphoreType.DMA((2, 2)),
+            pltpu.SemaphoreType.DMA((2,)),
         ],
         compiler_params=FROM_HBM,
         name="cut_prompt",
@@ -303,20 +329,22 @@
 
 
 def prompt_kernel(
-    bias_ref, q_ref, d_ref, prompt_ref, stats_ref, mask_ref, grad_ref, final_ref
+    bias_ref, q_ref, d_ref, prompt_ref, stats_ref, mask_ref, grad_hbm, final_hbm, grad_ref, final_ref, sems
 ):
     mask = mask_ref[...]
-    all_sums = []
+    rows = [(q_ref[0, :, columns(head)], d_ref[0, :, columns(head)]) for head in range(HEADS)]
+    all_sums, terms, stores = [], [], []
     for first in range(0, HEADS, STAGED):
         heads = range(first, first + STAGED)
-        rows = [(q_ref[0, :, columns(head)], d_ref[0, :, columns(head)]) for head in heads]
-        products = []
-        for head, (q, d) in zip(heads, rows):
-            kp = prompt_ref[:, head, :BAND, :].reshape(PMAX, HD)
-            vp = prompt_ref[:, head, BAND:, :].reshape(PMAX, HD)
-            products.append((nt(kp, q), nt(vp, d)))
-        settled_rows = []
-        for head, (scores, dprobs) in zip(heads, products):
+        raw = [
+            products(
+                prompt_ref[:, head, :BAND, :].reshape(PMAX, HD),
+                prompt_ref[:, head, BAND:, :].reshape(PMAX, HD),
+                *rows[head],
+            )
+            for head in heads
+        ]
+        for head, (scores, dprobs) in zip(heads, raw):
             x = scores * FACTOR + (mask + bias_ref[head] * LOG2E)
             stats = stats_ref[head]
             top = jnp.maximum(stats[0:1], top_of(x))
@@ -326,28 +354,37 @@
             delta = (stats[2:3] * rescale + sum_of(raised * dprobs)) * inverse
             probs = raised * inverse
             dscores = (probs * SCALE) * (dprobs - delta)
-            settled_rows.append((probs.astype(jnp.bfloat16), dscores.astype(jnp.bfloat16)))
+            terms.append((probs.astype(jnp.bfloat16), dscores.astype(jnp.bfloat16)))
             final_ref[head] = jnp.concatenate(
                 [top, inverse, delta, jnp.zeros((5, ROWS), jnp.float32)], axis=0
             )
             sums = stats[3:4] + sum_of(dscores) * (1.0 / SCALE)
             all_sums.append(sums[:, :HW] + sums[:, HW:])
-        grads = [
-            (nn(low_ds, q).astype(jnp.bfloat16), nn(low_probs, d).astype(jnp.bfloat16))
-            for (q, d), (low_probs, low_ds) in zip(rows, settled_rows)
-        ]
-        for head, (gk, gv) in zip(heads, grads):
-            grad_ref[:, head, :BAND, :] = gk.reshape(BANDS, BAND, HD)
-            grad_ref[:, head, BAND : 2 * BAND, :] = gv.reshape(BANDS, BAND, HD)
-
+
+    stores.append(pltpu.make_async_copy(final_ref, final_hbm, sems.at[HEADS // STAGED]))
+    stores[0].start()
     sums = jnp.concatenate(all_sums, axis=0)
     sums = sums + pltpu.roll(sums, HW // 2, 1)
     upper = sums.astype(jnp.bfloat16).astype(jnp.float32)
     lane = lax.broadcasted_iota(jnp.int32, (HEADS, HW), 1)
     tile = jnp.where(lane < HW // 2, upper, sums - upper).astype(jnp.bfloat16)
-    for band in range(BANDS):
-        for head in range(HEADS):
-            grad_ref[band, head, 2 * BAND :, :] = tile
+    for first in range(0, HEADS, STAGED):
+        for head in range(first, first + STAGED):
+            (q, d), (low_probs, low_ds) = rows[head], terms[head]
+            gk = nn(low_ds, q).astype(jnp.bfloat16)
+            gv = nn(low_probs, d).astype(jnp.bfloat16)
+            grad_ref[:, head, :BAND, :] = gk.reshape(BANDS, BAND, HD)
+            grad_ref[:, head, BAND : 2 * BAND, :] = gv.reshape(BANDS, BAND, HD)
+            for band in range(BANDS):
+                grad_ref[band, head, 2 * BAND :, :] = tile
+        here = pl.ds(first, STAGED)
+        store = pltpu.make_async_copy(
+            grad_ref.at[:, here], grad_hbm.at[:, here], sems.at[first // STAGED]
+        )
+        store.start()
+        stores.append(store)
+    for store in stores:
+        store.wait()
 
 
 def prompt_part(bias, queries, cotangent, prompt, stats, prompt_mask):
@@ -355,30 +392,52 @@
         prompt_kernel,
         out_shape=(low_array(BANDS, HEADS, SENT, HD), float_array(HEADS, 8, ROWS)),
         in_specs=[SMEM, VMEM, VMEM, VMEM, VMEM, VMEM],
-        out_specs=(VMEM,) * 2,
+        out_specs=(HBM, HBM),
+        scratch_shapes=[
+            pltpu.VMEM((BANDS, HEADS, SENT, HD), jnp.bfloat16),
+            pltpu.VMEM((HEADS, 8, ROWS), jnp.float32),
+            pltpu.SemaphoreType.DMA((HEADS // STAGED + 1,)),
+        ],
         compiler_params=PARAMS,
         cost_estimate=cost(4),
         name="prompt_part",
     )(bias, queries, cotangent, prompt, stats, prompt_mask)
 
 
-def settled(keys, values, q, d, added, final):
-    x = nt(keys, q) * FACTOR + added
-    probs = jnp.exp2(x - final[0:1]) * final[1:2]
-    dscores = (probs * SCALE) * (nt(values, d) - final[2:3])
+def products(keys, values, q, d):
+    return nt(keys, q), nt(values, d)
+
+
+def settled(scores, dprobs, added, final):
+    probs = jnp.exp2(scores * FACTOR + (added - final[0:1])) * final[1:2]
+    dscores = (probs * SCALE) * (dprobs - final[2:3])
     return probs.astype(jnp.bfloat16), dscores.astype(jnp.bfloat16)
 
 
 def halo_kernel(q_ref, d_ref, low_ref, high_ref, final_ref, mask_ref, glow_ref, ghigh_ref):
-    for head in range(HEADS):
-        cols = columns(head)
-        for half, (ref, out) in enumerate(((low_ref, glow_ref), (high_ref, ghigh_ref))):
-            part = slice(half * HW, (half + 1) * HW)
-            q, d = q_ref[0, part, cols], d_ref[0, part, cols]
-            final = final_ref[head, :, part]
-            probs, ds = settled(ref[0, :, cols], ref[1, :, cols], q, d, mask_ref[half], final)
-            out[0, :, cols] = nn(ds, q).astype(jnp.bfloat16)
-            out[1, :, cols] = nn(probs, d).astype(jnp.bfloat16)
+    sides = ((low_ref, glow_ref), (high_ref, ghigh_ref))
+    for first in range(0, HEADS, STAGED):
+        places = [
+            (half, slice(half * HW, (half + 1) * HW), head)
+            for head in range(first, first + STAGED)
+            for half in range(2)
+        ]
+        rows = [
+            (q_ref[0, part, columns(head)], d_ref[0, part, columns(head)])
+            for _, part, head in places
+        ]
+        raw = [
+            products(sides[half][0][0, :, columns(head)], sides[half][0][1, :, columns(head)], q, d)
+            for (half, _, head), (q, d) in zip(places, rows)
+        ]
+        terms = [
+            settled(*pair, mask_ref[half], final_ref[head, :, part])
+            for (half, part, head), pair in zip(places, raw)
+        ]
+        for (half, _, head), (q, d), (probs, ds) in zip(places, rows, terms):
+            out = sides[half][1]
+            out[0, :, columns(head)] = nn(ds, q).astype(jnp.bfloat16)
+            out[1, :, columns(head)] = nn(probs, d).astype(jnp.bfloat16)
 
 
 def halo_grads(queries, cotangent, low, high, final, halo_mask):
@@ -412,40 +471,70 @@
     gk_ref,
     gv_ref,
 ):
-    bias = bias_ref[pl.program_id(0)] * LOG2E
-    q, d, k, v = q_ref[0], d_ref[0], k_ref[0], v_ref[0]
-    kp = prompt_ref[:, 0, :BAND, :].reshape(PMAX, HD)
-    vp = prompt_ref[:, 0, BAND:, :].reshape(PMAX, HD)
-    final = final_ref[0]
-    probs, ds = settled(k, v, q, d, own_mask[...] + own_flag[...] * bias, final)
-    prompt_probs, prompt_ds = settled(kp, vp, q, d, prompt_mask[...] + bias, final)
-    gk_ref[...] = nn(ds, q)
-    gv_ref[...] = nn(probs, d)
-    attended = tn(probs, v) + tn(prompt_probs, vp)
-    grad_q = tn(ds, k) + tn(prompt_ds, kp)
-    for half, ref in enumerate((low_ref, high_ref)):
-        part = slice(half * HW, (half + 1) * HW)
-        probs, ds = settled(ref[0], ref[1], q[part], d[part], halo_mask[half], final[:, part])
-        attended_ref[0, part, :] = (attended[part] + tn(probs, ref[1])).astype(jnp.bfloat16)
-        gq_ref[0, part, :] = (grad_q[part] + tn(ds, ref[0])).astype(jnp.bfloat16)
+    members = range(GROUP)
+    step = pl.program_id(0)
+    blocks = []
+    for member in members:
+        cols = columns(member)
+        q, d = q_ref[0, :, cols], d_ref[0, :, cols]
+        kp = prompt_ref[:, member, :BAND, :].reshape(PMAX, HD)
+        vp = prompt_ref[:, member, BAND:, :].reshape(PMAX, HD)
+        blocks.append(
+            (
+                (k_ref[0, :, cols], v_ref[0, :, cols], q, d),
+                (kp, vp, q, d),
+                (low_ref[0, :, cols], low_ref[1, :, cols], q[:HW], d[:HW]),
+                (high_ref[0, :, cols], high_ref[1, :, cols], q[HW:], d[HW:]),
+            )
+        )
+    raw = [[products(*block) for block in parts] for parts in blocks]
+    terms = []
+    for member in members:
+        bias = bias_ref[step * GROUP + member] * LOG2E
+        final = final_ref[member]
+        added = (
+            own_mask[...] + own_flag[...] * bias,
+            prompt_mask[...] + bias,
+            halo_mask[0],
+            halo_mask[1],
+        )
+        finals = (final, final, final[:, :HW], final[:, HW:])
+        terms.append(
+            [settled(*pair, x, y) for pair, x, y in zip(raw[member], added, finals)]
+        )
+    for member in members:
+        cols = columns(member)
+        own, prompt, low, high = blocks[member]
+        (probs, ds), (probs_p, ds_p), (probs_l, ds_l), (probs_h, ds_h) = terms[member]
+        gk_ref[:, cols] = nn(ds, own[2])
+        gv_ref[:, cols] = nn(probs, own[3])
+        attended = tn(probs, own[1]) + tn(probs_p, prompt[1])
+        attended += jnp.concatenate([tn(probs_l, low[1]), tn(probs_h, high[1])], axis=0)
+        attended_ref[0, :, cols] = attended.astype(jnp.bfloat16)
+        grad_q = tn(ds, own[0]) + tn(ds_p, prompt[0])
+        grad_q += jnp.concatenate([tn(ds_l, low[0]), tn(ds_h, high[0])], axis=0)
+        gq_ref[0, :, cols] = grad_q.astype(jnp.bfloat16)
 
 
 def own_part(bias, queries, cotangent, key_rows, values, low, high, prompt, final, masks):
-    rows, halo = head_rows(), head_halo()
-    total = pl.BlockSpec((ROWS, HD), lambda head: (0, head))
+    rows = pl.BlockSpec((1, ROWS, GROUP * HD), lambda step: (0, 0, step))
+    halo = pl.BlockSpec((2, HW, GROUP * HD), lambda step: (0, 0, step))
+    pieces = pl.BlockSpec((BANDS, GROUP, 2 * BAND, HD), lambda step: (0, step, 0, 0))
+    tile = pl.BlockSpec((GROUP, 8, ROWS), lambda step: (step, 0, 0))
+    total = pl.BlockSpec((ROWS, GROUP * HD), lambda step: (0, step))
     return pl.pallas_call(
         own_kernel,
-        grid=(HEADS,),
+        grid=(HEADS // GROUP,),
         out_shape=(
             low_array(1, ROWS, WIDTH),
             low_array(1, ROWS, WIDTH),
             float_array(ROWS, WIDTH),
             float_array(ROWS, WIDTH),
         ),
-        in_specs=[SMEM, rows, rows, rows, rows, halo, halo, head_pieces(), head_tile(8, ROWS)]
+        in_specs=[SMEM, rows, rows, rows, rows, halo, halo, pieces, tile]
         + [whole(mask) for mask in MASKS],
         out_specs=(rows, rows, total, total),
-        compiler_params=FROM_HBM,
+        compiler_params=NEARLY,
         cost_estimate=cost(10),
         name="own_part",
     )(bias, queries, cotangent, key_rows, values, low, high, prompt, final, *masks)
@@ -472,7 +561,7 @@
         in_specs=[total, total, side, side],
         out_specs=(rows, rows, total, total),
         compiler_params=FROM_HBM,
-        cost_estimate=cost(20),
+        cost_estimate=cost(MERGE),
         name="merge",
     )(gk, gv, left, right)
 
@@ -535,7 +624,7 @@
             pltpu.SemaphoreType.DMA((2,)),
             pltpu.SemaphoreType.DMA((2,)),
         ],
-        compiler_params=FROM_HBM,
+        compiler_params=NEARLY,
         name="finish",
     )(starts, sumk, sumv, prompt, outk, outv)
 
@@ -581,9 +670,9 @@
     held, glow, ghigh = lax.optimization_barrier((held, glow, ghigh))
     owned, sums = gather(starts, held)
     returned = exchange(owned).reshape(BANDS, HEADS, 2 * BAND, HD)
+    grad_bias = jnp.sum(summed(sums, "dp", 1, 2), axis=1)
+    gk, grad_bias = lax.optimization_barrier((gk, grad_bias))
     outk, outv, sumk, sumv = merge(gk, gv, left, right)
-    sums, sumk = lax.optimization_barrier((sums, sumk))
-    grad_bias = jnp.sum(summed(sums, "dp", 1, 2), axis=1)
     grad_k, grad_v = finish(starts, outk, outv, sumk, sumv, returned)
     return attended, grad_q, grad_k, grad_v, grad_bias
 

time: 126 us -> 117 us (0.929)
  the two profiles are of different devices: /device:TPU:9 before, /device:TPU:4 now
where the time goes in v4:
time: 117 us; the launch traced here: 116 us
  starting transfers between devices  46.9 us (40%)
  Pallas kernels  32.2 us (28%)
  waiting for transfers between devices  30.7 us (26%)
  local copies, waits for them, and re-layouts  4.5 us (4%)
    all_to_all x4, starting transfers between devices, exchange(): return lax.all_to_all(pieces, 'ctx', 0, 0, tiled=True)  32 us
    all_to_all x4, waiting for transfers between devices, exchange(): return lax.all_to_all(pieces, 'ctx', 0, 0, tiled=True)  28.8 us
    ppermute x4, starting transfers between devices, shifted(): lax.ppermute(x, 'ctx', [(i, i + by) for i in range(peers) if 0 <= i + by...  11.4 us
    pallas_call x1, Pallas kernels, own_part(): pl.pallas_call(own_kernel, grid=(HEADS // GROUP,), out_shape=(low_array(1...  7.08 us
    pallas_call x1, Pallas kernels, window(): pl.pallas_call(window_kernel, grid=(HEADS,), out_shape=(float_array(HEADS...  6.18 us
    unnamed x42, local copies, waits for them, and re-layouts  4.5 us
    pallas_call x1, Pallas kernels, merge(): pl.pallas_call(merge_kernel, grid=(HEADS // GROUP,), out_shape=(low_array...  4.15 us
    pallas_call x1, Pallas kernels, finish(): pl.pallas_call(finish_kernel, out_shape=(low_array(1, ROWS, WIDTH),) * 2,...  3.49 us
  transfers between devices with their start and end apart: 11, of which 6 were waited for; matrix products, arithmetic and copies ran while one was open for 1% of the time, Pallas kernels for 20%

profile of v4, /device:TPU:4, one launch (start us, length us, event | category | flops | bytes accessed | tf_op | source)
XLA Modules:
  0.0 115.8 jit_solution(17853239868933572230)
XLA Ops:
  0.6 3.1 %cut_prompt.1 = (bf16[8,8,32,128]{3,2,1,0:T(8,128)(2,1)}, bf16[2,128,1024]{2,1,0:T(8,128)(2,1)}, bf16[2,128,1024]{2,1,0:T(8,128)(2,1)}) custom-call(s32[1,64]{1,0:T(1,128)} %starts_ref.9, bf16[1,256,1024]{2,1,0:T(8,128)(2,1)} %k_ref.3, bf16[1,256,1024]{2,1,0:T(8,128)(2,1)} %v_ref.3), custom_call_target="tpu_custom_call" | custom-call | tf_op jit(solution)/shard_map/cut_prompt/pallas_call | solution.py:117
  3.7 12.9 %all-to-all-start = ((bf16[64,32,128]{2,1,0:T(8,128)(2,1)}), bf16[64,32,128]{2,1,0:T(8,128)(2,1)S(1)}, u32[]{:S(2)}, u32[]{:S(2)}) async-start(bf16[64,32,128]{2,1,0:T(8,128)(2,1)} %bitcast.7), calls=%async_computation | async-start | bytes 1048576 | tf_op jit(solution)/shard_map/all_to_all | solution.py:633
  16.6 4.3 %collective-permute-start = (bf16[2,128,1024]{2,1,0:T(8,128)(2,1)}, bf16[2,128,1024]{2,1,0:T(8,128)(2,1)}, u32[]{:S(2)}, u32[]{:S(2)}) collective-permute-start(bf16[2,128,1024]{2,1,0:T(8,128)(2,1)} %get-tuple-element.34), channel_id=1, source_target_pairs={{0,1},{1,2},{2,3},{3,4},{4,5},{5,6},{6,7},{7,8},{8,9},{9,10},{10,1... | collective-permute-start | bytes 1572872 | tf_op jit(solution)/shard_map/ppermute | solution.py:638
  20.9 1.3 %collective-permute-start.1 = (bf16[2,128,1024]{2,1,0:T(8,128)(2,1)S(1)}, bf16[2,128,1024]{2,1,0:T(8,128)(2,1)}, u32[]{:S(2)}, u32[]{:S(2)}) collective-permute-start(bf16[2,128,1024]{2,1,0:T(8,128)(2,1)S(1)} %copy-done.20), channel_id=1, source_target_pairs={{1,0},{2,1},{3,2},{4,3},{5,4},{6,5},{7,6},{8,7},{9,8},{10,9},{11,1... | collective-permute-start | bytes 1572872 | tf_op jit(solution)/shard_map/ppermute | solution.py:638
  22.2 14.0 %all-to-all-done.in_ref = bf16[64,32,128]{2,1,0:T(8,128)(2,1)S(1)} async-done(((bf16[64,32,128]{2,1,0:T(8,128)(2,1)}), bf16[64,32,128]{2,1,0:T(8,128)(2,1)S(1)}, u32[]{:S(2)}, u32[]{:S(2)}) %all-to-all-start) | async-done | bytes 524320 | tf_op jit(solution)/shard_map/all_to_all | solution.py:633
  36.2 1.5 %route.1 = bf16[64,32,128]{2,1,0:T(8,128)(2,1)} custom-call(s32[1,64]{1,0:T(1,128)S(1)} %copy-done.3, bf16[64,32,128]{2,1,0:T(8,128)(2,1)S(1)} %all-to-all-done.in_ref), custom_call_target="tpu_custom_call" | custom-call | tf_op jit(solution)/shard_map/route/pallas_call | solution.py:150
  37.7 5.2 %all-to-all-start.1 = ((bf16[64,32,128]{2,1,0:T(8,128)(2,1)}), bf16[64,32,128]{2,1,0:T(8,128)(2,1)S(1)}, u32[]{:S(2)}, u32[]{:S(2)}) async-start(bf16[64,32,128]{2,1,0:T(8,128)(2,1)} %route.1), calls=%async_computation.1 | async-start | bytes 1048576 | tf_op jit(solution)/shard_map/all_to_all | solution.py:633
  43.0 6.2 %window.1 = (f32[8,8,256]{2,1,0:T(8,128)S(1)}, f32[256,256]{1,0:T(8,128)S(1)}, f32[256,256]{1,0:T(8,128)S(1)}, f32[2,128,128]{2,1,0:T(8,128)S(1)}, f32[128,256]{1,0:T(8,128)S(1)}) custom-call(s32[1,64]{1,0:T(1,128)S(1)} %copy-done.3, s32[1,64]{1,0:T(1,128)S(1)} %copy-done.8, f32[8]{0:T(128)S(1)} %copy-done.9, bf16[1,256,1024]{2,1,0:T(8,128)(2,1)S(1)} %copy-done.4, ...), custom_call_target="tpu_custom_call" | custom-call | flops 20000000000 | bytes 8388608 | tf_op jit(solution)/shard_map/window/pallas_call | solution.py:319
  49.2 0.6 copy-done.10
  49.8 0.7 copy-done.15
  50.5 0.7 copy-done.16
  51.2 8.1 %all-to-all-done.1 = bf16[64,32,128]{2,1,0:T(8,128)(2,1)S(1)} async-done(((bf16[64,32,128]{2,1,0:T(8,128)(2,1)}), bf16[64,32,128]{2,1,0:T(8,128)(2,1)S(1)}, u32[]{:S(2)}, u32[]{:S(2)}) %all-to-all-start.1) | async-done | bytes 524320 | tf_op jit(solution)/shard_map/all_to_all | solution.py:633
  59.4 2.7 %prompt_part.1 = (bf16[8,8,40,128]{3,2,1,0:T(8,128)(2,1)}, f32[8,8,256]{2,1,0:T(8,128)S(1)}) custom-call(f32[8]{0:T(128)S(1)} %copy-done.9, bf16[1,256,1024]{2,1,0:T(8,128)(2,1)S(1)} %copy-done.4, bf16[1,256,1024]{2,1,0:T(8,128)(2,1)S(1)} %copy-done.6, bf16[8,8,32,128]{3,2,1,0:T(8,128)(2,1)S(1)} %bitcast.4, f32[8,8,256]{2,1,0:T(8,128)S(1)} %get-tuple-element.37.stats_ref, ...), custom_call_target="tpu_custom_call" | custom-call | flops 4000000000 | bytes 8388608 | tf_op jit(solution)/shard_map/prompt_part/pallas_call | solution.py:391
  62.2 0.6 copy-done.13
  62.8 5.2 %all-to-all-start.2 = ((bf16[64,40,128]{2,1,0:T(8,128)(2,1)}), bf16[64,40,128]{2,1,0:T(8,128)(2,1)S(1)}, u32[]{:S(2)}, u32[]{:S(2)}) async-start(bf16[64,40,128]{2,1,0:T(8,128)(2,1)} %bitcast.2), calls=%async_computation.2 | async-start | bytes 1310720 | tf_op jit(solution)/shard_map/all_to_all | solution.py:633
  68.0 7.1 %own_part.1 = (bf16[1,256,1024]{2,1,0:T(8,128)(2,1)}, bf16[1,256,1024]{2,1,0:T(8,128)(2,1)}, f32[256,1024]{1,0:T(8,128)}, f32[256,1024]{1,0:T(8,128)}) custom-call(f32[8]{0:T(128)} %bias_ref.5, bf16[1,256,1024]{2,1,0:T(8,128)(2,1)} %q_ref.7, bf16[1,256,1024]{2,1,0:T(8,128)(2,1)} %d_ref.7, bf16[1,256,1024]{2,1,0:T(8,128)(2,1)} %k_ref.3, ...), custom_call_target="tpu_custom_call" | custom-call | flops 10000000000 | bytes 8388608 | tf_op jit(solution)/shard_map/own_part/pallas_call | solution.py:525
  75.1 2.4 %halo_grads.1 = (bf16[2,128,1024]{2,1,0:T(8,128)(2,1)S(1)}, bf16[2,128,1024]{2,1,0:T(8,128)(2,1)S(1)}) custom-call(bf16[1,256,1024]{2,1,0:T(8,128)(2,1)S(1)} %copy-done.5, bf16[1,256,1024]{2,1,0:T(8,128)(2,1)S(1)} %copy-done.7, bf16[2,128,1024]{2,1,0:T(8,128)(2,1)} %collective-permute-done.low_ref, bf16[2,128,1024]{2,1,0:T(8,128)(2,1)} %collective-permute-done.1.high_ref, ...), custom_call_target="tpu_custom_call" | custom-call | flops 4000000000 | bytes 8388608 | tf_op jit(solution)/shard_map/halo_grads/pallas_call | solution.py:444
  77.6 1.3 %collective-permute-start.6 = (bf16[2,128,1024]{2,1,0:T(8,128)(2,1)S(1)}, bf16[2,128,1024]{2,1,0:T(8,128)(2,1)S(1)}, u32[]{:S(2)}, u32[]{:S(2)}) collective-permute-start(bf16[2,128,1024]{2,1,0:T(8,128)(2,1)S(1)} %get-tuple-element.49), channel_id=1, source_target_pairs={{1,0},{2,1},{3,2},{4,3},{5,4},{6,5},{7,6},{8,7},{9,8},{10,9},{11,1... | collective-permute-start | bytes 1572872 | tf_op jit(solution)/shard_map/ppermute | solution.py:638
  78.9 4.6 %collective-permute-start.5 = (bf16[2,128,1024]{2,1,0:T(8,128)(2,1)S(1)}, bf16[2,128,1024]{2,1,0:T(8,128)(2,1)S(1)}, u32[]{:S(2)}, u32[]{:S(2)}) collective-permute-start(bf16[2,128,1024]{2,1,0:T(8,128)(2,1)S(1)} %get-tuple-element.50), channel_id=1, source_target_pairs={{0,1},{1,2},{2,3},{3,4},{4,5},{5,6},{6,7},{7,8},{8,9},{9,10},{10,1... | collective-permute-start | bytes 1572872 | tf_op jit(solution)/shard_map/ppermute | solution.py:638
  83.5 2.8 %all-to-all-done.2.in_ref = bf16[64,40,128]{2,1,0:T(8,128)(2,1)S(1)} async-done(((bf16[64,40,128]{2,1,0:T(8,128)(2,1)}), bf16[64,40,128]{2,1,0:T(8,128)(2,1)S(1)}, u32[]{:S(2)}, u32[]{:S(2)}) %all-to-all-start.2) | async-done | bytes 655392 | tf_op jit(solution)/shard_map/all_to_all | solution.py:633
  86.3 1.6 %gather.1 = (bf16[64,32,128]{2,1,0:T(8,128)(2,1)}, f32[8,128]{1,0:T(8,128)S(1)}) custom-call(s32[1,64]{1,0:T(1,128)S(1)} %copy-done.3, bf16[64,40,128]{2,1,0:T(8,128)(2,1)S(1)} %all-to-all-done.2.in_ref), custom_call_target="tpu_custom_call" | custom-call | tf_op jit(solution)/shard_map/gather/pallas_call | solution.py:179
  87.9 8.7 %all-to-all-start.3 = ((bf16[64,32,128]{2,1,0:T(8,128)(2,1)}), bf16[64,32,128]{2,1,0:T(8,128)(2,1)S(1)}, u32[]{:S(2)}, u32[]{:S(2)}) async-start(bf16[64,32,128]{2,1,0:T(8,128)(2,1)} %get-tuple-element.57), calls=%async_computation.3 | async-start | bytes 1048576 | tf_op jit(solution)/shard_map/all_to_all | solution.py:633
  96.7 0.9 collective-permute-start.3
  97.6 2.5 %collective-permute-start.2 = (f32[8,128]{1,0:T(8,128)S(1)}, f32[8,128]{1,0:T(8,128)S(1)}, u32[]{:S(2)}, u32[]{:S(2)}) collective-permute-start(f32[8,128]{1,0:T(8,128)S(1)} %get-tuple-element.52), channel_id=1, source_target_pairs={{0,64},{64,0},{128,192},{192,128},{1,65},{65,1},{129,193},{193,129... | collective-permute-start | bytes 12296 | tf_op jit(solution)/shard_map/ppermute | solution.py:643
  100.1 1.4 %collective-permute-done.4 = f32[8,128]{1,0:T(8,128)S(1)} collective-permute-done((f32[8,128]{1,0:T(8,128)S(1)}, f32[8,128]{1,0:T(8,128)S(1)}, u32[]{:S(2)}, u32[]{:S(2)}) %collective-permute-start.4) | collective-permute-done | bytes 4128 | tf_op jit(solution)/shard_map/ppermute | solution.py:643
  101.5 0.5 collective-permute-done.3
  101.9 0.6 add_reduce_fusion
  102.6 0.8 copy-done.18
  103.6 4.1 %merge.1 = (bf16[1,256,1024]{2,1,0:T(8,128)(2,1)}, bf16[1,256,1024]{2,1,0:T(8,128)(2,1)}, f32[256,1024]{1,0:T(8,128)}, f32[256,1024]{1,0:T(8,128)}) custom-call(f32[256,1024]{1,0:T(8,128)} %get-tuple-element.53.gk_ref, f32[256,1024]{1,0:T(8,128)} %get-tuple-element.54.gv_ref, bf16[2,128,1024]{2,1,0:T(8,128)(2,1)} %copy-done.19, bf16[2,128,1024]{2,1,0:T(8,128)(2,1)} %copy-done.18), custom_call_target="tpu_custom_call" | custom-call | flops 8000000000 | bytes 8388608 | tf_op jit(solution)/shard_map/merge/pallas_call | solution.py:557
  107.7 3.8 %all-to-all-done.3 = bf16[64,32,128]{2,1,0:T(8,128)(2,1)S(1)} async-done(((bf16[64,32,128]{2,1,0:T(8,128)(2,1)}), bf16[64,32,128]{2,1,0:T(8,128)(2,1)S(1)}, u32[]{:S(2)}, u32[]{:S(2)}) %all-to-all-start.3) | async-done | bytes 524320 | tf_op jit(solution)/shard_map/all_to_all | solution.py:633
  111.5 0.8 copy-done.17
  112.3 3.5 %finish.1 = (bf16[1,256,1024]{2,1,0:T(8,128)(2,1)}, bf16[1,256,1024]{2,1,0:T(8,128)(2,1)}) custom-call(s32[1,64]{1,0:T(1,128)} %starts_ref.9, f32[256,1024]{1,0:T(8,128)} %get-tuple-element.55.sumk_hbm, f32[256,1024]{1,0:T(8,128)} %get-tuple-element.56.sumv_hbm, bf16[8,8,32,128]{3,2,1,0:T(8,128)(2,1)} %bitcast.6, ...), custom_call_target="tpu_custom_call", output_to_operand_aliasing={{0}: (4, {}), {1}: (5, {})} | custom-call | tf_op jit(solution)/shard_map/finish/pallas_call | solution.py:615
  (42 shorter events, 0.4 us)
Async XLA Ops:
  3.7 17.2 %copy-start.20 = (bf16[2,128,1024]{2,1,0:T(8,128)(2,1)S(1)}, bf16[2,128,1024]{2,1,0:T(8,128)(2,1)}, u32[]{:S(2)}) copy-start(bf16[2,128,1024]{2,1,0:T(8,128)(2,1)} %get-tuple-element.35) | copy-start | bytes 1572868
  3.7 39.2 %copy-start.9 = (f32[8]{0:T(128)S(1)}, f32[8]{0:T(128)}, u32[]{:S(2)}) copy-start(f32[8]{0:T(128)} %bias_ref.5) | copy-start | bytes 100
  3.7 32.5 %all-to-all-start = ((bf16[64,32,128]{2,1,0:T(8,128)(2,1)}), bf16[64,32,128]{2,1,0:T(8,128)(2,1)S(1)}, u32[]{:S(2)}, u32[]{:S(2)}) async-start(bf16[64,32,128]{2,1,0:T(8,128)(2,1)} %bitcast.7), calls=%async_computation | async-start | bytes 1048576 | tf_op jit(solution)/shard_map/all_to_all | solution.py:633
  16.6 19.6 %copy-start.3 = (s32[1,64]{1,0:T(1,128)S(1)}, s32[1,64]{1,0:T(1,128)}, u32[]{:S(2)}) copy-start(s32[1,64]{1,0:T(1,128)} %starts_ref.9) | copy-start | bytes 772
  16.6 26.3 %collective-permute-start = (bf16[2,128,1024]{2,1,0:T(8,128)(2,1)}, bf16[2,128,1024]{2,1,0:T(8,128)(2,1)}, u32[]{:S(2)}, u32[]{:S(2)}) collective-permute-start(bf16[2,128,1024]{2,1,0:T(8,128)(2,1)} %get-tuple-element.34), channel_id=1, source_target_pairs={{0,1},{1,2},{2,3},{3,4},{4,5},{5,6},{6,7},{7,8},{8,9},{9,10},{10,1... | collective-permute-start | bytes 1572872 | tf_op jit(solution)/shard_map/ppermute | solution.py:638
  20.9 22.0 %collective-permute-start.1 = (bf16[2,128,1024]{2,1,0:T(8,128)(2,1)S(1)}, bf16[2,128,1024]{2,1,0:T(8,128)(2,1)}, u32[]{:S(2)}, u32[]{:S(2)}) collective-permute-start(bf16[2,128,1024]{2,1,0:T(8,128)(2,1)S(1)} %copy-done.20), channel_id=1, source_target_pairs={{1,0},{2,1},{3,2},{4,3},{5,4},{6,5},{7,6},{8,7},{9,8},{10,9},{11,1... | collective-permute-start | bytes 1572872 | tf_op jit(solution)/shard_map/ppermute | solution.py:638
  36.2 6.7 %copy-start.4 = (bf16[1,256,1024]{2,1,0:T(8,128)(2,1)S(1)}, bf16[1,256,1024]{2,1,0:T(8,128)(2,1)}, u32[]{:S(2)}) copy-start(bf16[1,256,1024]{2,1,0:T(8,128)(2,1)} %q_ref.7) | copy-start | bytes 1572868
  36.2 6.7 %copy-start.6 = (bf16[1,256,1024]{2,1,0:T(8,128)(2,1)S(1)}, bf16[1,256,1024]{2,1,0:T(8,128)(2,1)}, u32[]{:S(2)}) copy-start(bf16[1,256,1024]{2,1,0:T(8,128)(2,1)} %d_ref.7) | copy-start | bytes 1572868
  36.2 6.7 %copy-start.8 = (s32[1,64]{1,0:T(1,128)S(1)}, s32[1,64]{1,0:T(1,128)}, u32[]{:S(2)}) copy-start(s32[1,64]{1,0:T(1,128)} %lens_ref.1) | copy-start | bytes 772
  37.7 5.2 %copy-start.1 = (bf16[1,256,1024]{2,1,0:T(8,128)(2,1)S(1)}, bf16[1,256,1024]{2,1,0:T(8,128)(2,1)}, u32[]{:S(2)}) copy-start(bf16[1,256,1024]{2,1,0:T(8,128)(2,1)} %k_ref.3) | copy-start | bytes 1572868
  37.7 5.3 %copy-start.2 = (bf16[1,256,1024]{2,1,0:T(8,128)(2,1)S(1)}, bf16[1,256,1024]{2,1,0:T(8,128)(2,1)}, u32[]{:S(2)}) copy-start(bf16[1,256,1024]{2,1,0:T(8,128)(2,1)} %v_ref.3) | copy-start | bytes 1572868
  37.7 21.7 %all-to-all-start.1 = ((bf16[64,32,128]{2,1,0:T(8,128)(2,1)}), bf16[64,32,128]{2,1,0:T(8,128)(2,1)S(1)}, u32[]{:S(2)}, u32[]{:S(2)}) async-start(bf16[64,32,128]{2,1,0:T(8,128)(2,1)} %route.1), calls=%async_computation.1 | async-start | bytes 1048576 | tf_op jit(solution)/shard_map/all_to_all | solution.py:633
  49.2 0.7 copy-start.10
  49.8 0.7 copy-start.15
  50.5 0.7 copy-start.16
  51.2 10.9 %copy-start.12 = (f32[128,256]{1,0:T(8,128)}, f32[128,256]{1,0:T(8,128)S(1)}, u32[]{:S(2)}) copy-start(f32[128,256]{1,0:T(8,128)S(1)} %get-tuple-element.38.mask_ref.prompt_mask) | copy-start | bytes 393220
  59.4 2.8 %copy-start = (bf16[64,32,128]{2,1,0:T(8,128)(2,1)}, bf16[64,32,128]{2,1,0:T(8,128)(2,1)S(1)}, u32[]{:S(2)}) copy-start(bf16[64,32,128]{2,1,0:T(8,128)(2,1)S(1)} %all-to-all-done.1) | copy-start | bytes 1572868
  62.1 0.6 copy-start.13
  62.8 23.5 %all-to-all-start.2 = ((bf16[64,40,128]{2,1,0:T(8,128)(2,1)}), bf16[64,40,128]{2,1,0:T(8,128)(2,1)S(1)}, u32[]{:S(2)}, u32[]{:S(2)}) async-start(bf16[64,40,128]{2,1,0:T(8,128)(2,1)} %bitcast.2), calls=%async_computation.2 | async-start | bytes 1310720 | tf_op jit(solution)/shard_map/all_to_all | solution.py:633
  68.0 7.1 %copy-start.5 = (bf16[1,256,1024]{2,1,0:T(8,128)(2,1)S(1)}, bf16[1,256,1024]{2,1,0:T(8,128)(2,1)}, u32[]{:S(2)}) copy-start(bf16[1,256,1024]{2,1,0:T(8,128)(2,1)} %q_ref.7) | copy-start | bytes 1572868
  68.0 7.1 %copy-start.7 = (bf16[1,256,1024]{2,1,0:T(8,128)(2,1)S(1)}, bf16[1,256,1024]{2,1,0:T(8,128)(2,1)}, u32[]{:S(2)}) copy-start(bf16[1,256,1024]{2,1,0:T(8,128)(2,1)} %d_ref.7) | copy-start | bytes 1572868
  68.0 7.1 %copy-start.11 = (f32[2,128,128]{2,1,0:T(8,128)S(1)}, f32[2,128,128]{2,1,0:T(8,128)}, u32[]{:S(2)}) copy-start(f32[2,128,128]{2,1,0:T(8,128)} %copy-done.10) | copy-start | bytes 393220
  68.0 7.1 %copy-start.14 = (f32[8,8,256]{2,1,0:T(8,128)S(1)}, f32[8,8,256]{2,1,0:T(8,128)}, u32[]{:S(2)}) copy-start(f32[8,8,256]{2,1,0:T(8,128)} %copy-done.13) | copy-start | bytes 196612
  77.6 25.0 %collective-permute-start.6 = (bf16[2,128,1024]{2,1,0:T(8,128)(2,1)S(1)}, bf16[2,128,1024]{2,1,0:T(8,128)(2,1)S(1)}, u32[]{:S(2)}, u32[]{:S(2)}) collective-permute-start(bf16[2,128,1024]{2,1,0:T(8,128)(2,1)S(1)} %get-tuple-element.49), channel_id=1, source_target_pairs={{1,0},{2,1},{3,2},{4,3},{5,4},{6,5},{7,6},{8,7},{9,8},{10,9},{11,1... | collective-permute-start | bytes 1572872 | tf_op jit(solution)/shard_map/ppermute | solution.py:638
  78.9 23.7 %collective-permute-start.5 = (bf16[2,128,1024]{2,1,0:T(8,128)(2,1)S(1)}, bf16[2,128,1024]{2,1,0:T(8,128)(2,1)S(1)}, u32[]{:S(2)}, u32[]{:S(2)}) collective-permute-start(bf16[2,128,1024]{2,1,0:T(8,128)(2,1)S(1)} %get-tuple-element.50), channel_id=1, source_target_pairs={{0,1},{1,2},{2,3},{3,4},{4,5},{5,6},{6,7},{7,8},{8,9},{9,10},{10,1... | collective-permute-start | bytes 1572872 | tf_op jit(solution)/shard_map/ppermute | solution.py:638
  87.9 23.6 %all-to-all-start.3 = ((bf16[64,32,128]{2,1,0:T(8,128)(2,1)}), bf16[64,32,128]{2,1,0:T(8,128)(2,1)S(1)}, u32[]{:S(2)}, u32[]{:S(2)}) async-start(bf16[64,32,128]{2,1,0:T(8,128)(2,1)} %get-tuple-element.57), calls=%async_computation.3 | async-start | bytes 1048576 | tf_op jit(solution)/shard_map/all_to_all | solution.py:633
  96.6 4.8 %collective-permute-start.4 = (f32[8,128]{1,0:T(8,128)S(1)}, f32[8,128]{1,0:T(8,128)S(1)}, u32[]{:S(2)}, u32[]{:S(2)}) collective-permute-start(f32[8,128]{1,0:T(8,128)S(1)} %get-tuple-element.52), channel_id=1, source_target_pairs={{0,192},{64,128},{128,64},{192,0},{1,193},{65,129},{129,65},{193,1... | collective-permute-start | bytes 12296 | tf_op jit(solution)/shard_map/ppermute | solution.py:643
  96.7 5.2 %collective-permute-start.3 = (f32[8,128]{1,0:T(8,128)S(1)}, f32[8,128]{1,0:T(8,128)S(1)}, u32[]{:S(2)}, u32[]{:S(2)}) collective-permute-start(f32[8,128]{1,0:T(8,128)S(1)} %get-tuple-element.52), channel_id=1, source_target_pairs={{0,128},{64,192},{128,0},{192,64},{1,129},{65,193},{129,1},{193,65... | collective-permute-start | bytes 12296 | tf_op jit(solution)/shard_map/ppermute | solution.py:643
  97.6 4.3 %collective-permute-start.2 = (f32[8,128]{1,0:T(8,128)S(1)}, f32[8,128]{1,0:T(8,128)S(1)}, u32[]{:S(2)}, u32[]{:S(2)}) collective-permute-start(f32[8,128]{1,0:T(8,128)S(1)} %get-tuple-element.52), channel_id=1, source_target_pairs={{0,64},{64,0},{128,192},{192,128},{1,65},{65,1},{129,193},{193,129... | collective-permute-start | bytes 12296 | tf_op jit(solution)/shard_map/ppermute | solution.py:643
  102.6 0.8 copy-start.18
  102.6 1.0 copy-start.19
  111.5 0.8 copy-start.17

commit v5 on v4

--- a/solution.py
+++ b/solution.py
@@ -30,7 +30,7 @@
 HBM = pl.BlockSpec(memory_space=pltpu.HBM)
 PARAMS = pltpu.CompilerParams(vmem_limit_bytes=20 * 1024 * 1024)
 FROM_HBM = pltpu.CompilerParams(vmem_limit_bytes=60 * 1024 * 1024)
-NEARLY = pltpu.CompilerParams(vmem_limit_bytes=58 * 1024 * 1024)
+NEARLY = pltpu.CompilerParams(vmem_limit_bytes=52 * 1024 * 1024)
 
 
 def nt(a, b):
@@ -206,7 +206,7 @@
     ref[...] = jnp.where(allowed, 0.0, NEG)
 
 
-def hold_masks(starts_ref, lens_ref, own_mask, own_flag, halo_mask, prompt_mask):
+def hold_masks(starts_ref, lens_ref, own_mask, halo_mask, prompt_mask):
     me = lax.axis_index("ctx")
     last = starts_ref.shape[1] - 1
     begins, offset = own_start(starts_ref, me)
@@ -215,8 +215,8 @@
     key, row = grid_of(ROWS, ROWS)
     prompt = (key >= offset) & (key < offset + own_len)
     near = jnp.abs(row - key) <= HW
-    hold(own_mask, ((row >= offset) == (key >= offset)) & (prompt | near))
-    own_flag[...] = prompt.astype(jnp.float32)
+    hold(own_mask.at[0], ((row >= offset) == (key >= offset)) & (prompt | near))
+    own_mask[1] = prompt.astype(jnp.float32)
     start, length = carried_prompt(starts_ref, lens_ref, me)
     prompt_end = start + length - (me * ROWS - HW)
     next_begins, next_offset = own_start(starts_ref, jnp.minimum(me + 1, last))
@@ -249,7 +249,6 @@
     high_ref,
     stats_ref,
     own_mask,
-    own_flag,
     halo_mask,
     prompt_mask,
 ):
@@ -257,12 +256,12 @@
 
     @pl.when(head == 0)
     def _():
-        hold_masks(starts_ref, lens_ref, own_mask, own_flag, halo_mask, prompt_mask)
+        hold_masks(starts_ref, lens_ref, own_mask, halo_mask, prompt_mask)
 
     q, d, k, v = q_ref[0], d_ref[0], k_ref[0], v_ref[0]
     bias = bias_ref[head] * LOG2E
-    flag = own_flag[...]
-    x_own = nt(k, q) * FACTOR + (own_mask[...] + flag * bias)
+    flag = own_mask[1]
+    x_own = nt(k, q) * FACTOR + (own_mask[0] + flag * bias)
     x_low = nt(low_ref[0], q[:HW]) * FACTOR + halo_mask[0]
     x_high = nt(high_ref[0], q[HW:]) * FACTOR + halo_mask[1]
     tops = jnp.concatenate([top_of(x_low), top_of(x_high)], axis=1)
@@ -299,8 +298,7 @@
 
 
 MASKS = (
-    float_array(ROWS, ROWS),
-    float_array(ROWS, ROWS),
+    float_array(2, ROWS, ROWS),
     float_array(2, HW, HW),
     float_array(PMAX, ROWS),
 )
@@ -463,7 +461,6 @@
     prompt_ref,
     final_ref,
     own_mask,
-    own_flag,
     halo_mask,
     prompt_mask,
     attended_ref,
@@ -493,7 +490,7 @@
         bias = bias_ref[step * GROUP + member] * LOG2E
         final = final_ref[member]
         added = (
-            own_mask[...] + own_flag[...] * bias,
+            own_mask[0] + own_mask[1] * bias,
             prompt_mask[...] + bias,
             halo_mask[0],
             halo_mask[1],
@@ -540,13 +537,12 @@
     )(bias, queries, cotangent, key_rows, values, low, high, prompt, final, *masks)
 
 
-def merge_kernel(gk_ref, gv_ref, left_ref, right_ref, outk_ref, outv_ref, sumk_ref, sumv_ref):
-    terms = ((gk_ref, outk_ref, sumk_ref), (gv_ref, outv_ref, sumv_ref))
-    for part, (ref, out, sums) in enumerate(terms):
+def merge_kernel(gk_ref, gv_ref, left_ref, right_ref, outk_ref, outv_ref, sums_ref):
+    for part, (ref, out) in enumerate(((gk_ref, outk_ref), (gv_ref, outv_ref))):
         for half, side in enumerate((left_ref, right_ref)):
             rows = slice(half * HW, (half + 1) * HW)
             total = ref[rows, :] + side[part].astype(jnp.float32)
-            sums[rows, :] = total
+            sums_ref[part, rows, :] = total
             out[0, rows, :] = total.astype(jnp.bfloat16)
 
 
@@ -554,13 +550,14 @@
     total = pl.BlockSpec((ROWS, GROUP * HD), lambda step: (0, step))
     rows = pl.BlockSpec((1, ROWS, GROUP * HD), lambda step: (0, 0, step))
     side = pl.BlockSpec((2, HW, GROUP * HD), lambda step: (0, 0, step))
+    both = pl.BlockSpec((2, ROWS, GROUP * HD), lambda step: (0, 0, step))
     return pl.pallas_call(
         merge_kernel,
         grid=(HEADS // GROUP,),
-        out_shape=(low_array(1, ROWS, WIDTH),) * 2 + (float_array(ROWS, WIDTH),) * 2,
+        out_shape=(low_array(1, ROWS, WIDTH),) * 2 + (float_array(2, ROWS, WIDTH),),
         in_specs=[total, total, side, side],
-        out_specs=(rows, rows, total, total),
-        compiler_params=FROM_HBM,
+        out_specs=(rows, rows, both),
+        compiler_params=NEARLY,
         cost_estimate=cost(MERGE),
         name="merge",
     )(gk, gv, left, right)
@@ -568,8 +565,7 @@
 
 def finish_kernel(
     starts_ref,
-    sumk_hbm,
-    sumv_hbm,
+    sums_hbm,
     prompt_ref,
     _ink,
     _inv,
@@ -588,8 +584,8 @@
         base = pl.multiple_of(jnp.minimum(offset // BAND * BAND, ROWS - SPAN), BAND)
         span = pl.ds(base, SPAN)
         loads = [
-            pltpu.make_async_copy(ref.at[span, :], sums_ref.at[part], load_sems.at[part])
-            for part, ref in enumerate((sumk_hbm, sumv_hbm))
+            pltpu.make_async_copy(sums_hbm.at[part, span, :], sums_ref.at[part], load_sems.at[part])
+            for part in range(2)
         ]
         stores = [
             pltpu.make_async_copy(rows_ref.at[part], ref.at[0, span, :], store_sems.at[part])
@@ -611,13 +607,13 @@
             copy.wait()
 
 
-def finish(starts, outk, outv, sumk, sumv, prompt):
+def finish(starts, outk, outv, sums, prompt):
     return pl.pallas_call(
         finish_kernel,
         out_shape=(low_array(1, ROWS, WIDTH),) * 2,
-        in_specs=[SMEM, HBM, HBM, VMEM, HBM, HBM],
+        in_specs=[SMEM, HBM, VMEM, HBM, HBM],
         out_specs=(HBM, HBM),
-        input_output_aliases={4: 0, 5: 1},
+        input_output_aliases={3: 0, 4: 1},
         scratch_shapes=[
             pltpu.VMEM((2, SPAN, WIDTH), jnp.float32),
             pltpu.VMEM((2, SPAN, WIDTH), jnp.bfloat16),
@@ -626,7 +622,7 @@
         ],
         compiler_params=NEARLY,
         name="finish",
-    )(starts, sumk, sumv, prompt, outk, outv)
+    )(starts, sums, prompt, outk, outv)
 
 
 def exchange(pieces):
@@ -658,13 +654,13 @@
         starts, lens, bias, queries, cotangent, key_rows, values, low, high
     )
     prompt = exchange(route(starts, held)).reshape(BANDS, HEADS, 2 * BAND, HD)
-    gprompt, final = prompt_part(bias, queries, cotangent, prompt, stats, masks[3])
+    gprompt, final = prompt_part(bias, queries, cotangent, prompt, stats, masks[2])
     held = exchange(gprompt.reshape(count, SENT, HD))
     attended, grad_q, gk, gv = own_part(
         bias, queries, cotangent, key_rows, values, low, high, prompt, final, masks
     )
     final, gk = lax.optimization_barrier((final, gk))
-    glow, ghigh = halo_grads(queries, cotangent, low, high, final, masks[2])
+    glow, ghigh = halo_grads(queries, cotangent, low, high, final, masks[1])
     right = shifted(glow, -1)
     left = shifted(ghigh, 1)
     held, glow, ghigh = lax.optimization_barrier((held, glow, ghigh))
@@ -672,8 +668,8 @@
     returned = exchange(owned).reshape(BANDS, HEADS, 2 * BAND, HD)
     grad_bias = jnp.sum(summed(sums, "dp", 1, 2), axis=1)
     gk, grad_bias = lax.optimization_barrier((gk, grad_bias))
-    outk, outv, sumk, sumv = merge(gk, gv, left, right)
-    grad_k, grad_v = finish(starts, outk, outv, sumk, sumv, returned)
+    outk, outv, both = merge(gk, gv, left, right)
+    grad_k, grad_v = finish(starts, outk, outv, both, returned)
     return attended, grad_q, grad_k, grad_v, grad_bias
 
 

time: 117 us -> 115 us (0.983)
  local copies, waits for them, and re-layouts: 4.5 us -> 0.82 us
  waiting for transfers between devices: 30.7 us -> 32.5 us
    unnamed x42 -> x18, local copies, waits for them, and re-layouts: 4.5 us -> 0.82 us
    all_to_all x4, waiting for transfers between devices: 28.8 us -> 30.6 us  [exchange(): return lax.all_to_all(pieces, 'ctx', 0, 0, tiled=True)]
  transfers between devices with their start and end apart: 11 -> 11, of which waited for: 6 -> 6; matrix products, arithmetic and copies ran while one was open for 1% -> 1% of each run, Pallas kernels for 20% -> 21%
where the time goes in v5:
time: 115 us; the launch traced here: 114 us
  starting transfers between devices  47.2 us (41%)
  waiting for transfers between devices  32.5 us (28%)
  Pallas kernels  32.3 us (28%)
    all_to_all x4, starting transfers between devices, exchange(): return lax.all_to_all(pieces, 'ctx', 0, 0, tiled=True)  32.3 us
    all_to_all x4, waiting for transfers between devices, exchange(): return lax.all_to_all(pieces, 'ctx', 0, 0, tiled=True)  30.6 us
    ppermute x4, starting transfers between devices, shifted(): lax.ppermute(x, 'ctx', [(i, i + by) for i in range(peers) if 0 <= i + by...  11.4 us
    pallas_call x1, Pallas kernels, own_part(): pl.pallas_call(own_kernel, grid=(HEADS // GROUP,), out_shape=(low_array(1...  6.9 us
    pallas_call x1, Pallas kernels, window(): pl.pallas_call(window_kernel, grid=(HEADS,), out_shape=(float_array(HEADS...  6.18 us
    pallas_call x1, Pallas kernels, merge(): pl.pallas_call(merge_kernel, grid=(HEADS // GROUP,), out_shape=(low_array...  4 us
    ppermute x3, starting transfers between devices, partners(): lax.ppermute(x, axis, [(i, i ^ step) for i in range(peers)])  3.44 us
    pallas_call x1, Pallas kernels, halo_grads(): pl.pallas_call(halo_kernel, out_shape=(low_array(2, HW, WIDTH), low_array...  3.26 us
  transfers between devices with their start and end apart: 11, of which 6 were waited for; matrix products, arithmetic and copies ran while one was open for 1% of the time, Pallas kernels for 21%

profile of v5, /device:TPU:4, one launch (start us, length us, event | category | flops | bytes accessed | tf_op | source)
XLA Modules:
  0.0 114.3 jit_solution(17562725537494657609)
XLA Ops:
  0.6 0.0 copy-start.2
  0.7 3.2 %cut_prompt.1 = (bf16[8,8,32,128]{3,2,1,0:T(8,128)(2,1)}, bf16[2,128,1024]{2,1,0:T(8,128)(2,1)}, bf16[2,128,1024]{2,1,0:T(8,128)(2,1)}) custom-call(s32[1,64]{1,0:T(1,128)} %starts_ref.9, bf16[1,256,1024]{2,1,0:T(8,128)(2,1)} %k_ref.3, bf16[1,256,1024]{2,1,0:T(8,128)(2,1)} %v_ref.3), custom_call_target="tpu_custom_call" | custom-call | tf_op jit(solution)/shard_map/cut_prompt/pallas_call | solution.py:117
  3.9 12.7 %all-to-all-start = ((bf16[64,32,128]{2,1,0:T(8,128)(2,1)}), bf16[64,32,128]{2,1,0:T(8,128)(2,1)S(1)}, u32[]{:S(2)}, u32[]{:S(2)}) async-start(bf16[64,32,128]{2,1,0:T(8,128)(2,1)} %bitcast.7), calls=%async_computation | async-start | bytes 1048576 | tf_op jit(solution)/shard_map/all_to_all | solution.py:629
  16.7 4.3 %collective-permute-start = (bf16[2,128,1024]{2,1,0:T(8,128)(2,1)}, bf16[2,128,1024]{2,1,0:T(8,128)(2,1)}, u32[]{:S(2)}, u32[]{:S(2)}) collective-permute-start(bf16[2,128,1024]{2,1,0:T(8,128)(2,1)} %get-tuple-element.32), channel_id=1, source_target_pairs={{0,1},{1,2},{2,3},{3,4},{4,5},{5,6},{6,7},{7,8},{8,9},{9,10},{10,1... | collective-permute-start | bytes 1572872 | tf_op jit(solution)/shard_map/ppermute | solution.py:634
  20.9 1.3 %collective-permute-start.1 = (bf16[2,128,1024]{2,1,0:T(8,128)(2,1)}, bf16[2,128,1024]{2,1,0:T(8,128)(2,1)}, u32[]{:S(2)}, u32[]{:S(2)}) collective-permute-start(bf16[2,128,1024]{2,1,0:T(8,128)(2,1)} %get-tuple-element.33), channel_id=1, source_target_pairs={{1,0},{2,1},{3,2},{4,3},{5,4},{6,5},{7,6},{8,7},{9,8},{10,9},{11,1... | collective-permute-start | bytes 1572872 | tf_op jit(solution)/shard_map/ppermute | solution.py:634
  22.2 14.0 %all-to-all-done.in_ref = bf16[64,32,128]{2,1,0:T(8,128)(2,1)S(1)} async-done(((bf16[64,32,128]{2,1,0:T(8,128)(2,1)}), bf16[64,32,128]{2,1,0:T(8,128)(2,1)S(1)}, u32[]{:S(2)}, u32[]{:S(2)}) %all-to-all-start) | async-done | bytes 524320 | tf_op jit(solution)/shard_map/all_to_all | solution.py:629
  36.3 1.5 %route.1 = bf16[64,32,128]{2,1,0:T(8,128)(2,1)} custom-call(s32[1,64]{1,0:T(1,128)S(1)} %copy-done.3, bf16[64,32,128]{2,1,0:T(8,128)(2,1)S(1)} %all-to-all-done.in_ref), custom_call_target="tpu_custom_call" | custom-call | tf_op jit(solution)/shard_map/route/pallas_call | solution.py:150
  37.7 5.1 %all-to-all-start.1 = ((bf16[64,32,128]{2,1,0:T(8,128)(2,1)}), bf16[64,32,128]{2,1,0:T(8,128)(2,1)S(1)}, u32[]{:S(2)}, u32[]{:S(2)}) async-start(bf16[64,32,128]{2,1,0:T(8,128)(2,1)} %route.1), calls=%async_computation.1 | async-start | bytes 1048576 | tf_op jit(solution)/shard_map/all_to_all | solution.py:629
  42.9 6.2 %window.1 = (f32[8,8,256]{2,1,0:T(8,128)S(1)}, f32[2,256,256]{2,1,0:T(8,128)S(1)}, f32[2,128,128]{2,1,0:T(8,128)S(1)}, f32[128,256]{1,0:T(8,128)S(1)}) custom-call(s32[1,64]{1,0:T(1,128)S(1)} %copy-done.3, s32[1,64]{1,0:T(1,128)S(1)} %copy-done.6, f32[8]{0:T(128)S(1)} %copy-done.7, bf16[1,256,1024]{2,1,0:T(8,128)(2,1)S(1)} %copy-done.4, ...), custom_call_target="tpu_custom_call" | custom-call | flops 20000000000 | bytes 8388608 | tf_op jit(solution)/shard_map/window/pallas_call | solution.py:317
  49.1 0.0 copy-start.8
  49.1 0.8 copy-done.8
  49.9 9.4 %all-to-all-done.1 = bf16[64,32,128]{2,1,0:T(8,128)(2,1)S(1)} async-done(((bf16[64,32,128]{2,1,0:T(8,128)(2,1)}), bf16[64,32,128]{2,1,0:T(8,128)(2,1)S(1)}, u32[]{:S(2)}, u32[]{:S(2)}) %all-to-all-start.1) | async-done | bytes 524320 | tf_op jit(solution)/shard_map/all_to_all | solution.py:629
  59.3 2.7 %prompt_part.1 = (bf16[8,8,40,128]{3,2,1,0:T(8,128)(2,1)}, f32[8,8,256]{2,1,0:T(8,128)S(1)}) custom-call(f32[8]{0:T(128)S(1)} %copy-done.7, bf16[1,256,1024]{2,1,0:T(8,128)(2,1)S(1)} %copy-done.4, bf16[1,256,1024]{2,1,0:T(8,128)(2,1)S(1)} %copy-done.5, bf16[8,8,32,128]{3,2,1,0:T(8,128)(2,1)S(1)} %bitcast.5, f32[8,8,256]{2,1,0:T(8,128)S(1)} %get-tuple-element.35.stats_ref, ...), custom_call_target="tpu_custom_call" | custom-call | flops 4000000000 | bytes 8388608 | tf_op jit(solution)/shard_map/prompt_part/pallas_call | solution.py:389
  62.0 5.2 %all-to-all-start.2 = ((bf16[64,40,128]{2,1,0:T(8,128)(2,1)}), bf16[64,40,128]{2,1,0:T(8,128)(2,1)S(1)}, u32[]{:S(2)}, u32[]{:S(2)}) async-start(bf16[64,40,128]{2,1,0:T(8,128)(2,1)} %bitcast.2), calls=%async_computation.2 | async-start | bytes 1310720 | tf_op jit(solution)/shard_map/all_to_all | solution.py:629
  67.3 6.9 %own_part.1 = (bf16[1,256,1024]{2,1,0:T(8,128)(2,1)}, bf16[1,256,1024]{2,1,0:T(8,128)(2,1)}, f32[256,1024]{1,0:T(8,128)}, f32[256,1024]{1,0:T(8,128)}) custom-call(f32[8]{0:T(128)S(1)} %copy-done.7, bf16[1,256,1024]{2,1,0:T(8,128)(2,1)S(1)} %copy-done.4, bf16[1,256,1024]{2,1,0:T(8,128)(2,1)S(1)} %copy-done.5, bf16[1,256,1024]{2,1,0:T(8,128)(2,1)S(1)} %copy-done.1, ...), custom_call_target="tpu_custom_call" | custom-call | flops 10000000000 | bytes 8388608 | tf_op jit(solution)/shard_map/own_part/pallas_call | solution.py:522
  74.2 3.3 %halo_grads.1 = (bf16[2,128,1024]{2,1,0:T(8,128)(2,1)}, bf16[2,128,1024]{2,1,0:T(8,128)(2,1)S(1)}) custom-call(bf16[1,256,1024]{2,1,0:T(8,128)(2,1)S(1)} %copy-done.4, bf16[1,256,1024]{2,1,0:T(8,128)(2,1)S(1)} %copy-done.5, bf16[2,128,1024]{2,1,0:T(8,128)(2,1)} %collective-permute-done.low_ref, bf16[2,128,1024]{2,1,0:T(8,128)(2,1)} %collective-permute-done.1.high_ref, ...), custom_call_target="tpu_custom_call" | custom-call | flops 4000000000 | bytes 8388608 | tf_op jit(solution)/shard_map/halo_grads/pallas_call | solution.py:442
  77.4 1.3 %collective-permute-start.6 = (bf16[2,128,1024]{2,1,0:T(8,128)(2,1)}, bf16[2,128,1024]{2,1,0:T(8,128)(2,1)S(1)}, u32[]{:S(2)}, u32[]{:S(2)}) collective-permute-start(bf16[2,128,1024]{2,1,0:T(8,128)(2,1)} %get-tuple-element.46), channel_id=1, source_target_pairs={{1,0},{2,1},{3,2},{4,3},{5,4},{6,5},{7,6},{8,7},{9,8},{10,9},{11,1... | collective-permute-start | bytes 1572872 | tf_op jit(solution)/shard_map/ppermute | solution.py:634
  78.7 4.6 %collective-permute-start.5 = (bf16[2,128,1024]{2,1,0:T(8,128)(2,1)S(1)}, bf16[2,128,1024]{2,1,0:T(8,128)(2,1)S(1)}, u32[]{:S(2)}, u32[]{:S(2)}) collective-permute-start(bf16[2,128,1024]{2,1,0:T(8,128)(2,1)S(1)} %get-tuple-element.47), channel_id=1, source_target_pairs={{0,1},{1,2},{2,3},{3,4},{4,5},{5,6},{6,7},{7,8},{8,9},{9,10},{10,1... | collective-permute-start | bytes 1572872 | tf_op jit(solution)/shard_map/ppermute | solution.py:634
  83.3 2.3 %all-to-all-done.2.in_ref = bf16[64,40,128]{2,1,0:T(8,128)(2,1)S(1)} async-done(((bf16[64,40,128]{2,1,0:T(8,128)(2,1)}), bf16[64,40,128]{2,1,0:T(8,128)(2,1)S(1)}, u32[]{:S(2)}, u32[]{:S(2)}) %all-to-all-start.2) | async-done | bytes 655392 | tf_op jit(solution)/shard_map/all_to_all | solution.py:629
  85.6 1.6 %gather.1 = (bf16[64,32,128]{2,1,0:T(8,128)(2,1)}, f32[8,128]{1,0:T(8,128)S(1)}) custom-call(s32[1,64]{1,0:T(1,128)S(1)} %copy-done.3, bf16[64,40,128]{2,1,0:T(8,128)(2,1)S(1)} %all-to-all-done.2.in_ref), custom_call_target="tpu_custom_call" | custom-call | tf_op jit(solution)/shard_map/gather/pallas_call | solution.py:179
  87.2 9.3 %all-to-all-start.3 = ((bf16[64,32,128]{2,1,0:T(8,128)(2,1)}), bf16[64,32,128]{2,1,0:T(8,128)(2,1)S(1)}, u32[]{:S(2)}, u32[]{:S(2)}) async-start(bf16[64,32,128]{2,1,0:T(8,128)(2,1)} %get-tuple-element.53), calls=%async_computation.3 | async-start | bytes 1048576 | tf_op jit(solution)/shard_map/all_to_all | solution.py:629
  96.5 0.1 collective-permute-start.4
  96.6 0.8 collective-permute-start.3
  97.4 2.5 %collective-permute-start.2 = (f32[8,128]{1,0:T(8,128)S(1)}, f32[8,128]{1,0:T(8,128)S(1)}, u32[]{:S(2)}, u32[]{:S(2)}) collective-permute-start(f32[8,128]{1,0:T(8,128)S(1)} %get-tuple-element.49), channel_id=1, source_target_pairs={{0,64},{64,0},{128,192},{192,128},{1,65},{65,1},{129,193},{193,129... | collective-permute-start | bytes 12296 | tf_op jit(solution)/shard_map/ppermute | solution.py:639
  99.9 1.3 %collective-permute-done.4 = f32[8,128]{1,0:T(8,128)S(1)} collective-permute-done((f32[8,128]{1,0:T(8,128)S(1)}, f32[8,128]{1,0:T(8,128)S(1)}, u32[]{:S(2)}, u32[]{:S(2)}) %collective-permute-start.4) | collective-permute-done | bytes 4128 | tf_op jit(solution)/shard_map/ppermute | solution.py:639
  101.3 0.5 collective-permute-done.3
  101.8 0.0 collective-permute-done.2
  101.8 0.6 add_reduce_fusion
  102.4 0.0 collective-permute-done.6.right_ref
  102.4 4.0 %merge.1 = (bf16[1,256,1024]{2,1,0:T(8,128)(2,1)}, bf16[1,256,1024]{2,1,0:T(8,128)(2,1)}, f32[2,256,1024]{2,1,0:T(8,128)}) custom-call(f32[256,1024]{1,0:T(8,128)} %get-tuple-element.50.gk_ref, f32[256,1024]{1,0:T(8,128)} %get-tuple-element.51.gv_ref, bf16[2,128,1024]{2,1,0:T(8,128)(2,1)S(1)} %collective-permute-done.5.left_ref, ...), custom_call_target="tpu_custom_call" | custom-call | flops 8000000000 | bytes 8388608 | tf_op jit(solution)/shard_map/merge/pallas_call | solution.py:554
  106.4 5.0 %all-to-all-done.3 = bf16[64,32,128]{2,1,0:T(8,128)(2,1)S(1)} async-done(((bf16[64,32,128]{2,1,0:T(8,128)(2,1)}), bf16[64,32,128]{2,1,0:T(8,128)(2,1)S(1)}, u32[]{:S(2)}, u32[]{:S(2)}) %all-to-all-start.3) | async-done | bytes 524320 | tf_op jit(solution)/shard_map/all_to_all | solution.py:629
  111.4 3.0 %finish.1 = (bf16[1,256,1024]{2,1,0:T(8,128)(2,1)}, bf16[1,256,1024]{2,1,0:T(8,128)(2,1)}) custom-call(s32[1,64]{1,0:T(1,128)S(1)} %copy-done.3, f32[2,256,1024]{2,1,0:T(8,128)} %get-tuple-element.52.sums_hbm, bf16[8,8,32,128]{3,2,1,0:T(8,128)(2,1)S(1)} %bitcast.4, ...), custom_call_target="tpu_custom_call", output_to_operand_aliasing={{0}: (3, {}), {1}: (4, {})} | custom-call | tf_op jit(solution)/shard_map/finish/pallas_call | solution.py:611
  (18 shorter events, 0.0 us)
Async XLA Ops:
  0.6 35.6 %copy-start.3 = (s32[1,64]{1,0:T(1,128)S(1)}, s32[1,64]{1,0:T(1,128)}, u32[]{:S(2)}) copy-start(s32[1,64]{1,0:T(1,128)} %starts_ref.9) | copy-start | bytes 772
  0.6 42.2 %copy-start.2 = (bf16[1,256,1024]{2,1,0:T(8,128)(2,1)S(1)}, bf16[1,256,1024]{2,1,0:T(8,128)(2,1)}, u32[]{:S(2)}) copy-start(bf16[1,256,1024]{2,1,0:T(8,128)(2,1)} %v_ref.3) | copy-start | bytes 1572868
  0.7 42.2 %copy-start.1 = (bf16[1,256,1024]{2,1,0:T(8,128)(2,1)S(1)}, bf16[1,256,1024]{2,1,0:T(8,128)(2,1)}, u32[]{:S(2)}) copy-start(bf16[1,256,1024]{2,1,0:T(8,128)(2,1)} %k_ref.3) | copy-start | bytes 1572868
  0.7 42.2 %copy-start.5 = (bf16[1,256,1024]{2,1,0:T(8,128)(2,1)S(1)}, bf16[1,256,1024]{2,1,0:T(8,128)(2,1)}, u32[]{:S(2)}) copy-start(bf16[1,256,1024]{2,1,0:T(8,128)(2,1)} %d_ref.7) | copy-start | bytes 1572868
  0.7 42.2 %copy-start.4 = (bf16[1,256,1024]{2,1,0:T(8,128)(2,1)S(1)}, bf16[1,256,1024]{2,1,0:T(8,128)(2,1)}, u32[]{:S(2)}) copy-start(bf16[1,256,1024]{2,1,0:T(8,128)(2,1)} %q_ref.7) | copy-start | bytes 1572868
  0.7 42.2 %copy-start.7 = (f32[8]{0:T(128)S(1)}, f32[8]{0:T(128)}, u32[]{:S(2)}) copy-start(f32[8]{0:T(128)} %bias_ref.5) | copy-start | bytes 100
  0.7 42.2 %copy-start.6 = (s32[1,64]{1,0:T(1,128)S(1)}, s32[1,64]{1,0:T(1,128)}, u32[]{:S(2)}) copy-start(s32[1,64]{1,0:T(1,128)} %lens_ref.1) | copy-start | bytes 772
  3.9 32.4 %all-to-all-start = ((bf16[64,32,128]{2,1,0:T(8,128)(2,1)}), bf16[64,32,128]{2,1,0:T(8,128)(2,1)S(1)}, u32[]{:S(2)}, u32[]{:S(2)}) async-start(bf16[64,32,128]{2,1,0:T(8,128)(2,1)} %bitcast.7), calls=%async_computation | async-start | bytes 1048576 | tf_op jit(solution)/shard_map/all_to_all | solution.py:629
  16.7 26.2 %collective-permute-start = (bf16[2,128,1024]{2,1,0:T(8,128)(2,1)}, bf16[2,128,1024]{2,1,0:T(8,128)(2,1)}, u32[]{:S(2)}, u32[]{:S(2)}) collective-permute-start(bf16[2,128,1024]{2,1,0:T(8,128)(2,1)} %get-tuple-element.32), channel_id=1, source_target_pairs={{0,1},{1,2},{2,3},{3,4},{4,5},{5,6},{6,7},{7,8},{8,9},{9,10},{10,1... | collective-permute-start | bytes 1572872 | tf_op jit(solution)/shard_map/ppermute | solution.py:634
  20.9 21.9 %collective-permute-start.1 = (bf16[2,128,1024]{2,1,0:T(8,128)(2,1)}, bf16[2,128,1024]{2,1,0:T(8,128)(2,1)}, u32[]{:S(2)}, u32[]{:S(2)}) collective-permute-start(bf16[2,128,1024]{2,1,0:T(8,128)(2,1)} %get-tuple-element.33), channel_id=1, source_target_pairs={{1,0},{2,1},{3,2},{4,3},{5,4},{6,5},{7,6},{8,7},{9,8},{10,9},{11,1... | collective-permute-start | bytes 1572872 | tf_op jit(solution)/shard_map/ppermute | solution.py:634
  37.7 21.6 %all-to-all-start.1 = ((bf16[64,32,128]{2,1,0:T(8,128)(2,1)}), bf16[64,32,128]{2,1,0:T(8,128)(2,1)S(1)}, u32[]{:S(2)}, u32[]{:S(2)}) async-start(bf16[64,32,128]{2,1,0:T(8,128)(2,1)} %route.1), calls=%async_computation.1 | async-start | bytes 1048576 | tf_op jit(solution)/shard_map/all_to_all | solution.py:629
  49.1 0.8 copy-start.8
  59.3 2.7 %copy-start = (bf16[64,32,128]{2,1,0:T(8,128)(2,1)}, bf16[64,32,128]{2,1,0:T(8,128)(2,1)S(1)}, u32[]{:S(2)}) copy-start(bf16[64,32,128]{2,1,0:T(8,128)(2,1)S(1)} %all-to-all-done.1) | copy-start | bytes 1572868
  62.0 23.5 %all-to-all-start.2 = ((bf16[64,40,128]{2,1,0:T(8,128)(2,1)}), bf16[64,40,128]{2,1,0:T(8,128)(2,1)S(1)}, u32[]{:S(2)}, u32[]{:S(2)}) async-start(bf16[64,40,128]{2,1,0:T(8,128)(2,1)} %bitcast.2), calls=%async_computation.2 | async-start | bytes 1310720 | tf_op jit(solution)/shard_map/all_to_all | solution.py:629
  77.4 25.0 %collective-permute-start.6 = (bf16[2,128,1024]{2,1,0:T(8,128)(2,1)}, bf16[2,128,1024]{2,1,0:T(8,128)(2,1)S(1)}, u32[]{:S(2)}, u32[]{:S(2)}) collective-permute-start(bf16[2,128,1024]{2,1,0:T(8,128)(2,1)} %get-tuple-element.46), channel_id=1, source_target_pairs={{1,0},{2,1},{3,2},{4,3},{5,4},{6,5},{7,6},{8,7},{9,8},{10,9},{11,1... | collective-permute-start | bytes 1572872 | tf_op jit(solution)/shard_map/ppermute | solution.py:634
  78.7 23.7 %collective-permute-start.5 = (bf16[2,128,1024]{2,1,0:T(8,128)(2,1)S(1)}, bf16[2,128,1024]{2,1,0:T(8,128)(2,1)S(1)}, u32[]{:S(2)}, u32[]{:S(2)}) collective-permute-start(bf16[2,128,1024]{2,1,0:T(8,128)(2,1)S(1)} %get-tuple-element.47), channel_id=1, source_target_pairs={{0,1},{1,2},{2,3},{3,4},{4,5},{5,6},{6,7},{7,8},{8,9},{9,10},{10,1... | collective-permute-start | bytes 1572872 | tf_op jit(solution)/shard_map/ppermute | solution.py:634
  87.2 24.2 %all-to-all-start.3 = ((bf16[64,32,128]{2,1,0:T(8,128)(2,1)}), bf16[64,32,128]{2,1,0:T(8,128)(2,1)S(1)}, u32[]{:S(2)}, u32[]{:S(2)}) async-start(bf16[64,32,128]{2,1,0:T(8,128)(2,1)} %get-tuple-element.53), calls=%async_computation.3 | async-start | bytes 1048576 | tf_op jit(solution)/shard_map/all_to_all | solution.py:629
  96.5 4.8 %collective-permute-start.4 = (f32[8,128]{1,0:T(8,128)S(1)}, f32[8,128]{1,0:T(8,128)S(1)}, u32[]{:S(2)}, u32[]{:S(2)}) collective-permute-start(f32[8,128]{1,0:T(8,128)S(1)} %get-tuple-element.49), channel_id=1, source_target_pairs={{0,192},{64,128},{128,64},{192,0},{1,193},{65,129},{129,65},{193,1... | collective-permute-start | bytes 12296 | tf_op jit(solution)/shard_map/ppermute | solution.py:639
  96.6 5.2 %collective-permute-start.3 = (f32[8,128]{1,0:T(8,128)S(1)}, f32[8,128]{1,0:T(8,128)S(1)}, u32[]{:S(2)}, u32[]{:S(2)}) collective-permute-start(f32[8,128]{1,0:T(8,128)S(1)} %get-tuple-element.49), channel_id=1, source_target_pairs={{0,128},{64,192},{128,0},{192,64},{1,129},{65,193},{129,1},{193,65... | collective-permute-start | bytes 12296 | tf_op jit(solution)/shard_map/ppermute | solution.py:639
  97.4 4.4 %collective-permute-start.2 = (f32[8,128]{1,0:T(8,128)S(1)}, f32[8,128]{1,0:T(8,128)S(1)}, u32[]{:S(2)}, u32[]{:S(2)}) collective-permute-start(f32[8,128]{1,0:T(8,128)S(1)} %get-tuple-element.49), channel_id=1, source_target_pairs={{0,64},{64,0},{128,192},{192,128},{1,65},{65,1},{129,193},{193,129... | collective-permute-start | bytes 12296 | tf_op jit(solution)/shard_map/ppermute | solution.py:639

commit v6 on v5

--- a/solution.py
+++ b/solution.py
@@ -101,9 +101,12 @@
         stores[2 * part].start()
         stores[2 * part + 1].start()
         here = pl.ds(part * BAND, BAND)
-        for head in range(HEADS):
-            rows = nn(pick, ref[:, columns(head)]).astype(jnp.bfloat16)
-            out_ref[:, head, here, :] = rows.reshape(BANDS, BAND, HD)
+        for first in range(0, HEADS, GROUP):
+            cols = slice(first * HD, (first + GROUP) * HD)
+            rows = nn(pick, ref[:, cols]).astype(jnp.bfloat16)
+            for member in range(GROUP):
+                piece = rows[:, columns(member)].reshape(BANDS, BAND, HD)
+                out_ref[:, first + member, here, :] = piece
         store = pltpu.make_async_copy(
             out_ref.at[:, :, here, :], out_hbm.at[:, :, here, :], out_sems.at[part]
         )
@@ -667,7 +670,6 @@
     owned, sums = gather(starts, held)
     returned = exchange(owned).reshape(BANDS, HEADS, 2 * BAND, HD)
     grad_bias = jnp.sum(summed(sums, "dp", 1, 2), axis=1)
-    gk, grad_bias = lax.optimization_barrier((gk, grad_bias))
     outk, outv, both = merge(gk, gv, left, right)
     grad_k, grad_v = finish(starts, outk, outv, both, returned)
     return attended, grad_q, grad_k, grad_v, grad_bias

time: 115 us -> 116 us (level)
    all_to_all x4, waiting for transfers between devices: 30.6 us -> 33.5 us  [exchange(): return lax.all_to_all(pieces, 'ctx', 0, 0, tiled=True)]
    ppermute x3, waiting for transfers between devices: 1.85 us -> 0.01 us  [partners(): lax.ppermute(x, axis, [(i, i ^ step) for i in range(peers)])]
  transfers between devices with their start and end apart: 11 -> 11, of which waited for: 6 -> 4; matrix products, arithmetic and copies ran while one was open for 1% -> 1% of each run, Pallas kernels for 21% -> 20%
where the time goes in v6:
time: 116 us; the launch traced here: 115 us
  starting transfers between devices  47 us (41%)
  waiting for transfers between devices  33.5 us (29%)
  Pallas kernels  32.3 us (28%)
    all_to_all x4, waiting for transfers between devices, exchange(): return lax.all_to_all(pieces, 'ctx', 0, 0, tiled=True)  33.5 us
    all_to_all x4, starting transfers between devices, exchange(): return lax.all_to_all(pieces, 'ctx', 0, 0, tiled=True)  33.2 us
    ppermute x4, starting transfers between devices, shifted(): lax.ppermute(x, 'ctx', [(i, i + by) for i in range(peers) if 0 <= i + by...  10.4 us
    pallas_call x1, Pallas kernels, own_part(): pl.pallas_call(own_kernel, grid=(HEADS // GROUP,), out_shape=(low_array(1...  6.91 us
    pallas_call x1, Pallas kernels, window(): pl.pallas_call(window_kernel, grid=(HEADS,), out_shape=(float_array(HEADS...  6.19 us
    pallas_call x1, Pallas kernels, merge(): pl.pallas_call(merge_kernel, grid=(HEADS // GROUP,), out_shape=(low_array...  4 us
    ppermute x3, starting transfers between devices, partners(): lax.ppermute(x, axis, [(i, i ^ step) for i in range(peers)])  3.44 us
    pallas_call x1, Pallas kernels, halo_grads(): pl.pallas_call(halo_kernel, out_shape=(low_array(2, HW, WIDTH), low_array...  3.29 us
  transfers between devices with their start and end apart: 11, of which 4 were waited for; matrix products, arithmetic and copies ran while one was open for 1% of the time, Pallas kernels for 20%

profile of v6, /device:TPU:4, one launch (start us, length us, event | category | flops | bytes accessed | tf_op | source)
XLA Modules:
  0.0 115.1 jit_solution(7717339226979482235)
XLA Ops:
  0.6 0.0 copy-start.2
  0.7 3.1 %cut_prompt.1 = (bf16[8,8,32,128]{3,2,1,0:T(8,128)(2,1)}, bf16[2,128,1024]{2,1,0:T(8,128)(2,1)}, bf16[2,128,1024]{2,1,0:T(8,128)(2,1)}) custom-call(s32[1,64]{1,0:T(1,128)} %starts_ref.9, bf16[1,256,1024]{2,1,0:T(8,128)(2,1)} %k_ref.3, bf16[1,256,1024]{2,1,0:T(8,128)(2,1)} %v_ref.3), custom_call_target="tpu_custom_call" | custom-call | tf_op jit(solution)/shard_map/cut_prompt/pallas_call | solution.py:120
  3.8 12.8 %all-to-all-start = ((bf16[64,32,128]{2,1,0:T(8,128)(2,1)}), bf16[64,32,128]{2,1,0:T(8,128)(2,1)S(1)}, u32[]{:S(2)}, u32[]{:S(2)}) async-start(bf16[64,32,128]{2,1,0:T(8,128)(2,1)} %bitcast.7), calls=%async_computation | async-start | bytes 1048576 | tf_op jit(solution)/shard_map/all_to_all | solution.py:632
  16.6 4.3 %collective-permute-start = (bf16[2,128,1024]{2,1,0:T(8,128)(2,1)}, bf16[2,128,1024]{2,1,0:T(8,128)(2,1)}, u32[]{:S(2)}, u32[]{:S(2)}) collective-permute-start(bf16[2,128,1024]{2,1,0:T(8,128)(2,1)} %get-tuple-element.30), channel_id=1, source_target_pairs={{0,1},{1,2},{2,3},{3,4},{4,5},{5,6},{6,7},{7,8},{8,9},{9,10},{10,1... | collective-permute-start | bytes 1572872 | tf_op jit(solution)/shard_map/ppermute | solution.py:637
  20.9 1.3 %collective-permute-start.1 = (bf16[2,128,1024]{2,1,0:T(8,128)(2,1)}, bf16[2,128,1024]{2,1,0:T(8,128)(2,1)}, u32[]{:S(2)}, u32[]{:S(2)}) collective-permute-start(bf16[2,128,1024]{2,1,0:T(8,128)(2,1)} %get-tuple-element.31), channel_id=1, source_target_pairs={{1,0},{2,1},{3,2},{4,3},{5,4},{6,5},{7,6},{8,7},{9,8},{10,9},{11,1... | collective-permute-start | bytes 1572872 | tf_op jit(solution)/shard_map/ppermute | solution.py:637
  22.2 14.0 %all-to-all-done.in_ref = bf16[64,32,128]{2,1,0:T(8,128)(2,1)S(1)} async-done(((bf16[64,32,128]{2,1,0:T(8,128)(2,1)}), bf16[64,32,128]{2,1,0:T(8,128)(2,1)S(1)}, u32[]{:S(2)}, u32[]{:S(2)}) %all-to-all-start) | async-done | bytes 524320 | tf_op jit(solution)/shard_map/all_to_all | solution.py:632
  36.2 1.5 %route.1 = bf16[64,32,128]{2,1,0:T(8,128)(2,1)} custom-call(s32[1,64]{1,0:T(1,128)S(1)} %copy-done.3, bf16[64,32,128]{2,1,0:T(8,128)(2,1)S(1)} %all-to-all-done.in_ref), custom_call_target="tpu_custom_call" | custom-call | tf_op jit(solution)/shard_map/route/pallas_call | solution.py:153
  37.7 5.1 %all-to-all-start.1 = ((bf16[64,32,128]{2,1,0:T(8,128)(2,1)}), bf16[64,32,128]{2,1,0:T(8,128)(2,1)S(1)}, u32[]{:S(2)}, u32[]{:S(2)}) async-start(bf16[64,32,128]{2,1,0:T(8,128)(2,1)} %route.1), calls=%async_computation.1 | async-start | bytes 1048576 | tf_op jit(solution)/shard_map/all_to_all | solution.py:632
  42.8 0.0 collective-permute-done.low_ref
  42.8 6.2 %window.1 = (f32[8,8,256]{2,1,0:T(8,128)S(1)}, f32[2,256,256]{2,1,0:T(8,128)S(1)}, f32[2,128,128]{2,1,0:T(8,128)S(1)}, f32[128,256]{1,0:T(8,128)S(1)}) custom-call(s32[1,64]{1,0:T(1,128)S(1)} %copy-done.3, s32[1,64]{1,0:T(1,128)S(1)} %copy-done.6, f32[8]{0:T(128)S(1)} %copy-done.7, bf16[1,256,1024]{2,1,0:T(8,128)(2,1)S(1)} %copy-done.4, ...), custom_call_target="tpu_custom_call" | custom-call | flops 20000000000 | bytes 8388608 | tf_op jit(solution)/shard_map/window/pallas_call | solution.py:320
  49.0 0.0 copy-start.8
  49.1 0.8 copy-done.8
  49.8 9.3 %all-to-all-done.1 = bf16[64,32,128]{2,1,0:T(8,128)(2,1)S(1)} async-done(((bf16[64,32,128]{2,1,0:T(8,128)(2,1)}), bf16[64,32,128]{2,1,0:T(8,128)(2,1)S(1)}, u32[]{:S(2)}, u32[]{:S(2)}) %all-to-all-start.1) | async-done | bytes 524320 | tf_op jit(solution)/shard_map/all_to_all | solution.py:632
  59.2 2.7 %prompt_part.1 = (bf16[8,8,40,128]{3,2,1,0:T(8,128)(2,1)}, f32[8,8,256]{2,1,0:T(8,128)S(1)}) custom-call(f32[8]{0:T(128)S(1)} %copy-done.7, bf16[1,256,1024]{2,1,0:T(8,128)(2,1)S(1)} %copy-done.4, bf16[1,256,1024]{2,1,0:T(8,128)(2,1)S(1)} %copy-done.5, bf16[8,8,32,128]{3,2,1,0:T(8,128)(2,1)S(1)} %bitcast.5, f32[8,8,256]{2,1,0:T(8,128)S(1)} %get-tuple-element.33.stats_ref, ...), custom_call_target="tpu_custom_call" | custom-call | flops 4000000000 | bytes 8388608 | tf_op jit(solution)/shard_map/prompt_part/pallas_call | solution.py:392
  61.9 5.2 %all-to-all-start.2 = ((bf16[64,40,128]{2,1,0:T(8,128)(2,1)}), bf16[64,40,128]{2,1,0:T(8,128)(2,1)S(1)}, u32[]{:S(2)}, u32[]{:S(2)}) async-start(bf16[64,40,128]{2,1,0:T(8,128)(2,1)} %bitcast.2), calls=%async_computation.2 | async-start | bytes 1310720 | tf_op jit(solution)/shard_map/all_to_all | solution.py:632
  67.1 6.9 %own_part.1 = (bf16[1,256,1024]{2,1,0:T(8,128)(2,1)}, bf16[1,256,1024]{2,1,0:T(8,128)(2,1)}, f32[256,1024]{1,0:T(8,128)}, f32[256,1024]{1,0:T(8,128)}) custom-call(f32[8]{0:T(128)S(1)} %copy-done.7, bf16[1,256,1024]{2,1,0:T(8,128)(2,1)S(1)} %copy-done.4, bf16[1,256,1024]{2,1,0:T(8,128)(2,1)S(1)} %copy-done.5, bf16[1,256,1024]{2,1,0:T(8,128)(2,1)S(1)} %copy-done.1, ...), custom_call_target="tpu_custom_call" | custom-call | flops 10000000000 | bytes 8388608 | tf_op jit(solution)/shard_map/own_part/pallas_call | solution.py:525
  74.0 3.3 %halo_grads.1 = (bf16[2,128,1024]{2,1,0:T(8,128)(2,1)S(1)}, bf16[2,128,1024]{2,1,0:T(8,128)(2,1)}) custom-call(bf16[1,256,1024]{2,1,0:T(8,128)(2,1)S(1)} %copy-done.4, bf16[1,256,1024]{2,1,0:T(8,128)(2,1)S(1)} %copy-done.5, bf16[2,128,1024]{2,1,0:T(8,128)(2,1)} %collective-permute-done.low_ref, bf16[2,128,1024]{2,1,0:T(8,128)(2,1)} %collective-permute-done.1.high_ref, ...), custom_call_target="tpu_custom_call" | custom-call | flops 4000000000 | bytes 8388608 | tf_op jit(solution)/shard_map/halo_grads/pallas_call | solution.py:445
  77.3 3.5 %collective-permute-start.2 = (bf16[2,128,1024]{2,1,0:T(8,128)(2,1)}, bf16[2,128,1024]{2,1,0:T(8,128)(2,1)S(1)}, u32[]{:S(2)}, u32[]{:S(2)}) collective-permute-start(bf16[2,128,1024]{2,1,0:T(8,128)(2,1)} %get-tuple-element.44), channel_id=1, source_target_pairs={{0,1},{1,2},{2,3},{3,4},{4,5},{5,6},{6,7},{7,8},{8,9},{9,10},{10,1... | collective-permute-start | bytes 1572872 | tf_op jit(solution)/shard_map/ppermute | solution.py:637
  80.8 1.3 %collective-permute-start.3 = (bf16[2,128,1024]{2,1,0:T(8,128)(2,1)S(1)}, bf16[2,128,1024]{2,1,0:T(8,128)(2,1)S(1)}, u32[]{:S(2)}, u32[]{:S(2)}) collective-permute-start(bf16[2,128,1024]{2,1,0:T(8,128)(2,1)S(1)} %get-tuple-element.45), channel_id=1, source_target_pairs={{1,0},{2,1},{3,2},{4,3},{5,4},{6,5},{7,6},{8,7},{9,8},{10,9},{11,1... | collective-permute-start | bytes 1572872 | tf_op jit(solution)/shard_map/ppermute | solution.py:637
  82.1 3.3 %all-to-all-done.2.in_ref = bf16[64,40,128]{2,1,0:T(8,128)(2,1)S(1)} async-done(((bf16[64,40,128]{2,1,0:T(8,128)(2,1)}), bf16[64,40,128]{2,1,0:T(8,128)(2,1)S(1)}, u32[]{:S(2)}, u32[]{:S(2)}) %all-to-all-start.2) | async-done | bytes 655392 | tf_op jit(solution)/shard_map/all_to_all | solution.py:632
  85.4 1.6 %gather.1 = (bf16[64,32,128]{2,1,0:T(8,128)(2,1)}, f32[8,128]{1,0:T(8,128)S(1)}) custom-call(s32[1,64]{1,0:T(1,128)S(1)} %copy-done.3, bf16[64,40,128]{2,1,0:T(8,128)(2,1)S(1)} %all-to-all-done.2.in_ref), custom_call_target="tpu_custom_call" | custom-call | tf_op jit(solution)/shard_map/gather/pallas_call | solution.py:182
  87.1 10.2 %all-to-all-start.3 = ((bf16[64,32,128]{2,1,0:T(8,128)(2,1)}), bf16[64,32,128]{2,1,0:T(8,128)(2,1)S(1)}, u32[]{:S(2)}, u32[]{:S(2)}) async-start(bf16[64,32,128]{2,1,0:T(8,128)(2,1)} %get-tuple-element.49), calls=%async_computation.3 | async-start | bytes 1048576 | tf_op jit(solution)/shard_map/all_to_all | solution.py:632
  97.2 0.1 collective-permute-start.6
  97.3 0.9 collective-permute-start.5
  98.2 2.5 %collective-permute-start.4 = (f32[8,128]{1,0:T(8,128)S(1)}, f32[8,128]{1,0:T(8,128)S(1)}, u32[]{:S(2)}, u32[]{:S(2)}) collective-permute-start(f32[8,128]{1,0:T(8,128)S(1)} %get-tuple-element.54), channel_id=1, source_target_pairs={{0,64},{64,0},{128,192},{192,128},{1,65},{65,1},{129,193},{193,129... | collective-permute-start | bytes 12296 | tf_op jit(solution)/shard_map/ppermute | solution.py:642
  100.7 0.0 collective-permute-done.2.left_ref
  100.7 0.0 collective-permute-done.3.right_ref
  100.7 4.0 %merge.1 = (bf16[1,256,1024]{2,1,0:T(8,128)(2,1)}, bf16[1,256,1024]{2,1,0:T(8,128)(2,1)}, f32[2,256,1024]{2,1,0:T(8,128)}) custom-call(f32[256,1024]{1,0:T(8,128)} %get-tuple-element.41.gk_ref, f32[256,1024]{1,0:T(8,128)} %get-tuple-element.42.gv_ref, bf16[2,128,1024]{2,1,0:T(8,128)(2,1)S(1)} %collective-permute-done.2.left_ref, ...), custom_call_target="tpu_custom_call" | custom-call | flops 8000000000 | bytes 8388608 | tf_op jit(solution)/shard_map/merge/pallas_call | solution.py:557
  104.7 0.0 collective-permute-done.6
  104.7 0.6 add_reduce_fusion
  105.4 6.8 %all-to-all-done.3 = bf16[64,32,128]{2,1,0:T(8,128)(2,1)S(1)} async-done(((bf16[64,32,128]{2,1,0:T(8,128)(2,1)}), bf16[64,32,128]{2,1,0:T(8,128)(2,1)S(1)}, u32[]{:S(2)}, u32[]{:S(2)}) %all-to-all-start.3) | async-done | bytes 524320 | tf_op jit(solution)/shard_map/all_to_all | solution.py:632
  112.1 3.0 %finish.1 = (bf16[1,256,1024]{2,1,0:T(8,128)(2,1)}, bf16[1,256,1024]{2,1,0:T(8,128)(2,1)}) custom-call(s32[1,64]{1,0:T(1,128)S(1)} %copy-done.3, f32[2,256,1024]{2,1,0:T(8,128)} %get-tuple-element.46.sums_hbm, bf16[8,8,32,128]{3,2,1,0:T(8,128)(2,1)S(1)} %bitcast.4, ...), custom_call_target="tpu_custom_call", output_to_operand_aliasing={{0}: (3, {}), {1}: (4, {})} | custom-call | tf_op jit(solution)/shard_map/finish/pallas_call | solution.py:614
  (18 shorter events, 0.0 us)
Async XLA Ops:
  0.6 35.6 %copy-start.3 = (s32[1,64]{1,0:T(1,128)S(1)}, s32[1,64]{1,0:T(1,128)}, u32[]{:S(2)}) copy-start(s32[1,64]{1,0:T(1,128)} %starts_ref.9) | copy-start | bytes 772
  0.6 42.1 %copy-start.2 = (bf16[1,256,1024]{2,1,0:T(8,128)(2,1)S(1)}, bf16[1,256,1024]{2,1,0:T(8,128)(2,1)}, u32[]{:S(2)}) copy-start(bf16[1,256,1024]{2,1,0:T(8,128)(2,1)} %v_ref.3) | copy-start | bytes 1572868
  0.7 42.1 %copy-start.1 = (bf16[1,256,1024]{2,1,0:T(8,128)(2,1)S(1)}, bf16[1,256,1024]{2,1,0:T(8,128)(2,1)}, u32[]{:S(2)}) copy-start(bf16[1,256,1024]{2,1,0:T(8,128)(2,1)} %k_ref.3) | copy-start | bytes 1572868
  0.7 42.1 %copy-start.5 = (bf16[1,256,1024]{2,1,0:T(8,128)(2,1)S(1)}, bf16[1,256,1024]{2,1,0:T(8,128)(2,1)}, u32[]{:S(2)}) copy-start(bf16[1,256,1024]{2,1,0:T(8,128)(2,1)} %d_ref.7) | copy-start | bytes 1572868
  0.7 42.1 %copy-start.4 = (bf16[1,256,1024]{2,1,0:T(8,128)(2,1)S(1)}, bf16[1,256,1024]{2,1,0:T(8,128)(2,1)}, u32[]{:S(2)}) copy-start(bf16[1,256,1024]{2,1,0:T(8,128)(2,1)} %q_ref.7) | copy-start | bytes 1572868
  0.7 42.1 %copy-start.7 = (f32[8]{0:T(128)S(1)}, f32[8]{0:T(128)}, u32[]{:S(2)}) copy-start(f32[8]{0:T(128)} %bias_ref.5) | copy-start | bytes 100
  0.7 42.1 %copy-start.6 = (s32[1,64]{1,0:T(1,128)S(1)}, s32[1,64]{1,0:T(1,128)}, u32[]{:S(2)}) copy-start(s32[1,64]{1,0:T(1,128)} %lens_ref.1) | copy-start | bytes 772
  3.8 32.4 %all-to-all-start = ((bf16[64,32,128]{2,1,0:T(8,128)(2,1)}), bf16[64,32,128]{2,1,0:T(8,128)(2,1)S(1)}, u32[]{:S(2)}, u32[]{:S(2)}) async-start(bf16[64,32,128]{2,1,0:T(8,128)(2,1)} %bitcast.7), calls=%async_computation | async-start | bytes 1048576 | tf_op jit(solution)/shard_map/all_to_all | solution.py:632
  16.6 26.2 %collective-permute-start = (bf16[2,128,1024]{2,1,0:T(8,128)(2,1)}, bf16[2,128,1024]{2,1,0:T(8,128)(2,1)}, u32[]{:S(2)}, u32[]{:S(2)}) collective-permute-start(bf16[2,128,1024]{2,1,0:T(8,128)(2,1)} %get-tuple-element.30), channel_id=1, source_target_pairs={{0,1},{1,2},{2,3},{3,4},{4,5},{5,6},{6,7},{7,8},{8,9},{9,10},{10,1... | collective-permute-start | bytes 1572872 | tf_op jit(solution)/shard_map/ppermute | solution.py:637
  20.9 21.9 %collective-permute-start.1 = (bf16[2,128,1024]{2,1,0:T(8,128)(2,1)}, bf16[2,128,1024]{2,1,0:T(8,128)(2,1)}, u32[]{:S(2)}, u32[]{:S(2)}) collective-permute-start(bf16[2,128,1024]{2,1,0:T(8,128)(2,1)} %get-tuple-element.31), channel_id=1, source_target_pairs={{1,0},{2,1},{3,2},{4,3},{5,4},{6,5},{7,6},{8,7},{9,8},{10,9},{11,1... | collective-permute-start | bytes 1572872 | tf_op jit(solution)/shard_map/ppermute | solution.py:637
  37.7 21.5 %all-to-all-start.1 = ((bf16[64,32,128]{2,1,0:T(8,128)(2,1)}), bf16[64,32,128]{2,1,0:T(8,128)(2,1)S(1)}, u32[]{:S(2)}, u32[]{:S(2)}) async-start(bf16[64,32,128]{2,1,0:T(8,128)(2,1)} %route.1), calls=%async_computation.1 | async-start | bytes 1048576 | tf_op jit(solution)/shard_map/all_to_all | solution.py:632
  49.0 0.8 copy-start.8
  59.2 2.7 %copy-start = (bf16[64,32,128]{2,1,0:T(8,128)(2,1)}, bf16[64,32,128]{2,1,0:T(8,128)(2,1)S(1)}, u32[]{:S(2)}) copy-start(bf16[64,32,128]{2,1,0:T(8,128)(2,1)S(1)} %all-to-all-done.1) | copy-start | bytes 1572868
  61.9 23.5 %all-to-all-start.2 = ((bf16[64,40,128]{2,1,0:T(8,128)(2,1)}), bf16[64,40,128]{2,1,0:T(8,128)(2,1)S(1)}, u32[]{:S(2)}, u32[]{:S(2)}) async-start(bf16[64,40,128]{2,1,0:T(8,128)(2,1)} %bitcast.2), calls=%async_computation.2 | async-start | bytes 1310720 | tf_op jit(solution)/shard_map/all_to_all | solution.py:632
  77.3 23.4 %collective-permute-start.2 = (bf16[2,128,1024]{2,1,0:T(8,128)(2,1)}, bf16[2,128,1024]{2,1,0:T(8,128)(2,1)S(1)}, u32[]{:S(2)}, u32[]{:S(2)}) collective-permute-start(bf16[2,128,1024]{2,1,0:T(8,128)(2,1)} %get-tuple-element.44), channel_id=1, source_target_pairs={{0,1},{1,2},{2,3},{3,4},{4,5},{5,6},{6,7},{7,8},{8,9},{9,10},{10,1... | collective-permute-start | bytes 1572872 | tf_op jit(solution)/shard_map/ppermute | solution.py:637
  80.8 19.9 %collective-permute-start.3 = (bf16[2,128,1024]{2,1,0:T(8,128)(2,1)S(1)}, bf16[2,128,1024]{2,1,0:T(8,128)(2,1)S(1)}, u32[]{:S(2)}, u32[]{:S(2)}) collective-permute-start(bf16[2,128,1024]{2,1,0:T(8,128)(2,1)S(1)} %get-tuple-element.45), channel_id=1, source_target_pairs={{1,0},{2,1},{3,2},{4,3},{5,4},{6,5},{7,6},{8,7},{9,8},{10,9},{11,1... | collective-permute-start | bytes 1572872 | tf_op jit(solution)/shard_map/ppermute | solution.py:637
  87.1 25.1 %all-to-all-start.3 = ((bf16[64,32,128]{2,1,0:T(8,128)(2,1)}), bf16[64,32,128]{2,1,0:T(8,128)(2,1)S(1)}, u32[]{:S(2)}, u32[]{:S(2)}) async-start(bf16[64,32,128]{2,1,0:T(8,128)(2,1)} %get-tuple-element.49), calls=%async_computation.3 | async-start | bytes 1048576 | tf_op jit(solution)/shard_map/all_to_all | solution.py:632
  97.2 7.5 %collective-permute-start.6 = (f32[8,128]{1,0:T(8,128)S(1)}, f32[8,128]{1,0:T(8,128)S(1)}, u32[]{:S(2)}, u32[]{:S(2)}) collective-permute-start(f32[8,128]{1,0:T(8,128)S(1)} %get-tuple-element.54), channel_id=1, source_target_pairs={{0,192},{64,128},{128,64},{192,0},{1,193},{65,129},{129,65},{193,1... | collective-permute-start | bytes 12296 | tf_op jit(solution)/shard_map/ppermute | solution.py:642
  97.3 7.4 %collective-permute-start.5 = (f32[8,128]{1,0:T(8,128)S(1)}, f32[8,128]{1,0:T(8,128)S(1)}, u32[]{:S(2)}, u32[]{:S(2)}) collective-permute-start(f32[8,128]{1,0:T(8,128)S(1)} %get-tuple-element.54), channel_id=1, source_target_pairs={{0,128},{64,192},{128,0},{192,64},{1,129},{65,193},{129,1},{193,65... | collective-permute-start | bytes 12296 | tf_op jit(solution)/shard_map/ppermute | solution.py:642
  98.2 6.5 %collective-permute-start.4 = (f32[8,128]{1,0:T(8,128)S(1)}, f32[8,128]{1,0:T(8,128)S(1)}, u32[]{:S(2)}, u32[]{:S(2)}) collective-permute-start(f32[8,128]{1,0:T(8,128)S(1)} %get-tuple-element.54), channel_id=1, source_target_pairs={{0,64},{64,0},{128,192},{192,128},{1,65},{65,1},{129,193},{193,129... | collective-permute-start | bytes 12296 | tf_op jit(solution)/shard_map/ppermute | solution.py:642

commit v7 on v6

--- a/solution.py
+++ b/solution.py
@@ -540,7 +540,7 @@
     )(bias, queries, cotangent, key_rows, values, low, high, prompt, final, *masks)
 
 
-def merge_kernel(gk_ref, gv_ref, left_ref, right_ref, outk_ref, outv_ref, sums_ref):
+def merge_kernel(right_ref, left_ref, gk_ref, gv_ref, outk_ref, outv_ref, sums_ref):
     for part, (ref, out) in enumerate(((gk_ref, outk_ref), (gv_ref, outv_ref))):
         for half, side in enumerate((left_ref, right_ref)):
             rows = slice(half * HW, (half + 1) * HW)
@@ -558,12 +558,12 @@
         merge_kernel,
         grid=(HEADS // GROUP,),
         out_shape=(low_array(1, ROWS, WIDTH),) * 2 + (float_array(2, ROWS, WIDTH),),
-        in_specs=[total, total, side, side],
+        in_specs=[side, side, total, total],
         out_specs=(rows, rows, both),
         compiler_params=NEARLY,
         cost_estimate=cost(MERGE),
         name="merge",
-    )(gk, gv, left, right)
+    )(right, left, gk, gv)
 
 
 def finish_kernel(

time: 116 us -> 115 us (level)
  transfers between devices with their start and end apart: 11 -> 11, of which waited for: 4 -> 4; matrix products, arithmetic and copies ran while one was open for 1% -> 1% of each run, Pallas kernels for 20% -> 21%
where the time goes in v7:
time: 115 us; the launch traced here: 114 us
  starting transfers between devices  47.2 us (41%)
  waiting for transfers between devices  32.4 us (28%)
  Pallas kernels  32.3 us (28%)
    all_to_all x4, waiting for transfers between devices, exchange(): return lax.all_to_all(pieces, 'ctx', 0, 0, tiled=True)  32.3 us
    all_to_all x4, starting transfers between devices, exchange(): return lax.all_to_all(pieces, 'ctx', 0, 0, tiled=True)  32.3 us
    ppermute x4, starting transfers between devices, shifted(): lax.ppermute(x, 'ctx', [(i, i + by) for i in range(peers) if 0 <= i + by...  11.4 us
    pallas_call x1, Pallas kernels, own_part(): pl.pallas_call(own_kernel, grid=(HEADS // GROUP,), out_shape=(low_array(1...  6.91 us
    pallas_call x1, Pallas kernels, window(): pl.pallas_call(window_kernel, grid=(HEADS,), out_shape=(float_array(HEADS...  6.19 us
    pallas_call x1, Pallas kernels, merge(): pl.pallas_call(merge_kernel, grid=(HEADS // GROUP,), out_shape=(low_array...  4.08 us
    ppermute x3, starting transfers between devices, partners(): lax.ppermute(x, axis, [(i, i ^ step) for i in range(peers)])  3.44 us
    pallas_call x1, Pallas kernels, halo_grads(): pl.pallas_call(halo_kernel, out_shape=(low_array(2, HW, WIDTH), low_array...  3.27 us
  transfers between devices with their start and end apart: 11, of which 4 were waited for; matrix products, arithmetic and copies ran while one was open for 1% of the time, Pallas kernels for 21%

profile of v7, /device:TPU:4, one launch (start us, length us, event | category | flops | bytes accessed | tf_op | source)
XLA Modules:
  0.0 114.2 jit_solution(9078852096437170255)
XLA Ops:
  0.6 0.0 copy-start.2
  0.7 3.1 %cut_prompt.1 = (bf16[8,8,32,128]{3,2,1,0:T(8,128)(2,1)}, bf16[2,128,1024]{2,1,0:T(8,128)(2,1)}, bf16[2,128,1024]{2,1,0:T(8,128)(2,1)}) custom-call(s32[1,64]{1,0:T(1,128)} %starts_ref.9, bf16[1,256,1024]{2,1,0:T(8,128)(2,1)} %k_ref.3, bf16[1,256,1024]{2,1,0:T(8,128)(2,1)} %v_ref.3), custom_call_target="tpu_custom_call" | custom-call | tf_op jit(solution)/shard_map/cut_prompt/pallas_call | solution.py:120
  3.8 12.8 %all-to-all-start = ((bf16[64,32,128]{2,1,0:T(8,128)(2,1)}), bf16[64,32,128]{2,1,0:T(8,128)(2,1)S(1)}, u32[]{:S(2)}, u32[]{:S(2)}) async-start(bf16[64,32,128]{2,1,0:T(8,128)(2,1)} %bitcast.7), calls=%async_computation | async-start | bytes 1048576 | tf_op jit(solution)/shard_map/all_to_all | solution.py:632
  16.6 4.3 %collective-permute-start = (bf16[2,128,1024]{2,1,0:T(8,128)(2,1)}, bf16[2,128,1024]{2,1,0:T(8,128)(2,1)}, u32[]{:S(2)}, u32[]{:S(2)}) collective-permute-start(bf16[2,128,1024]{2,1,0:T(8,128)(2,1)} %get-tuple-element.30), channel_id=1, source_target_pairs={{0,1},{1,2},{2,3},{3,4},{4,5},{5,6},{6,7},{7,8},{8,9},{9,10},{10,1... | collective-permute-start | bytes 1572872 | tf_op jit(solution)/shard_map/ppermute | solution.py:637
  20.9 1.3 %collective-permute-start.1 = (bf16[2,128,1024]{2,1,0:T(8,128)(2,1)}, bf16[2,128,1024]{2,1,0:T(8,128)(2,1)}, u32[]{:S(2)}, u32[]{:S(2)}) collective-permute-start(bf16[2,128,1024]{2,1,0:T(8,128)(2,1)} %get-tuple-element.31), channel_id=1, source_target_pairs={{1,0},{2,1},{3,2},{4,3},{5,4},{6,5},{7,6},{8,7},{9,8},{10,9},{11,1... | collective-permute-start | bytes 1572872 | tf_op jit(solution)/shard_map/ppermute | solution.py:637
  22.2 14.0 %all-to-all-done.in_ref = bf16[64,32,128]{2,1,0:T(8,128)(2,1)S(1)} async-done(((bf16[64,32,128]{2,1,0:T(8,128)(2,1)}), bf16[64,32,128]{2,1,0:T(8,128)(2,1)S(1)}, u32[]{:S(2)}, u32[]{:S(2)}) %all-to-all-start) | async-done | bytes 524320 | tf_op jit(solution)/shard_map/all_to_all | solution.py:632
  36.2 1.5 %route.1 = bf16[64,32,128]{2,1,0:T(8,128)(2,1)} custom-call(s32[1,64]{1,0:T(1,128)S(1)} %copy-done.3, bf16[64,32,128]{2,1,0:T(8,128)(2,1)S(1)} %all-to-all-done.in_ref), custom_call_target="tpu_custom_call" | custom-call | tf_op jit(solution)/shard_map/route/pallas_call | solution.py:153
  37.7 5.1 %all-to-all-start.1 = ((bf16[64,32,128]{2,1,0:T(8,128)(2,1)}), bf16[64,32,128]{2,1,0:T(8,128)(2,1)S(1)}, u32[]{:S(2)}, u32[]{:S(2)}) async-start(bf16[64,32,128]{2,1,0:T(8,128)(2,1)} %route.1), calls=%async_computation.1 | async-start | bytes 1048576 | tf_op jit(solution)/shard_map/all_to_all | solution.py:632
  42.8 0.0 collective-permute-done.1.high_ref
  42.8 6.2 %window.1 = (f32[8,8,256]{2,1,0:T(8,128)S(1)}, f32[2,256,256]{2,1,0:T(8,128)S(1)}, f32[2,128,128]{2,1,0:T(8,128)S(1)}, f32[128,256]{1,0:T(8,128)S(1)}) custom-call(s32[1,64]{1,0:T(1,128)S(1)} %copy-done.3, s32[1,64]{1,0:T(1,128)S(1)} %copy-done.6, f32[8]{0:T(128)S(1)} %copy-done.7, bf16[1,256,1024]{2,1,0:T(8,128)(2,1)S(1)} %copy-done.4, ...), custom_call_target="tpu_custom_call" | custom-call | flops 20000000000 | bytes 8388608 | tf_op jit(solution)/shard_map/window/pallas_call | solution.py:320
  49.0 0.0 copy-start.8
  49.1 0.8 copy-done.8
  49.8 9.3 %all-to-all-done.1 = bf16[64,32,128]{2,1,0:T(8,128)(2,1)S(1)} async-done(((bf16[64,32,128]{2,1,0:T(8,128)(2,1)}), bf16[64,32,128]{2,1,0:T(8,128)(2,1)S(1)}, u32[]{:S(2)}, u32[]{:S(2)}) %all-to-all-start.1) | async-done | bytes 524320 | tf_op jit(solution)/shard_map/all_to_all | solution.py:632
  59.2 2.7 %prompt_part.1 = (bf16[8,8,40,128]{3,2,1,0:T(8,128)(2,1)}, f32[8,8,256]{2,1,0:T(8,128)S(1)}) custom-call(f32[8]{0:T(128)S(1)} %copy-done.7, bf16[1,256,1024]{2,1,0:T(8,128)(2,1)S(1)} %copy-done.4, bf16[1,256,1024]{2,1,0:T(8,128)(2,1)S(1)} %copy-done.5, bf16[8,8,32,128]{3,2,1,0:T(8,128)(2,1)S(1)} %bitcast.5, f32[8,8,256]{2,1,0:T(8,128)S(1)} %get-tuple-element.33.stats_ref, ...), custom_call_target="tpu_custom_call" | custom-call | flops 4000000000 | bytes 8388608 | tf_op jit(solution)/shard_map/prompt_part/pallas_call | solution.py:392
  61.9 5.2 %all-to-all-start.2 = ((bf16[64,40,128]{2,1,0:T(8,128)(2,1)}), bf16[64,40,128]{2,1,0:T(8,128)(2,1)S(1)}, u32[]{:S(2)}, u32[]{:S(2)}) async-start(bf16[64,40,128]{2,1,0:T(8,128)(2,1)} %bitcast.2), calls=%async_computation.2 | async-start | bytes 1310720 | tf_op jit(solution)/shard_map/all_to_all | solution.py:632
  67.1 6.9 %own_part.1 = (bf16[1,256,1024]{2,1,0:T(8,128)(2,1)}, bf16[1,256,1024]{2,1,0:T(8,128)(2,1)}, f32[256,1024]{1,0:T(8,128)}, f32[256,1024]{1,0:T(8,128)}) custom-call(f32[8]{0:T(128)S(1)} %copy-done.7, bf16[1,256,1024]{2,1,0:T(8,128)(2,1)S(1)} %copy-done.4, bf16[1,256,1024]{2,1,0:T(8,128)(2,1)S(1)} %copy-done.5, bf16[1,256,1024]{2,1,0:T(8,128)(2,1)S(1)} %copy-done.1, ...), custom_call_target="tpu_custom_call" | custom-call | flops 10000000000 | bytes 8388608 | tf_op jit(solution)/shard_map/own_part/pallas_call | solution.py:525
  74.0 3.3 %halo_grads.1 = (bf16[2,128,1024]{2,1,0:T(8,128)(2,1)}, bf16[2,128,1024]{2,1,0:T(8,128)(2,1)S(1)}) custom-call(bf16[1,256,1024]{2,1,0:T(8,128)(2,1)S(1)} %copy-done.4, bf16[1,256,1024]{2,1,0:T(8,128)(2,1)S(1)} %copy-done.5, bf16[2,128,1024]{2,1,0:T(8,128)(2,1)} %collective-permute-done.low_ref, bf16[2,128,1024]{2,1,0:T(8,128)(2,1)} %collective-permute-done.1.high_ref, ...), custom_call_target="tpu_custom_call" | custom-call | flops 4000000000 | bytes 8388608 | tf_op jit(solution)/shard_map/halo_grads/pallas_call | solution.py:445
  77.3 1.3 %collective-permute-start.2 = (bf16[2,128,1024]{2,1,0:T(8,128)(2,1)}, bf16[2,128,1024]{2,1,0:T(8,128)(2,1)S(1)}, u32[]{:S(2)}, u32[]{:S(2)}) collective-permute-start(bf16[2,128,1024]{2,1,0:T(8,128)(2,1)} %get-tuple-element.42), channel_id=1, source_target_pairs={{1,0},{2,1},{3,2},{4,3},{5,4},{6,5},{7,6},{8,7},{9,8},{10,9},{11,1... | collective-permute-start | bytes 1572872 | tf_op jit(solution)/shard_map/ppermute | solution.py:637
  78.6 4.6 %collective-permute-start.3 = (bf16[2,128,1024]{2,1,0:T(8,128)(2,1)S(1)}, bf16[2,128,1024]{2,1,0:T(8,128)(2,1)S(1)}, u32[]{:S(2)}, u32[]{:S(2)}) collective-permute-start(bf16[2,128,1024]{2,1,0:T(8,128)(2,1)S(1)} %get-tuple-element.43), channel_id=1, source_target_pairs={{0,1},{1,2},{2,3},{3,4},{4,5},{5,6},{6,7},{7,8},{8,9},{9,10},{10,1... | collective-permute-start | bytes 1572872 | tf_op jit(solution)/shard_map/ppermute | solution.py:637
  83.2 2.3 %all-to-all-done.2.in_ref = bf16[64,40,128]{2,1,0:T(8,128)(2,1)S(1)} async-done(((bf16[64,40,128]{2,1,0:T(8,128)(2,1)}), bf16[64,40,128]{2,1,0:T(8,128)(2,1)S(1)}, u32[]{:S(2)}, u32[]{:S(2)}) %all-to-all-start.2) | async-done | bytes 655392 | tf_op jit(solution)/shard_map/all_to_all | solution.py:632
  85.4 1.6 %gather.1 = (bf16[64,32,128]{2,1,0:T(8,128)(2,1)}, f32[8,128]{1,0:T(8,128)S(1)}) custom-call(s32[1,64]{1,0:T(1,128)S(1)} %copy-done.3, bf16[64,40,128]{2,1,0:T(8,128)(2,1)S(1)} %all-to-all-done.2.in_ref), custom_call_target="tpu_custom_call" | custom-call | tf_op jit(solution)/shard_map/gather/pallas_call | solution.py:182
  87.0 9.3 %all-to-all-start.3 = ((bf16[64,32,128]{2,1,0:T(8,128)(2,1)}), bf16[64,32,128]{2,1,0:T(8,128)(2,1)S(1)}, u32[]{:S(2)}, u32[]{:S(2)}) async-start(bf16[64,32,128]{2,1,0:T(8,128)(2,1)} %get-tuple-element.49), calls=%async_computation.3 | async-start | bytes 1048576 | tf_op jit(solution)/shard_map/all_to_all | solution.py:632
  96.4 0.1 collective-permute-start.6
  96.5 0.9 collective-permute-start.5
  97.4 2.4 %collective-permute-start.4 = (f32[8,128]{1,0:T(8,128)S(1)}, f32[8,128]{1,0:T(8,128)S(1)}, u32[]{:S(2)}, u32[]{:S(2)}) collective-permute-start(f32[8,128]{1,0:T(8,128)S(1)} %get-tuple-element.54), channel_id=1, source_target_pairs={{0,64},{64,0},{128,192},{192,128},{1,65},{65,1},{129,193},{193,129... | collective-permute-start | bytes 12296 | tf_op jit(solution)/shard_map/ppermute | solution.py:642
  99.8 0.0 collective-permute-done.2.right_ref
  99.8 0.0 collective-permute-done.3.left_ref
  99.8 4.1 %merge.1 = (bf16[1,256,1024]{2,1,0:T(8,128)(2,1)}, bf16[1,256,1024]{2,1,0:T(8,128)(2,1)}, f32[2,256,1024]{2,1,0:T(8,128)}) custom-call(bf16[2,128,1024]{2,1,0:T(8,128)(2,1)S(1)} %collective-permute-done.2.right_ref, bf16[2,128,1024]{2,1,0:T(8,128)(2,1)S(1)} %collective-permute-done.3.left_ref, f32[256,1024]{1,0:T(8,128)} %get-tuple-element.44.gk_ref, ...), custom_call_target="tpu_custom_call" | custom-call | flops 8000000000 | bytes 8388608 | tf_op jit(solution)/shard_map/merge/pallas_call | solution.py:557
  103.9 0.0 collective-permute-done.6
  103.9 0.6 add_reduce_fusion
  104.5 6.7 %all-to-all-done.3 = bf16[64,32,128]{2,1,0:T(8,128)(2,1)S(1)} async-done(((bf16[64,32,128]{2,1,0:T(8,128)(2,1)}), bf16[64,32,128]{2,1,0:T(8,128)(2,1)S(1)}, u32[]{:S(2)}, u32[]{:S(2)}) %all-to-all-start.3) | async-done | bytes 524320 | tf_op jit(solution)/shard_map/all_to_all | solution.py:632
  111.2 3.0 %finish.1 = (bf16[1,256,1024]{2,1,0:T(8,128)(2,1)}, bf16[1,256,1024]{2,1,0:T(8,128)(2,1)}) custom-call(s32[1,64]{1,0:T(1,128)S(1)} %copy-done.3, f32[2,256,1024]{2,1,0:T(8,128)} %get-tuple-element.46.sums_hbm, bf16[8,8,32,128]{3,2,1,0:T(8,128)(2,1)S(1)} %bitcast.4, ...), custom_call_target="tpu_custom_call", output_to_operand_aliasing={{0}: (3, {}), {1}: (4, {})} | custom-call | tf_op jit(solution)/shard_map/finish/pallas_call | solution.py:614
  (18 shorter events, 0.0 us)
Async XLA Ops:
  0.6 35.6 %copy-start.3 = (s32[1,64]{1,0:T(1,128)S(1)}, s32[1,64]{1,0:T(1,128)}, u32[]{:S(2)}) copy-start(s32[1,64]{1,0:T(1,128)} %starts_ref.9) | copy-start | bytes 772
  0.6 42.1 %copy-start.2 = (bf16[1,256,1024]{2,1,0:T(8,128)(2,1)S(1)}, bf16[1,256,1024]{2,1,0:T(8,128)(2,1)}, u32[]{:S(2)}) copy-start(bf16[1,256,1024]{2,1,0:T(8,128)(2,1)} %v_ref.3) | copy-start | bytes 1572868
  0.7 42.1 %copy-start.1 = (bf16[1,256,1024]{2,1,0:T(8,128)(2,1)S(1)}, bf16[1,256,1024]{2,1,0:T(8,128)(2,1)}, u32[]{:S(2)}) copy-start(bf16[1,256,1024]{2,1,0:T(8,128)(2,1)} %k_ref.3) | copy-start | bytes 1572868
  0.7 42.1 %copy-start.5 = (bf16[1,256,1024]{2,1,0:T(8,128)(2,1)S(1)}, bf16[1,256,1024]{2,1,0:T(8,128)(2,1)}, u32[]{:S(2)}) copy-start(bf16[1,256,1024]{2,1,0:T(8,128)(2,1)} %d_ref.7) | copy-start | bytes 1572868
  0.7 42.1 %copy-start.4 = (bf16[1,256,1024]{2,1,0:T(8,128)(2,1)S(1)}, bf16[1,256,1024]{2,1,0:T(8,128)(2,1)}, u32[]{:S(2)}) copy-start(bf16[1,256,1024]{2,1,0:T(8,128)(2,1)} %q_ref.7) | copy-start | bytes 1572868
  0.7 42.1 %copy-start.7 = (f32[8]{0:T(128)S(1)}, f32[8]{0:T(128)}, u32[]{:S(2)}) copy-start(f32[8]{0:T(128)} %bias_ref.5) | copy-start | bytes 100
  0.7 42.1 %copy-start.6 = (s32[1,64]{1,0:T(1,128)S(1)}, s32[1,64]{1,0:T(1,128)}, u32[]{:S(2)}) copy-start(s32[1,64]{1,0:T(1,128)} %lens_ref.1) | copy-start | bytes 772
  3.8 32.4 %all-to-all-start = ((bf16[64,32,128]{2,1,0:T(8,128)(2,1)}), bf16[64,32,128]{2,1,0:T(8,128)(2,1)S(1)}, u32[]{:S(2)}, u32[]{:S(2)}) async-start(bf16[64,32,128]{2,1,0:T(8,128)(2,1)} %bitcast.7), calls=%async_computation | async-start | bytes 1048576 | tf_op jit(solution)/shard_map/all_to_all | solution.py:632
  16.6 26.2 %collective-permute-start = (bf16[2,128,1024]{2,1,0:T(8,128)(2,1)}, bf16[2,128,1024]{2,1,0:T(8,128)(2,1)}, u32[]{:S(2)}, u32[]{:S(2)}) collective-permute-start(bf16[2,128,1024]{2,1,0:T(8,128)(2,1)} %get-tuple-element.30), channel_id=1, source_target_pairs={{0,1},{1,2},{2,3},{3,4},{4,5},{5,6},{6,7},{7,8},{8,9},{9,10},{10,1... | collective-permute-start | bytes 1572872 | tf_op jit(solution)/shard_map/ppermute | solution.py:637
  20.9 21.9 %collective-permute-start.1 = (bf16[2,128,1024]{2,1,0:T(8,128)(2,1)}, bf16[2,128,1024]{2,1,0:T(8,128)(2,1)}, u32[]{:S(2)}, u32[]{:S(2)}) collective-permute-start(bf16[2,128,1024]{2,1,0:T(8,128)(2,1)} %get-tuple-element.31), channel_id=1, source_target_pairs={{1,0},{2,1},{3,2},{4,3},{5,4},{6,5},{7,6},{8,7},{9,8},{10,9},{11,1... | collective-permute-start | bytes 1572872 | tf_op jit(solution)/shard_map/ppermute | solution.py:637
  37.7 21.5 %all-to-all-start.1 = ((bf16[64,32,128]{2,1,0:T(8,128)(2,1)}), bf16[64,32,128]{2,1,0:T(8,128)(2,1)S(1)}, u32[]{:S(2)}, u32[]{:S(2)}) async-start(bf16[64,32,128]{2,1,0:T(8,128)(2,1)} %route.1), calls=%async_computation.1 | async-start | bytes 1048576 | tf_op jit(solution)/shard_map/all_to_all | solution.py:632
  49.0 0.8 copy-start.8
  59.2 2.7 %copy-start = (bf16[64,32,128]{2,1,0:T(8,128)(2,1)}, bf16[64,32,128]{2,1,0:T(8,128)(2,1)S(1)}, u32[]{:S(2)}) copy-start(bf16[64,32,128]{2,1,0:T(8,128)(2,1)S(1)} %all-to-all-done.1) | copy-start | bytes 1572868
  61.9 23.5 %all-to-all-start.2 = ((bf16[64,40,128]{2,1,0:T(8,128)(2,1)}), bf16[64,40,128]{2,1,0:T(8,128)(2,1)S(1)}, u32[]{:S(2)}, u32[]{:S(2)}) async-start(bf16[64,40,128]{2,1,0:T(8,128)(2,1)} %bitcast.2), calls=%async_computation.2 | async-start | bytes 1310720 | tf_op jit(solution)/shard_map/all_to_all | solution.py:632
  77.3 22.5 %collective-permute-start.2 = (bf16[2,128,1024]{2,1,0:T(8,128)(2,1)}, bf16[2,128,1024]{2,1,0:T(8,128)(2,1)S(1)}, u32[]{:S(2)}, u32[]{:S(2)}) collective-permute-start(bf16[2,128,1024]{2,1,0:T(8,128)(2,1)} %get-tuple-element.42), channel_id=1, source_target_pairs={{1,0},{2,1},{3,2},{4,3},{5,4},{6,5},{7,6},{8,7},{9,8},{10,9},{11,1... | collective-permute-start | bytes 1572872 | tf_op jit(solution)/shard_map/ppermute | solution.py:637
  78.6 21.2 %collective-permute-start.3 = (bf16[2,128,1024]{2,1,0:T(8,128)(2,1)S(1)}, bf16[2,128,1024]{2,1,0:T(8,128)(2,1)S(1)}, u32[]{:S(2)}, u32[]{:S(2)}) collective-permute-start(bf16[2,128,1024]{2,1,0:T(8,128)(2,1)S(1)} %get-tuple-element.43), channel_id=1, source_target_pairs={{0,1},{1,2},{2,3},{3,4},{4,5},{5,6},{6,7},{7,8},{8,9},{9,10},{10,1... | collective-permute-start | bytes 1572872 | tf_op jit(solution)/shard_map/ppermute | solution.py:637
  87.0 24.2 %all-to-all-start.3 = ((bf16[64,32,128]{2,1,0:T(8,128)(2,1)}), bf16[64,32,128]{2,1,0:T(8,128)(2,1)S(1)}, u32[]{:S(2)}, u32[]{:S(2)}) async-start(bf16[64,32,128]{2,1,0:T(8,128)(2,1)} %get-tuple-element.49), calls=%async_computation.3 | async-start | bytes 1048576 | tf_op jit(solution)/shard_map/all_to_all | solution.py:632
  96.4 7.5 %collective-permute-start.6 = (f32[8,128]{1,0:T(8,128)S(1)}, f32[8,128]{1,0:T(8,128)S(1)}, u32[]{:S(2)}, u32[]{:S(2)}) collective-permute-start(f32[8,128]{1,0:T(8,128)S(1)} %get-tuple-element.54), channel_id=1, source_target_pairs={{0,192},{64,128},{128,64},{192,0},{1,193},{65,129},{129,65},{193,1... | collective-permute-start | bytes 12296 | tf_op jit(solution)/shard_map/ppermute | solution.py:642
  96.5 7.4 %collective-permute-start.5 = (f32[8,128]{1,0:T(8,128)S(1)}, f32[8,128]{1,0:T(8,128)S(1)}, u32[]{:S(2)}, u32[]{:S(2)}) collective-permute-start(f32[8,128]{1,0:T(8,128)S(1)} %get-tuple-element.54), channel_id=1, source_target_pairs={{0,128},{64,192},{128,0},{192,64},{1,129},{65,193},{129,1},{193,65... | collective-permute-start | bytes 12296 | tf_op jit(solution)/shard_map/ppermute | solution.py:642
  97.4 6.6 %collective-permute-start.4 = (f32[8,128]{1,0:T(8,128)S(1)}, f32[8,128]{1,0:T(8,128)S(1)}, u32[]{:S(2)}, u32[]{:S(2)}) collective-permute-start(f32[8,128]{1,0:T(8,128)S(1)} %get-tuple-element.54), channel_id=1, source_target_pairs={{0,64},{64,0},{128,192},{192,128},{1,65},{65,1},{129,193},{193,129... | collective-permute-start | bytes 12296 | tf_op jit(solution)/shard_map/ppermute | solution.py:642

commit v8 on v7

--- a/solution.py
+++ b/solution.py
@@ -1,3 +1,4 @@
+import functools
 import math
 
 import jax
@@ -20,6 +21,7 @@
 GROUP = 2
 STAGED = 4
 MERGE = 8
+OWN = (5, 1)
 NEG = -1e30
 LOG2E = math.log2(math.e)
 SCALE = 1.0 / math.sqrt(HD)
@@ -454,6 +456,7 @@
 
 
 def own_kernel(
+    first,
     bias_ref,
     q_ref,
     d_ref,
@@ -466,13 +469,11 @@
     own_mask,
     halo_mask,
     prompt_mask,
-    attended_ref,
-    gq_ref,
-    gk_ref,
-    gv_ref,
+    *rest,
 ):
+    attended_ref, gq_ref, gk_ref, gv_ref = rest[-4:]
     members = range(GROUP)
-    step = pl.program_id(0)
+    step = first + pl.program_id(0)
     blocks = []
     for member in members:
         cols = columns(member)
@@ -516,28 +517,32 @@
         gq_ref[0, :, cols] = grad_q.astype(jnp.bfloat16)
 
 
-def own_part(bias, queries, cotangent, key_rows, values, low, high, prompt, final, masks):
-    rows = pl.BlockSpec((1, ROWS, GROUP * HD), lambda step: (0, 0, step))
-    halo = pl.BlockSpec((2, HW, GROUP * HD), lambda step: (0, 0, step))
-    pieces = pl.BlockSpec((BANDS, GROUP, 2 * BAND, HD), lambda step: (0, step, 0, 0))
-    tile = pl.BlockSpec((GROUP, 8, ROWS), lambda step: (step, 0, 0))
-    total = pl.BlockSpec((ROWS, GROUP * HD), lambda step: (0, step))
-    return pl.pallas_call(
-        own_kernel,
-        grid=(HEADS // GROUP,),
+def own_part(half, bias, queries, cotangent, key_rows, values, low, high, prompt, final, masks, begun):
+    steps = HEADS // GROUP // 2
+    first = half * steps
+    rows = pl.BlockSpec((1, ROWS, GROUP * HD), lambda step: (0, 0, first + step))
+    halo = pl.BlockSpec((2, HW, GROUP * HD), lambda step: (0, 0, first + step))
+    pieces = pl.BlockSpec((BANDS, GROUP, 2 * BAND, HD), lambda step: (0, first + step, 0, 0))
+    tile = pl.BlockSpec((GROUP, 8, ROWS), lambda step: (first + step, 0, 0))
+    total = pl.BlockSpec((ROWS, GROUP * HD), lambda step: (0, first + step))
+    specs = [SMEM, rows, rows, rows, rows, halo, halo, pieces, tile]
+    specs += [whole(mask) for mask in MASKS]
+    return pl.pallas_call(
+        functools.partial(own_kernel, first),
+        grid=(steps,),
         out_shape=(
             low_array(1, ROWS, WIDTH),
             low_array(1, ROWS, WIDTH),
             float_array(ROWS, WIDTH),
             float_array(ROWS, WIDTH),
         ),
-        in_specs=[SMEM, rows, rows, rows, rows, halo, halo, pieces, tile]
-        + [whole(mask) for mask in MASKS],
+        in_specs=specs + [HBM] * len(begun),
         out_specs=(rows, rows, total, total),
+        input_output_aliases={len(specs) + index: index for index in range(len(begun))},
         compiler_params=NEARLY,
-        cost_estimate=cost(10),
+        cost_estimate=cost(OWN[half]),
         name="own_part",
-    )(bias, queries, cotangent, key_rows, values, low, high, prompt, final, *masks)
+    )(bias, queries, cotangent, key_rows, values, low, high, prompt, final, *masks, *begun)
 
 
 def merge_kernel(right_ref, left_ref, gk_ref, gv_ref, outk_ref, outv_ref, sums_ref):
@@ -659,10 +664,9 @@
     prompt = exchange(route(starts, held)).reshape(BANDS, HEADS, 2 * BAND, HD)
     gprompt, final = prompt_part(bias, queries, cotangent, prompt, stats, masks[2])
     held = exchange(gprompt.reshape(count, SENT, HD))
-    attended, grad_q, gk, gv = own_part(
-        bias, queries, cotangent, key_rows, values, low, high, prompt, final, masks
-    )
-    final, gk = lax.optimization_barrier((final, gk))
+    arrays = (queries, cotangent, key_rows, values, low, high, prompt)
+    begun = own_part(0, bias, *arrays, final, masks, ())
+    final, begun = lax.optimization_barrier((final, begun))
     glow, ghigh = halo_grads(queries, cotangent, low, high, final, masks[1])
     right = shifted(glow, -1)
     left = shifted(ghigh, 1)
@@ -670,6 +674,8 @@
     owned, sums = gather(starts, held)
     returned = exchange(owned).reshape(BANDS, HEADS, 2 * BAND, HD)
     grad_bias = jnp.sum(summed(sums, "dp", 1, 2), axis=1)
+    final, _ = lax.optimization_barrier((final, sums))
+    attended, grad_q, gk, gv = own_part(1, bias, *arrays, final, masks, begun)
     outk, outv, both = merge(gk, gv, left, right)
     grad_k, grad_v = finish(starts, outk, outv, both, returned)
     return attended, grad_q, grad_k, grad_v, grad_bias

time: 115 us -> 113 us (0.983)
  waiting for transfers between devices: 32.4 us -> 29.4 us
  Pallas kernels: 32.3 us -> 34.4 us
  starting transfers between devices: 47.2 us -> 45.9 us
    all_to_all x4, waiting for transfers between devices: 32.3 us -> 29.3 us  [exchange(): return lax.all_to_all(pieces, 'ctx', 0, 0, tiled=True)]
    all_to_all x4, starting transfers between devices: 32.3 us -> 30.3 us  [exchange(): return lax.all_to_all(pieces, 'ctx', 0, 0, tiled=True)]
    pallas_call x1 -> x2, Pallas kernels: 6.91 us -> 8.77 us  [own_part(): pl.pallas_call(functools.partial(own_kernel, first), grid=(steps,), out_s...]
  transfers between devices with their start and end apart: 11 -> 11, of which waited for: 4 -> 4; matrix products, arithmetic and copies ran while one was open for 1% -> 1% of each run, Pallas kernels for 21% -> 23%
where the time goes in v8:
time: 113 us; the launch traced here: 112 us
  starting transfers between devices  45.9 us (41%)
  Pallas kernels  34.4 us (30%)
  waiting for transfers between devices  29.4 us (26%)
    all_to_all x4, starting transfers between devices, exchange(): return lax.all_to_all(pieces, 'ctx', 0, 0, tiled=True)  30.3 us
    all_to_all x4, waiting for transfers between devices, exchange(): return lax.all_to_all(pieces, 'ctx', 0, 0, tiled=True)  29.3 us
    ppermute x4, starting transfers between devices, shifted(): lax.ppermute(x, 'ctx', [(i, i + by) for i in range(peers) if 0 <= i + by...  12.2 us
    pallas_call x2, Pallas kernels, own_part(): pl.pallas_call(functools.partial(own_kernel, first), grid=(steps,), out_s...  8.77 us
    pallas_call x1, Pallas kernels, window(): pl.pallas_call(window_kernel, grid=(HEADS,), out_shape=(float_array(HEADS...  6.2 us
    pallas_call x1, Pallas kernels, merge(): pl.pallas_call(merge_kernel, grid=(HEADS // GROUP,), out_shape=(low_array...  4.12 us
    ppermute x3, starting transfers between devices, partners(): lax.ppermute(x, axis, [(i, i ^ step) for i in range(peers)])  3.46 us
    pallas_call x1, Pallas kernels, halo_grads(): pl.pallas_call(halo_kernel, out_shape=(low_array(2, HW, WIDTH), low_array...  3.38 us
  transfers between devices with their start and end apart: 11, of which 4 were waited for; matrix products, arithmetic and copies ran while one was open for 1% of the time, Pallas kernels for 23%

profile of v8, /device:TPU:4, one launch (start us, length us, event | category | flops | bytes accessed | tf_op | source)
XLA Modules:
  0.0 112.0 jit_solution(17549508713789586440)
XLA Ops:
  0.7 0.0 copy-start.2
  0.7 3.1 %cut_prompt.1 = (bf16[8,8,32,128]{3,2,1,0:T(8,128)(2,1)}, bf16[2,128,1024]{2,1,0:T(8,128)(2,1)}, bf16[2,128,1024]{2,1,0:T(8,128)(2,1)}) custom-call(s32[1,64]{1,0:T(1,128)} %starts_ref.9, bf16[1,256,1024]{2,1,0:T(8,128)(2,1)} %k_ref.5, bf16[1,256,1024]{2,1,0:T(8,128)(2,1)} %v_ref.5), custom_call_target="tpu_custom_call" | custom-call | tf_op jit(solution)/shard_map/cut_prompt/pallas_call | solution.py:122
  3.8 12.8 %all-to-all-start = ((bf16[64,32,128]{2,1,0:T(8,128)(2,1)}), bf16[64,32,128]{2,1,0:T(8,128)(2,1)S(1)}, u32[]{:S(2)}, u32[]{:S(2)}) async-start(bf16[64,32,128]{2,1,0:T(8,128)(2,1)} %bitcast.8), calls=%async_computation | async-start | bytes 1048576 | tf_op jit(solution)/shard_map/all_to_all | solution.py:637
  16.6 4.3 %collective-permute-start = (bf16[2,128,1024]{2,1,0:T(8,128)(2,1)}, bf16[2,128,1024]{2,1,0:T(8,128)(2,1)}, u32[]{:S(2)}, u32[]{:S(2)}) collective-permute-start(bf16[2,128,1024]{2,1,0:T(8,128)(2,1)} %get-tuple-element.38), channel_id=1, source_target_pairs={{0,1},{1,2},{2,3},{3,4},{4,5},{5,6},{6,7},{7,8},{8,9},{9,10},{10,1... | collective-permute-start | bytes 1572872 | tf_op jit(solution)/shard_map/ppermute | solution.py:642
  20.9 1.3 %collective-permute-start.1 = (bf16[2,128,1024]{2,1,0:T(8,128)(2,1)}, bf16[2,128,1024]{2,1,0:T(8,128)(2,1)}, u32[]{:S(2)}, u32[]{:S(2)}) collective-permute-start(bf16[2,128,1024]{2,1,0:T(8,128)(2,1)} %get-tuple-element.39), channel_id=1, source_target_pairs={{1,0},{2,1},{3,2},{4,3},{5,4},{6,5},{7,6},{8,7},{9,8},{10,9},{11,1... | collective-permute-start | bytes 1572872 | tf_op jit(solution)/shard_map/ppermute | solution.py:642
  22.1 14.0 %all-to-all-done.in_ref = bf16[64,32,128]{2,1,0:T(8,128)(2,1)S(1)} async-done(((bf16[64,32,128]{2,1,0:T(8,128)(2,1)}), bf16[64,32,128]{2,1,0:T(8,128)(2,1)S(1)}, u32[]{:S(2)}, u32[]{:S(2)}) %all-to-all-start) | async-done | bytes 524320 | tf_op jit(solution)/shard_map/all_to_all | solution.py:637
  36.2 1.5 %route.1 = bf16[64,32,128]{2,1,0:T(8,128)(2,1)} custom-call(s32[1,64]{1,0:T(1,128)S(1)} %copy-done.6, bf16[64,32,128]{2,1,0:T(8,128)(2,1)S(1)} %all-to-all-done.in_ref), custom_call_target="tpu_custom_call" | custom-call | tf_op jit(solution)/shard_map/route/pallas_call | solution.py:155
  37.7 5.1 %all-to-all-start.1 = ((bf16[64,32,128]{2,1,0:T(8,128)(2,1)}), bf16[64,32,128]{2,1,0:T(8,128)(2,1)S(1)}, u32[]{:S(2)}, u32[]{:S(2)}) async-start(bf16[64,32,128]{2,1,0:T(8,128)(2,1)} %route.1), calls=%async_computation.1 | async-start | bytes 1048576 | tf_op jit(solution)/shard_map/all_to_all | solution.py:637
  42.8 0.0 collective-permute-done.1.high_ref
  42.8 6.2 %window.1 = (f32[8,8,256]{2,1,0:T(8,128)S(1)}, f32[2,256,256]{2,1,0:T(8,128)S(1)}, f32[2,128,128]{2,1,0:T(8,128)S(1)}, f32[128,256]{1,0:T(8,128)S(1)}) custom-call(s32[1,64]{1,0:T(1,128)S(1)} %copy-done.6, s32[1,64]{1,0:T(1,128)S(1)} %copy-done.8, f32[8]{0:T(128)S(1)} %copy-done.7, bf16[1,256,1024]{2,1,0:T(8,128)(2,1)S(1)} %copy-done.3, ...), custom_call_target="tpu_custom_call" | custom-call | flops 20000000000 | bytes 8388608 | tf_op jit(solution)/shard_map/window/pallas_call | solution.py:322
  49.1 0.0 copy-start.5
  49.1 0.8 copy-done.5
  49.8 9.3 %all-to-all-done.1 = bf16[64,32,128]{2,1,0:T(8,128)(2,1)S(1)} async-done(((bf16[64,32,128]{2,1,0:T(8,128)(2,1)}), bf16[64,32,128]{2,1,0:T(8,128)(2,1)S(1)}, u32[]{:S(2)}, u32[]{:S(2)}) %all-to-all-start.1) | async-done | bytes 524320 | tf_op jit(solution)/shard_map/all_to_all | solution.py:637
  59.2 2.7 %prompt_part.1 = (bf16[8,8,40,128]{3,2,1,0:T(8,128)(2,1)}, f32[8,8,256]{2,1,0:T(8,128)S(1)}) custom-call(f32[8]{0:T(128)S(1)} %copy-done.7, bf16[1,256,1024]{2,1,0:T(8,128)(2,1)S(1)} %copy-done.3, bf16[1,256,1024]{2,1,0:T(8,128)(2,1)S(1)} %copy-done.4, bf16[8,8,32,128]{3,2,1,0:T(8,128)(2,1)S(1)} %bitcast.5, f32[8,8,256]{2,1,0:T(8,128)S(1)} %get-tuple-element.41.stats_ref, ...), custom_call_target="tpu_custom_call" | custom-call | flops 4000000000 | bytes 8388608 | tf_op jit(solution)/shard_map/prompt_part/pallas_call | solution.py:394
  61.9 5.2 %all-to-all-start.2 = ((bf16[64,40,128]{2,1,0:T(8,128)(2,1)}), bf16[64,40,128]{2,1,0:T(8,128)(2,1)S(1)}, u32[]{:S(2)}, u32[]{:S(2)}) async-start(bf16[64,40,128]{2,1,0:T(8,128)(2,1)} %bitcast.2), calls=%async_computation.2 | async-start | bytes 1310720 | tf_op jit(solution)/shard_map/all_to_all | solution.py:637
  67.1 4.4 %own_part.2 = (bf16[1,256,1024]{2,1,0:T(8,128)(2,1)}, bf16[1,256,1024]{2,1,0:T(8,128)(2,1)}, f32[256,1024]{1,0:T(8,128)}, f32[256,1024]{1,0:T(8,128)}) custom-call(f32[8]{0:T(128)S(1)} %copy-done.7, bf16[1,256,1024]{2,1,0:T(8,128)(2,1)S(1)} %copy-done.3, bf16[1,256,1024]{2,1,0:T(8,128)(2,1)S(1)} %copy-done.4, bf16[1,256,1024]{2,1,0:T(8,128)(2,1)S(1)} %copy-done.1, ...), custom_call_target="tpu_custom_call" | custom-call | flops 5000000000 | bytes 8388608 | tf_op jit(solution)/shard_map/own_part/pallas_call | solution.py:530
  71.5 3.4 %halo_grads.1 = (bf16[2,128,1024]{2,1,0:T(8,128)(2,1)}, bf16[2,128,1024]{2,1,0:T(8,128)(2,1)}) custom-call(bf16[1,256,1024]{2,1,0:T(8,128)(2,1)S(1)} %copy-done.3, bf16[1,256,1024]{2,1,0:T(8,128)(2,1)S(1)} %copy-done.4, bf16[2,128,1024]{2,1,0:T(8,128)(2,1)} %collective-permute-done.low_ref, bf16[2,128,1024]{2,1,0:T(8,128)(2,1)} %collective-permute-done.1.high_ref, ...), custom_call_target="tpu_custom_call" | custom-call | flops 4000000000 | bytes 8388608 | tf_op jit(solution)/shard_map/halo_grads/pallas_call | solution.py:447
  74.9 1.3 %collective-permute-start.2 = (bf16[2,128,1024]{2,1,0:T(8,128)(2,1)}, bf16[2,128,1024]{2,1,0:T(8,128)(2,1)S(1)}, u32[]{:S(2)}, u32[]{:S(2)}) collective-permute-start(bf16[2,128,1024]{2,1,0:T(8,128)(2,1)} %get-tuple-element.52), channel_id=1, source_target_pairs={{1,0},{2,1},{3,2},{4,3},{5,4},{6,5},{7,6},{8,7},{9,8},{10,9},{11,1... | collective-permute-start | bytes 1572872 | tf_op jit(solution)/shard_map/ppermute | solution.py:642
  76.2 5.4 %collective-permute-start.3 = (bf16[2,128,1024]{2,1,0:T(8,128)(2,1)}, bf16[2,128,1024]{2,1,0:T(8,128)(2,1)}, u32[]{:S(2)}, u32[]{:S(2)}) collective-permute-start(bf16[2,128,1024]{2,1,0:T(8,128)(2,1)} %get-tuple-element.53), channel_id=1, source_target_pairs={{0,1},{1,2},{2,3},{3,4},{4,5},{5,6},{6,7},{7,8},{8,9},{9,10},{10,1... | collective-permute-start | bytes 1572872 | tf_op jit(solution)/shard_map/ppermute | solution.py:642
  81.6 3.9 %all-to-all-done.2.in_ref = bf16[64,40,128]{2,1,0:T(8,128)(2,1)S(1)} async-done(((bf16[64,40,128]{2,1,0:T(8,128)(2,1)}), bf16[64,40,128]{2,1,0:T(8,128)(2,1)S(1)}, u32[]{:S(2)}, u32[]{:S(2)}) %all-to-all-start.2) | async-done | bytes 655392 | tf_op jit(solution)/shard_map/all_to_all | solution.py:637
  85.4 1.6 %gather.1 = (bf16[64,32,128]{2,1,0:T(8,128)(2,1)}, f32[8,128]{1,0:T(8,128)S(1)}) custom-call(s32[1,64]{1,0:T(1,128)S(1)} %copy-done.6, bf16[64,40,128]{2,1,0:T(8,128)(2,1)S(1)} %all-to-all-done.2.in_ref), custom_call_target="tpu_custom_call" | custom-call | tf_op jit(solution)/shard_map/gather/pallas_call | solution.py:184
  87.0 7.2 %all-to-all-start.3 = ((bf16[64,32,128]{2,1,0:T(8,128)(2,1)}), bf16[64,32,128]{2,1,0:T(8,128)(2,1)S(1)}, u32[]{:S(2)}, u32[]{:S(2)}) async-start(bf16[64,32,128]{2,1,0:T(8,128)(2,1)} %get-tuple-element.66), calls=%async_computation.3 | async-start | bytes 1048576 | tf_op jit(solution)/shard_map/all_to_all | solution.py:637
  94.3 0.1 collective-permute-start.4
  94.4 0.9 collective-permute-start.5
  95.3 2.5 %collective-permute-start.6 = (f32[8,128]{1,0:T(8,128)S(1)}, f32[8,128]{1,0:T(8,128)S(1)}, u32[]{:S(2)}, u32[]{:S(2)}) collective-permute-start(f32[8,128]{1,0:T(8,128)S(1)} %get-tuple-element.55), channel_id=1, source_target_pairs={{0,192},{64,128},{128,64},{192,0},{1,193},{65,129},{129,65},{193,1... | collective-permute-start | bytes 12296 | tf_op jit(solution)/shard_map/ppermute | solution.py:647
  97.8 4.4 %own_part.3 = (bf16[1,256,1024]{2,1,0:T(8,128)(2,1)}, bf16[1,256,1024]{2,1,0:T(8,128)(2,1)}, f32[256,1024]{1,0:T(8,128)}, f32[256,1024]{1,0:T(8,128)}) custom-call(f32[8]{0:T(128)S(1)} %copy-done.7, bf16[1,256,1024]{2,1,0:T(8,128)(2,1)S(1)} %copy-done.3, ...), custom_call_target="tpu_custom_call", output_to_operand_aliasing={{0}: (12, {}), {1}: (13, {}), {2}: (14, {}), {3}: (15, {})} | custom-call | flops 1000000000 | bytes 8388608 | tf_op jit(solution)/shard_map/own_part/pallas_call | solution.py:530
  102.1 0.0 collective-permute-done.2.right_ref
  102.1 4.1 %merge.1 = (bf16[1,256,1024]{2,1,0:T(8,128)(2,1)}, bf16[1,256,1024]{2,1,0:T(8,128)(2,1)}, f32[2,256,1024]{2,1,0:T(8,128)}) custom-call(bf16[2,128,1024]{2,1,0:T(8,128)(2,1)S(1)} %collective-permute-done.2.right_ref, bf16[2,128,1024]{2,1,0:T(8,128)(2,1)} %collective-permute-done.3.left_ref, f32[256,1024]{1,0:T(8,128)} %get-tuple-element.63.gk_ref, ...), custom_call_target="tpu_custom_call" | custom-call | flops 8000000000 | bytes 8388608 | tf_op jit(solution)/shard_map/merge/pallas_call | solution.py:562
  106.3 0.0 collective-permute-done.4
  106.3 0.6 add_reduce_fusion
  106.9 2.1 %all-to-all-done.3 = bf16[64,32,128]{2,1,0:T(8,128)(2,1)S(1)} async-done(((bf16[64,32,128]{2,1,0:T(8,128)(2,1)}), bf16[64,32,128]{2,1,0:T(8,128)(2,1)S(1)}, u32[]{:S(2)}, u32[]{:S(2)}) %all-to-all-start.3) | async-done | bytes 524320 | tf_op jit(solution)/shard_map/all_to_all | solution.py:637
  109.0 3.0 %finish.1 = (bf16[1,256,1024]{2,1,0:T(8,128)(2,1)}, bf16[1,256,1024]{2,1,0:T(8,128)(2,1)}) custom-call(s32[1,64]{1,0:T(1,128)S(1)} %copy-done.6, f32[2,256,1024]{2,1,0:T(8,128)} %get-tuple-element.65.sums_hbm, bf16[8,8,32,128]{3,2,1,0:T(8,128)(2,1)S(1)} %bitcast.4, ...), custom_call_target="tpu_custom_call", output_to_operand_aliasing={{0}: (3, {}), {1}: (4, {})} | custom-call | tf_op jit(solution)/shard_map/finish/pallas_call | solution.py:619
  (19 shorter events, 0.0 us)
Async XLA Ops:
  0.6 35.6 %copy-start.6 = (s32[1,64]{1,0:T(1,128)S(1)}, s32[1,64]{1,0:T(1,128)}, u32[]{:S(2)}) copy-start(s32[1,64]{1,0:T(1,128)} %starts_ref.9) | copy-start | bytes 772
  0.6 42.1 %copy-start.1 = (bf16[1,256,1024]{2,1,0:T(8,128)(2,1)S(1)}, bf16[1,256,1024]{2,1,0:T(8,128)(2,1)}, u32[]{:S(2)}) copy-start(bf16[1,256,1024]{2,1,0:T(8,128)(2,1)} %k_ref.5) | copy-start | bytes 1572868
  0.7 42.1 %copy-start.2 = (bf16[1,256,1024]{2,1,0:T(8,128)(2,1)S(1)}, bf16[1,256,1024]{2,1,0:T(8,128)(2,1)}, u32[]{:S(2)}) copy-start(bf16[1,256,1024]{2,1,0:T(8,128)(2,1)} %v_ref.5) | copy-start | bytes 1572868
  0.7 42.1 %copy-start.4 = (bf16[1,256,1024]{2,1,0:T(8,128)(2,1)S(1)}, bf16[1,256,1024]{2,1,0:T(8,128)(2,1)}, u32[]{:S(2)}) copy-start(bf16[1,256,1024]{2,1,0:T(8,128)(2,1)} %d_ref.9) | copy-start | bytes 1572868
  0.7 42.1 %copy-start.8 = (s32[1,64]{1,0:T(1,128)S(1)}, s32[1,64]{1,0:T(1,128)}, u32[]{:S(2)}) copy-start(s32[1,64]{1,0:T(1,128)} %lens_ref.1) | copy-start | bytes 772
  0.7 42.1 %copy-start.7 = (f32[8]{0:T(128)S(1)}, f32[8]{0:T(128)}, u32[]{:S(2)}) copy-start(f32[8]{0:T(128)} %bias_ref.7) | copy-start | bytes 100
  0.7 42.1 %copy-start.3 = (bf16[1,256,1024]{2,1,0:T(8,128)(2,1)S(1)}, bf16[1,256,1024]{2,1,0:T(8,128)(2,1)}, u32[]{:S(2)}) copy-start(bf16[1,256,1024]{2,1,0:T(8,128)(2,1)} %q_ref.9) | copy-start | bytes 1572868
  3.8 32.4 %all-to-all-start = ((bf16[64,32,128]{2,1,0:T(8,128)(2,1)}), bf16[64,32,128]{2,1,0:T(8,128)(2,1)S(1)}, u32[]{:S(2)}, u32[]{:S(2)}) async-start(bf16[64,32,128]{2,1,0:T(8,128)(2,1)} %bitcast.8), calls=%async_computation | async-start | bytes 1048576 | tf_op jit(solution)/shard_map/all_to_all | solution.py:637
  16.6 26.2 %collective-permute-start = (bf16[2,128,1024]{2,1,0:T(8,128)(2,1)}, bf16[2,128,1024]{2,1,0:T(8,128)(2,1)}, u32[]{:S(2)}, u32[]{:S(2)}) collective-permute-start(bf16[2,128,1024]{2,1,0:T(8,128)(2,1)} %get-tuple-element.38), channel_id=1, source_target_pairs={{0,1},{1,2},{2,3},{3,4},{4,5},{5,6},{6,7},{7,8},{8,9},{9,10},{10,1... | collective-permute-start | bytes 1572872 | tf_op jit(solution)/shard_map/ppermute | solution.py:642
  20.9 21.9 %collective-permute-start.1 = (bf16[2,128,1024]{2,1,0:T(8,128)(2,1)}, bf16[2,128,1024]{2,1,0:T(8,128)(2,1)}, u32[]{:S(2)}, u32[]{:S(2)}) collective-permute-start(bf16[2,128,1024]{2,1,0:T(8,128)(2,1)} %get-tuple-element.39), channel_id=1, source_target_pairs={{1,0},{2,1},{3,2},{4,3},{5,4},{6,5},{7,6},{8,7},{9,8},{10,9},{11,1... | collective-permute-start | bytes 1572872 | tf_op jit(solution)/shard_map/ppermute | solution.py:642
  37.7 21.5 %all-to-all-start.1 = ((bf16[64,32,128]{2,1,0:T(8,128)(2,1)}), bf16[64,32,128]{2,1,0:T(8,128)(2,1)S(1)}, u32[]{:S(2)}, u32[]{:S(2)}) async-start(bf16[64,32,128]{2,1,0:T(8,128)(2,1)} %route.1), calls=%async_computation.1 | async-start | bytes 1048576 | tf_op jit(solution)/shard_map/all_to_all | solution.py:637
  49.1 0.8 copy-start.5
  59.2 2.7 %copy-start = (bf16[64,32,128]{2,1,0:T(8,128)(2,1)}, bf16[64,32,128]{2,1,0:T(8,128)(2,1)S(1)}, u32[]{:S(2)}) copy-start(bf16[64,32,128]{2,1,0:T(8,128)(2,1)S(1)} %all-to-all-done.1) | copy-start | bytes 1572868
  61.9 23.5 %all-to-all-start.2 = ((bf16[64,40,128]{2,1,0:T(8,128)(2,1)}), bf16[64,40,128]{2,1,0:T(8,128)(2,1)S(1)}, u32[]{:S(2)}, u32[]{:S(2)}) async-start(bf16[64,40,128]{2,1,0:T(8,128)(2,1)} %bitcast.2), calls=%async_computation.2 | async-start | bytes 1310720 | tf_op jit(solution)/shard_map/all_to_all | solution.py:637
  74.9 27.2 %collective-permute-start.2 = (bf16[2,128,1024]{2,1,0:T(8,128)(2,1)}, bf16[2,128,1024]{2,1,0:T(8,128)(2,1)S(1)}, u32[]{:S(2)}, u32[]{:S(2)}) collective-permute-start(bf16[2,128,1024]{2,1,0:T(8,128)(2,1)} %get-tuple-element.52), channel_id=1, source_target_pairs={{1,0},{2,1},{3,2},{4,3},{5,4},{6,5},{7,6},{8,7},{9,8},{10,9},{11,1... | collective-permute-start | bytes 1572872 | tf_op jit(solution)/shard_map/ppermute | solution.py:642
  76.2 25.9 %collective-permute-start.3 = (bf16[2,128,1024]{2,1,0:T(8,128)(2,1)}, bf16[2,128,1024]{2,1,0:T(8,128)(2,1)}, u32[]{:S(2)}, u32[]{:S(2)}) collective-permute-start(bf16[2,128,1024]{2,1,0:T(8,128)(2,1)} %get-tuple-element.53), channel_id=1, source_target_pairs={{0,1},{1,2},{2,3},{3,4},{4,5},{5,6},{6,7},{7,8},{8,9},{9,10},{10,1... | collective-permute-start | bytes 1572872 | tf_op jit(solution)/shard_map/ppermute | solution.py:642
  87.0 22.0 %all-to-all-start.3 = ((bf16[64,32,128]{2,1,0:T(8,128)(2,1)}), bf16[64,32,128]{2,1,0:T(8,128)(2,1)S(1)}, u32[]{:S(2)}, u32[]{:S(2)}) async-start(bf16[64,32,128]{2,1,0:T(8,128)(2,1)} %get-tuple-element.66), calls=%async_computation.3 | async-start | bytes 1048576 | tf_op jit(solution)/shard_map/all_to_all | solution.py:637
  94.3 12.0 %collective-permute-start.4 = (f32[8,128]{1,0:T(8,128)S(1)}, f32[8,128]{1,0:T(8,128)S(1)}, u32[]{:S(2)}, u32[]{:S(2)}) collective-permute-start(f32[8,128]{1,0:T(8,128)S(1)} %get-tuple-element.55), channel_id=1, source_target_pairs={{0,64},{64,0},{128,192},{192,128},{1,65},{65,1},{129,193},{193,129... | collective-permute-start | bytes 12296 | tf_op jit(solution)/shard_map/ppermute | solution.py:647
  94.4 11.9 %collective-permute-start.5 = (f32[8,128]{1,0:T(8,128)S(1)}, f32[8,128]{1,0:T(8,128)S(1)}, u32[]{:S(2)}, u32[]{:S(2)}) collective-permute-start(f32[8,128]{1,0:T(8,128)S(1)} %get-tuple-element.55), channel_id=1, source_target_pairs={{0,128},{64,192},{128,0},{192,64},{1,129},{65,193},{129,1},{193,65... | collective-permute-start | bytes 12296 | tf_op jit(solution)/shard_map/ppermute | solution.py:647
  95.3 11.0 %collective-permute-start.6 = (f32[8,128]{1,0:T(8,128)S(1)}, f32[8,128]{1,0:T(8,128)S(1)}, u32[]{:S(2)}, u32[]{:S(2)}) collective-permute-start(f32[8,128]{1,0:T(8,128)S(1)} %get-tuple-element.55), channel_id=1, source_target_pairs={{0,192},{64,128},{128,64},{192,0},{1,193},{65,129},{129,65},{193,1... | collective-permute-start | bytes 12296 | tf_op jit(solution)/shard_map/ppermute | solution.py:647

commit v9 on v8

--- a/solution.py
+++ b/solution.py
@@ -581,6 +581,7 @@
     outv_hbm,
     sums_ref,
     rows_ref,
+    placed_ref,
     load_sems,
     store_sems,
 ):
@@ -604,12 +605,12 @@
         frame, row = grid_of(SPAN, PMAX)
         place = (frame == row + (offset - base)).astype(jnp.bfloat16)
         for part in range(2):
+            for head in range(HEADS):
+                piece = prompt_ref[:, head, part * BAND : (part + 1) * BAND, :].reshape(PMAX, HD)
+                placed_ref[part, :, columns(head)] = nn(place, piece)
+        for part in range(2):
             loads[part].wait()
-            for head in range(HEADS):
-                cols = columns(head)
-                piece = prompt_ref[:, head, part * BAND : (part + 1) * BAND, :].reshape(PMAX, HD)
-                total = sums_ref[part, :, cols] + nn(place, piece)
-                rows_ref[part, :, cols] = total.astype(jnp.bfloat16)
+            rows_ref[part] = (sums_ref[part] + placed_ref[part]).astype(jnp.bfloat16)
             stores[part].start()
         for copy in stores:
             copy.wait()
@@ -625,6 +626,7 @@
         scratch_shapes=[
             pltpu.VMEM((2, SPAN, WIDTH), jnp.float32),
             pltpu.VMEM((2, SPAN, WIDTH), jnp.bfloat16),
+            pltpu.VMEM((2, SPAN, WIDTH), jnp.float32),
             pltpu.SemaphoreType.DMA((2,)),
             pltpu.SemaphoreType.DMA((2,)),
         ],

time: 113 us -> 113 us (level)
  no operation moved by 1% of the time
where the time goes in v9:
time: 113 us; the launch traced here: 112 us
  starting transfers between devices  45.9 us (41%)
  Pallas kernels  34.3 us (30%)
  waiting for transfers between devices  29.4 us (26%)
    all_to_all x4, starting transfers between devices, exchange(): return lax.all_to_all(pieces, 'ctx', 0, 0, tiled=True)  30.3 us
    all_to_all x4, waiting for transfers between devices, exchange(): return lax.all_to_all(pieces, 'ctx', 0, 0, tiled=True)  29.3 us
    ppermute x4, starting transfers between devices, shifted(): lax.ppermute(x, 'ctx', [(i, i + by) for i in range(peers) if 0 <= i + by...  12.2 us
    pallas_call x2, Pallas kernels, own_part(): pl.pallas_call(functools.partial(own_kernel, first), grid=(steps,), out_s...  8.77 us
    pallas_call x1, Pallas kernels, window(): pl.pallas_call(window_kernel, grid=(HEADS,), out_shape=(float_array(HEADS...  6.2 us
    pallas_call x1, Pallas kernels, merge(): pl.pallas_call(merge_kernel, grid=(HEADS // GROUP,), out_shape=(low_array...  4.12 us
    ppermute x3, starting transfers between devices, partners(): lax.ppermute(x, axis, [(i, i ^ step) for i in range(peers)])  3.46 us
    pallas_call x1, Pallas kernels, halo_grads(): pl.pallas_call(halo_kernel, out_shape=(low_array(2, HW, WIDTH), low_array...  3.38 us
  transfers between devices with their start and end apart: 11, of which 4 were waited for; matrix products, arithmetic and copies ran while one was open for 1% of the time, Pallas kernels for 23%

profile of v9, /device:TPU:4, one launch (start us, length us, event | category | flops | bytes accessed | tf_op | source)
XLA Modules:
  0.0 111.9 jit_solution(13037479651695877849)
XLA Ops:
  0.7 0.0 copy-start.2
  0.7 3.1 %cut_prompt.1 = (bf16[8,8,32,128]{3,2,1,0:T(8,128)(2,1)}, bf16[2,128,1024]{2,1,0:T(8,128)(2,1)}, bf16[2,128,1024]{2,1,0:T(8,128)(2,1)}) custom-call(s32[1,64]{1,0:T(1,128)} %starts_ref.9, bf16[1,256,1024]{2,1,0:T(8,128)(2,1)} %k_ref.5, bf16[1,256,1024]{2,1,0:T(8,128)(2,1)} %v_ref.5), custom_call_target="tpu_custom_call" | custom-call | tf_op jit(solution)/shard_map/cut_prompt/pallas_call | solution.py:122
  3.8 12.8 %all-to-all-start = ((bf16[64,32,128]{2,1,0:T(8,128)(2,1)}), bf16[64,32,128]{2,1,0:T(8,128)(2,1)S(1)}, u32[]{:S(2)}, u32[]{:S(2)}) async-start(bf16[64,32,128]{2,1,0:T(8,128)(2,1)} %bitcast.8), calls=%async_computation | async-start | bytes 1048576 | tf_op jit(solution)/shard_map/all_to_all | solution.py:639
  16.6 4.3 %collective-permute-start = (bf16[2,128,1024]{2,1,0:T(8,128)(2,1)}, bf16[2,128,1024]{2,1,0:T(8,128)(2,1)}, u32[]{:S(2)}, u32[]{:S(2)}) collective-permute-start(bf16[2,128,1024]{2,1,0:T(8,128)(2,1)} %get-tuple-element.38), channel_id=1, source_target_pairs={{0,1},{1,2},{2,3},{3,4},{4,5},{5,6},{6,7},{7,8},{8,9},{9,10},{10,1... | collective-permute-start | bytes 1572872 | tf_op jit(solution)/shard_map/ppermute | solution.py:644
  20.9 1.3 %collective-permute-start.1 = (bf16[2,128,1024]{2,1,0:T(8,128)(2,1)}, bf16[2,128,1024]{2,1,0:T(8,128)(2,1)}, u32[]{:S(2)}, u32[]{:S(2)}) collective-permute-start(bf16[2,128,1024]{2,1,0:T(8,128)(2,1)} %get-tuple-element.39), channel_id=1, source_target_pairs={{1,0},{2,1},{3,2},{4,3},{5,4},{6,5},{7,6},{8,7},{9,8},{10,9},{11,1... | collective-permute-start | bytes 1572872 | tf_op jit(solution)/shard_map/ppermute | solution.py:644
  22.1 14.0 %all-to-all-done.in_ref = bf16[64,32,128]{2,1,0:T(8,128)(2,1)S(1)} async-done(((bf16[64,32,128]{2,1,0:T(8,128)(2,1)}), bf16[64,32,128]{2,1,0:T(8,128)(2,1)S(1)}, u32[]{:S(2)}, u32[]{:S(2)}) %all-to-all-start) | async-done | bytes 524320 | tf_op jit(solution)/shard_map/all_to_all | solution.py:639
  36.2 1.5 %route.1 = bf16[64,32,128]{2,1,0:T(8,128)(2,1)} custom-call(s32[1,64]{1,0:T(1,128)S(1)} %copy-done.6, bf16[64,32,128]{2,1,0:T(8,128)(2,1)S(1)} %all-to-all-done.in_ref), custom_call_target="tpu_custom_call" | custom-call | tf_op jit(solution)/shard_map/route/pallas_call | solution.py:155
  37.7 5.1 %all-to-all-start.1 = ((bf16[64,32,128]{2,1,0:T(8,128)(2,1)}), bf16[64,32,128]{2,1,0:T(8,128)(2,1)S(1)}, u32[]{:S(2)}, u32[]{:S(2)}) async-start(bf16[64,32,128]{2,1,0:T(8,128)(2,1)} %route.1), calls=%async_computation.1 | async-start | bytes 1048576 | tf_op jit(solution)/shard_map/all_to_all | solution.py:639
  42.8 0.0 collective-permute-done.low_ref
  42.8 6.2 %window.1 = (f32[8,8,256]{2,1,0:T(8,128)S(1)}, f32[2,256,256]{2,1,0:T(8,128)S(1)}, f32[2,128,128]{2,1,0:T(8,128)S(1)}, f32[128,256]{1,0:T(8,128)S(1)}) custom-call(s32[1,64]{1,0:T(1,128)S(1)} %copy-done.6, s32[1,64]{1,0:T(1,128)S(1)} %copy-done.8, f32[8]{0:T(128)S(1)} %copy-done.7, bf16[1,256,1024]{2,1,0:T(8,128)(2,1)S(1)} %copy-done.3, ...), custom_call_target="tpu_custom_call" | custom-call | flops 20000000000 | bytes 8388608 | tf_op jit(solution)/shard_map/window/pallas_call | solution.py:322
  49.1 0.0 copy-start.5
  49.1 0.8 copy-done.5
  49.8 9.3 %all-to-all-done.1 = bf16[64,32,128]{2,1,0:T(8,128)(2,1)S(1)} async-done(((bf16[64,32,128]{2,1,0:T(8,128)(2,1)}), bf16[64,32,128]{2,1,0:T(8,128)(2,1)S(1)}, u32[]{:S(2)}, u32[]{:S(2)}) %all-to-all-start.1) | async-done | bytes 524320 | tf_op jit(solution)/shard_map/all_to_all | solution.py:639
  59.2 2.7 %prompt_part.1 = (bf16[8,8,40,128]{3,2,1,0:T(8,128)(2,1)}, f32[8,8,256]{2,1,0:T(8,128)S(1)}) custom-call(f32[8]{0:T(128)S(1)} %copy-done.7, bf16[1,256,1024]{2,1,0:T(8,128)(2,1)S(1)} %copy-done.3, bf16[1,256,1024]{2,1,0:T(8,128)(2,1)S(1)} %copy-done.4, bf16[8,8,32,128]{3,2,1,0:T(8,128)(2,1)S(1)} %bitcast.5, f32[8,8,256]{2,1,0:T(8,128)S(1)} %get-tuple-element.41.stats_ref, ...), custom_call_target="tpu_custom_call" | custom-call | flops 4000000000 | bytes 8388608 | tf_op jit(solution)/shard_map/prompt_part/pallas_call | solution.py:394
  61.9 5.2 %all-to-all-start.2 = ((bf16[64,40,128]{2,1,0:T(8,128)(2,1)}), bf16[64,40,128]{2,1,0:T(8,128)(2,1)S(1)}, u32[]{:S(2)}, u32[]{:S(2)}) async-start(bf16[64,40,128]{2,1,0:T(8,128)(2,1)} %bitcast.2), calls=%async_computation.2 | async-start | bytes 1310720 | tf_op jit(solution)/shard_map/all_to_all | solution.py:639
  67.1 4.4 %own_part.2 = (bf16[1,256,1024]{2,1,0:T(8,128)(2,1)}, bf16[1,256,1024]{2,1,0:T(8,128)(2,1)}, f32[256,1024]{1,0:T(8,128)}, f32[256,1024]{1,0:T(8,128)}) custom-call(f32[8]{0:T(128)S(1)} %copy-done.7, bf16[1,256,1024]{2,1,0:T(8,128)(2,1)S(1)} %copy-done.3, bf16[1,256,1024]{2,1,0:T(8,128)(2,1)S(1)} %copy-done.4, bf16[1,256,1024]{2,1,0:T(8,128)(2,1)S(1)} %copy-done.1, ...), custom_call_target="tpu_custom_call" | custom-call | flops 5000000000 | bytes 8388608 | tf_op jit(solution)/shard_map/own_part/pallas_call | solution.py:530
  71.5 3.4 %halo_grads.1 = (bf16[2,128,1024]{2,1,0:T(8,128)(2,1)}, bf16[2,128,1024]{2,1,0:T(8,128)(2,1)}) custom-call(bf16[1,256,1024]{2,1,0:T(8,128)(2,1)S(1)} %copy-done.3, bf16[1,256,1024]{2,1,0:T(8,128)(2,1)S(1)} %copy-done.4, bf16[2,128,1024]{2,1,0:T(8,128)(2,1)} %collective-permute-done.low_ref, bf16[2,128,1024]{2,1,0:T(8,128)(2,1)} %collective-permute-done.1.high_ref, ...), custom_call_target="tpu_custom_call" | custom-call | flops 4000000000 | bytes 8388608 | tf_op jit(solution)/shard_map/halo_grads/pallas_call | solution.py:447
  74.9 1.3 %collective-permute-start.2 = (bf16[2,128,1024]{2,1,0:T(8,128)(2,1)}, bf16[2,128,1024]{2,1,0:T(8,128)(2,1)S(1)}, u32[]{:S(2)}, u32[]{:S(2)}) collective-permute-start(bf16[2,128,1024]{2,1,0:T(8,128)(2,1)} %get-tuple-element.52), channel_id=1, source_target_pairs={{1,0},{2,1},{3,2},{4,3},{5,4},{6,5},{7,6},{8,7},{9,8},{10,9},{11,1... | collective-permute-start | bytes 1572872 | tf_op jit(solution)/shard_map/ppermute | solution.py:644
  76.2 5.4 %collective-permute-start.3 = (bf16[2,128,1024]{2,1,0:T(8,128)(2,1)}, bf16[2,128,1024]{2,1,0:T(8,128)(2,1)}, u32[]{:S(2)}, u32[]{:S(2)}) collective-permute-start(bf16[2,128,1024]{2,1,0:T(8,128)(2,1)} %get-tuple-element.53), channel_id=1, source_target_pairs={{0,1},{1,2},{2,3},{3,4},{4,5},{5,6},{6,7},{7,8},{8,9},{9,10},{10,1... | collective-permute-start | bytes 1572872 | tf_op jit(solution)/shard_map/ppermute | solution.py:644
  81.6 3.9 %all-to-all-done.2.in_ref = bf16[64,40,128]{2,1,0:T(8,128)(2,1)S(1)} async-done(((bf16[64,40,128]{2,1,0:T(8,128)(2,1)}), bf16[64,40,128]{2,1,0:T(8,128)(2,1)S(1)}, u32[]{:S(2)}, u32[]{:S(2)}) %all-to-all-start.2) | async-done | bytes 655392 | tf_op jit(solution)/shard_map/all_to_all | solution.py:639
  85.4 1.6 %gather.1 = (bf16[64,32,128]{2,1,0:T(8,128)(2,1)}, f32[8,128]{1,0:T(8,128)S(1)}) custom-call(s32[1,64]{1,0:T(1,128)S(1)} %copy-done.6, bf16[64,40,128]{2,1,0:T(8,128)(2,1)S(1)} %all-to-all-done.2.in_ref), custom_call_target="tpu_custom_call" | custom-call | tf_op jit(solution)/shard_map/gather/pallas_call | solution.py:184
  87.0 7.2 %all-to-all-start.3 = ((bf16[64,32,128]{2,1,0:T(8,128)(2,1)}), bf16[64,32,128]{2,1,0:T(8,128)(2,1)S(1)}, u32[]{:S(2)}, u32[]{:S(2)}) async-start(bf16[64,32,128]{2,1,0:T(8,128)(2,1)} %get-tuple-element.66), calls=%async_computation.3 | async-start | bytes 1048576 | tf_op jit(solution)/shard_map/all_to_all | solution.py:639
  94.3 0.1 collective-permute-start.4
  94.4 0.9 collective-permute-start.5
  95.3 2.5 %collective-permute-start.6 = (f32[8,128]{1,0:T(8,128)S(1)}, f32[8,128]{1,0:T(8,128)S(1)}, u32[]{:S(2)}, u32[]{:S(2)}) collective-permute-start(f32[8,128]{1,0:T(8,128)S(1)} %get-tuple-element.55), channel_id=1, source_target_pairs={{0,192},{64,128},{128,64},{192,0},{1,193},{65,129},{129,65},{193,1... | collective-permute-start | bytes 12296 | tf_op jit(solution)/shard_map/ppermute | solution.py:649
  97.8 4.4 %own_part.3 = (bf16[1,256,1024]{2,1,0:T(8,128)(2,1)}, bf16[1,256,1024]{2,1,0:T(8,128)(2,1)}, f32[256,1024]{1,0:T(8,128)}, f32[256,1024]{1,0:T(8,128)}) custom-call(f32[8]{0:T(128)S(1)} %copy-done.7, bf16[1,256,1024]{2,1,0:T(8,128)(2,1)S(1)} %copy-done.3, ...), custom_call_target="tpu_custom_call", output_to_operand_aliasing={{0}: (12, {}), {1}: (13, {}), {2}: (14, {}), {3}: (15, {})} | custom-call | flops 1000000000 | bytes 8388608 | tf_op jit(solution)/shard_map/own_part/pallas_call | solution.py:530
  102.1 0.0 collective-permute-done.3.left_ref
  102.1 4.1 %merge.1 = (bf16[1,256,1024]{2,1,0:T(8,128)(2,1)}, bf16[1,256,1024]{2,1,0:T(8,128)(2,1)}, f32[2,256,1024]{2,1,0:T(8,128)}) custom-call(bf16[2,128,1024]{2,1,0:T(8,128)(2,1)S(1)} %collective-permute-done.2.right_ref, bf16[2,128,1024]{2,1,0:T(8,128)(2,1)} %collective-permute-done.3.left_ref, f32[256,1024]{1,0:T(8,128)} %get-tuple-element.63.gk_ref, ...), custom_call_target="tpu_custom_call" | custom-call | flops 8000000000 | bytes 8388608 | tf_op jit(solution)/shard_map/merge/pallas_call | solution.py:562
  106.3 0.0 collective-permute-done.4
  106.3 0.6 add_reduce_fusion
  106.9 2.1 %all-to-all-done.3 = bf16[64,32,128]{2,1,0:T(8,128)(2,1)S(1)} async-done(((bf16[64,32,128]{2,1,0:T(8,128)(2,1)}), bf16[64,32,128]{2,1,0:T(8,128)(2,1)S(1)}, u32[]{:S(2)}, u32[]{:S(2)}) %all-to-all-start.3) | async-done | bytes 524320 | tf_op jit(solution)/shard_map/all_to_all | solution.py:639
  109.0 2.9 %finish.1 = (bf16[1,256,1024]{2,1,0:T(8,128)(2,1)}, bf16[1,256,1024]{2,1,0:T(8,128)(2,1)}) custom-call(s32[1,64]{1,0:T(1,128)S(1)} %copy-done.6, f32[2,256,1024]{2,1,0:T(8,128)} %get-tuple-element.65.sums_hbm, bf16[8,8,32,128]{3,2,1,0:T(8,128)(2,1)S(1)} %bitcast.4, ...), custom_call_target="tpu_custom_call", output_to_operand_aliasing={{0}: (3, {}), {1}: (4, {})} | custom-call | tf_op jit(solution)/shard_map/finish/pallas_call | solution.py:620
  (19 shorter events, 0.0 us)
Async XLA Ops:
  0.6 35.6 %copy-start.6 = (s32[1,64]{1,0:T(1,128)S(1)}, s32[1,64]{1,0:T(1,128)}, u32[]{:S(2)}) copy-start(s32[1,64]{1,0:T(1,128)} %starts_ref.9) | copy-start | bytes 772
  0.6 42.1 %copy-start.1 = (bf16[1,256,1024]{2,1,0:T(8,128)(2,1)S(1)}, bf16[1,256,1024]{2,1,0:T(8,128)(2,1)}, u32[]{:S(2)}) copy-start(bf16[1,256,1024]{2,1,0:T(8,128)(2,1)} %k_ref.5) | copy-start | bytes 1572868
  0.7 42.1 %copy-start.2 = (bf16[1,256,1024]{2,1,0:T(8,128)(2,1)S(1)}, bf16[1,256,1024]{2,1,0:T(8,128)(2,1)}, u32[]{:S(2)}) copy-start(bf16[1,256,1024]{2,1,0:T(8,128)(2,1)} %v_ref.5) | copy-start | bytes 1572868
  0.7 42.1 %copy-start.4 = (bf16[1,256,1024]{2,1,0:T(8,128)(2,1)S(1)}, bf16[1,256,1024]{2,1,0:T(8,128)(2,1)}, u32[]{:S(2)}) copy-start(bf16[1,256,1024]{2,1,0:T(8,128)(2,1)} %d_ref.9) | copy-start | bytes 1572868
  0.7 42.1 %copy-start.8 = (s32[1,64]{1,0:T(1,128)S(1)}, s32[1,64]{1,0:T(1,128)}, u32[]{:S(2)}) copy-start(s32[1,64]{1,0:T(1,128)} %lens_ref.1) | copy-start | bytes 772
  0.7 42.1 %copy-start.7 = (f32[8]{0:T(128)S(1)}, f32[8]{0:T(128)}, u32[]{:S(2)}) copy-start(f32[8]{0:T(128)} %bias_ref.7) | copy-start | bytes 100
  0.7 42.1 %copy-start.3 = (bf16[1,256,1024]{2,1,0:T(8,128)(2,1)S(1)}, bf16[1,256,1024]{2,1,0:T(8,128)(2,1)}, u32[]{:S(2)}) copy-start(bf16[1,256,1024]{2,1,0:T(8,128)(2,1)} %q_ref.9) | copy-start | bytes 1572868
  3.8 32.4 %all-to-all-start = ((bf16[64,32,128]{2,1,0:T(8,128)(2,1)}), bf16[64,32,128]{2,1,0:T(8,128)(2,1)S(1)}, u32[]{:S(2)}, u32[]{:S(2)}) async-start(bf16[64,32,128]{2,1,0:T(8,128)(2,1)} %bitcast.8), calls=%async_computation | async-start | bytes 1048576 | tf_op jit(solution)/shard_map/all_to_all | solution.py:639
  16.6 26.2 %collective-permute-start = (bf16[2,128,1024]{2,1,0:T(8,128)(2,1)}, bf16[2,128,1024]{2,1,0:T(8,128)(2,1)}, u32[]{:S(2)}, u32[]{:S(2)}) collective-permute-start(bf16[2,128,1024]{2,1,0:T(8,128)(2,1)} %get-tuple-element.38), channel_id=1, source_target_pairs={{0,1},{1,2},{2,3},{3,4},{4,5},{5,6},{6,7},{7,8},{8,9},{9,10},{10,1... | collective-permute-start | bytes 1572872 | tf_op jit(solution)/shard_map/ppermute | solution.py:644
  20.9 21.9 %collective-permute-start.1 = (bf16[2,128,1024]{2,1,0:T(8,128)(2,1)}, bf16[2,128,1024]{2,1,0:T(8,128)(2,1)}, u32[]{:S(2)}, u32[]{:S(2)}) collective-permute-start(bf16[2,128,1024]{2,1,0:T(8,128)(2,1)} %get-tuple-element.39), channel_id=1, source_target_pairs={{1,0},{2,1},{3,2},{4,3},{5,4},{6,5},{7,6},{8,7},{9,8},{10,9},{11,1... | collective-permute-start | bytes 1572872 | tf_op jit(solution)/shard_map/ppermute | solution.py:644
  37.7 21.5 %all-to-all-start.1 = ((bf16[64,32,128]{2,1,0:T(8,128)(2,1)}), bf16[64,32,128]{2,1,0:T(8,128)(2,1)S(1)}, u32[]{:S(2)}, u32[]{:S(2)}) async-start(bf16[64,32,128]{2,1,0:T(8,128)(2,1)} %route.1), calls=%async_computation.1 | async-start | bytes 1048576 | tf_op jit(solution)/shard_map/all_to_all | solution.py:639
  49.1 0.8 copy-start.5
  59.2 2.7 %copy-start = (bf16[64,32,128]{2,1,0:T(8,128)(2,1)}, bf16[64,32,128]{2,1,0:T(8,128)(2,1)S(1)}, u32[]{:S(2)}) copy-start(bf16[64,32,128]{2,1,0:T(8,128)(2,1)S(1)} %all-to-all-done.1) | copy-start | bytes 1572868
  61.9 23.5 %all-to-all-start.2 = ((bf16[64,40,128]{2,1,0:T(8,128)(2,1)}), bf16[64,40,128]{2,1,0:T(8,128)(2,1)S(1)}, u32[]{:S(2)}, u32[]{:S(2)}) async-start(bf16[64,40,128]{2,1,0:T(8,128)(2,1)} %bitcast.2), calls=%async_computation.2 | async-start | bytes 1310720 | tf_op jit(solution)/shard_map/all_to_all | solution.py:639
  74.9 27.2 %collective-permute-start.2 = (bf16[2,128,1024]{2,1,0:T(8,128)(2,1)}, bf16[2,128,1024]{2,1,0:T(8,128)(2,1)S(1)}, u32[]{:S(2)}, u32[]{:S(2)}) collective-permute-start(bf16[2,128,1024]{2,1,0:T(8,128)(2,1)} %get-tuple-element.52), channel_id=1, source_target_pairs={{1,0},{2,1},{3,2},{4,3},{5,4},{6,5},{7,6},{8,7},{9,8},{10,9},{11,1... | collective-permute-start | bytes 1572872 | tf_op jit(solution)/shard_map/ppermute | solution.py:644
  76.2 25.9 %collective-permute-start.3 = (bf16[2,128,1024]{2,1,0:T(8,128)(2,1)}, bf16[2,128,1024]{2,1,0:T(8,128)(2,1)}, u32[]{:S(2)}, u32[]{:S(2)}) collective-permute-start(bf16[2,128,1024]{2,1,0:T(8,128)(2,1)} %get-tuple-element.53), channel_id=1, source_target_pairs={{0,1},{1,2},{2,3},{3,4},{4,5},{5,6},{6,7},{7,8},{8,9},{9,10},{10,1... | collective-permute-start | bytes 1572872 | tf_op jit(solution)/shard_map/ppermute | solution.py:644
  87.0 22.0 %all-to-all-start.3 = ((bf16[64,32,128]{2,1,0:T(8,128)(2,1)}), bf16[64,32,128]{2,1,0:T(8,128)(2,1)S(1)}, u32[]{:S(2)}, u32[]{:S(2)}) async-start(bf16[64,32,128]{2,1,0:T(8,128)(2,1)} %get-tuple-element.66), calls=%async_computation.3 | async-start | bytes 1048576 | tf_op jit(solution)/shard_map/all_to_all | solution.py:639
  94.3 12.0 %collective-permute-start.4 = (f32[8,128]{1,0:T(8,128)S(1)}, f32[8,128]{1,0:T(8,128)S(1)}, u32[]{:S(2)}, u32[]{:S(2)}) collective-permute-start(f32[8,128]{1,0:T(8,128)S(1)} %get-tuple-element.55), channel_id=1, source_target_pairs={{0,64},{64,0},{128,192},{192,128},{1,65},{65,1},{129,193},{193,129... | collective-permute-start | bytes 12296 | tf_op jit(solution)/shard_map/ppermute | solution.py:649
  94.4 11.9 %collective-permute-start.5 = (f32[8,128]{1,0:T(8,128)S(1)}, f32[8,128]{1,0:T(8,128)S(1)}, u32[]{:S(2)}, u32[]{:S(2)}) collective-permute-start(f32[8,128]{1,0:T(8,128)S(1)} %get-tuple-element.55), channel_id=1, source_target_pairs={{0,128},{64,192},{128,0},{192,64},{1,129},{65,193},{129,1},{193,65... | collective-permute-start | bytes 12296 | tf_op jit(solution)/shard_map/ppermute | solution.py:649
  95.3 11.0 %collective-permute-start.6 = (f32[8,128]{1,0:T(8,128)S(1)}, f32[8,128]{1,0:T(8,128)S(1)}, u32[]{:S(2)}, u32[]{:S(2)}) collective-permute-start(f32[8,128]{1,0:T(8,128)S(1)} %get-tuple-element.55), channel_id=1, source_target_pairs={{0,192},{64,128},{128,64},{192,0},{1,193},{65,129},{129,65},{193,1... | collective-permute-start | bytes 12296 | tf_op jit(solution)/shard_map/ppermute | solution.py:649
